TPU v7x, 256 devices: a whole 4x4x8 slice. The times are simulated.
256 devices in a mesh: row: 16 (over z, core), col: 4 (over y), rep: 4 (over x).
Axes of the slice: x: 4, y: 4, z: 8, core: 2. Of those that a mesh axis runs over, the one named last changes fastest.
Arguments:
- density: bfloat16 [8192, 8192], P('row', 'col'), may hold values from -1.5 to 1.75, as said below
- pattern_density: int32 [256, 256], P('row', 'col'), may hold values 0 or 1
- pattern_square: int32 [256, 256], P('row', 'col'), may hold values 0 or 1
- pattern_cube: int32 [256, 256], P('row', 'col'), may hold values 0 or 1
Outputs:
- purified: bfloat16 [8192, 8192], P('row', ('col', 'rep'))
Inputs may be any that keep to these rules, and one draw needn't show every extreme that they name: `density`: symmetric.
All inputs are finite; a program needn't handle non-finite values. No bound on the sum of `pattern_density` or of `pattern_square` or of `pattern_cube` on one device may be relied on, other than what follows from the above.
Results may differ from a plain program's by a relative error of at most 0.0054.
Values may be sent and summed in bfloat16 or wider, within the bound.
No kernel may reach another device: no remote copies, remote signals or barrier semaphores. Data moves between devices by JAX's collectives and lax.ppermute only.
A program may use at most 64 MiB of HBM per device.

v0:
```python
import functools

import jax
import jax.numpy as jnp
from jax import lax
from jax.experimental import pallas as pl
from jax.experimental.pallas import tpu as pltpu
from jax.sharding import PartitionSpec as P

BLK = 32
BF = jnp.bfloat16
F32 = jnp.float32
VMEM = pl.BlockSpec(memory_space=pltpu.VMEM)
SMEM = pl.BlockSpec(memory_space=pltpu.SMEM)
NT = (((1,), (1,)), ((), ()))
NN = (((1,), (0,)), ((), ()))

SLOTS = (0, -1, 1, -2, 2, -3, 3, 4)
CHUNKS = ((0, 1, 2), (3, 4), (5, 6), (7,))
PHASES = ((0, 1), (2,), (3,))


def call(kernel, out_shape, n_in, scratch=(), flops=0, byts=0, mib=24, aliases={}):
    return pl.pallas_call(
        kernel,
        out_shape=out_shape,
        in_specs=[SMEM] + [VMEM] * (n_in - 1),
        out_specs=jax.tree.map(lambda _: VMEM, out_shape),
        scratch_shapes=list(scratch),
        input_output_aliases=aliases,
        compiler_params=pltpu.CompilerParams(vmem_limit_bytes=mib << 20),
        cost_estimate=pl.CostEstimate(flops=flops, bytes_accessed=byts, transcendentals=0),
    )


def shape(*dims, dtype=BF):
    return jax.ShapeDtypeStruct(dims, dtype)


def iota(dims, axis):
    return lax.broadcasted_iota(jnp.int32, dims, axis)


def dot(a, b, dims=NN):
    return lax.dot_general(a, b, dims, preferred_element_type=F32)


def row_of_slot(index, z, core, layer):
    slot = index // 8
    other = (index // 4) % 2
    offset = jnp.where(slot == 7, 4, jnp.where(slot % 2 == 1, -((slot + 1) // 2), slot // 2))
    chip = lax.rem(z + offset + 8, 8)
    band = 2 * chip + lax.rem(core + other, 2)
    return 16 * band + 4 * layer + index % 4


def prep_kernel(s_ref, *refs):
    both_ref, local_ref, cube_ref, density_ref, left_ref, mk_ref, mt_ref, ms_ref, mc_ref = refs
    z, core, col, layer = s_ref[0], s_ref[1], s_ref[2], s_ref[3]
    wide = (iota((64, 2048), 0) == iota((64, 2048), 1) // BLK).astype(BF)
    roll = (iota((16, 16), 1) == lax.rem(iota((16, 16), 0) + 4 * col, 16)).astype(BF)
    local = dot(dot(roll, local_ref[...].astype(BF)).astype(BF), wide).astype(BF)
    for quarter in range(4):
        start = pl.multiple_of(128 * lax.rem(col + quarter, 4), 128)
        for block in range(4):
            at = 4 * quarter + block
            left_ref[pl.ds(BLK * at, BLK), :] = (
                density_ref[pl.ds(start + BLK * block, BLK), :] * local[at : at + 1, :]
            )
    at = iota((64, 1024), 1)
    block_row = 16 * (at // 64) + at % 16
    mine_too = (at // 16) % 4
    share = row_of_slot(iota((64, 1024), 0), z, core, layer)
    pick = jnp.where((block_row == share) & (mine_too == col), 1.0, 0.0).astype(BF)
    both = both_ref[...].reshape(1024, 128)
    mk = dot(pick, both)[:, :64].astype(BF)
    mt = jnp.zeros((64, 64), F32)
    ms = jnp.zeros((16, 64), F32)
    square_row = iota((16, 1024), 0) + 16 * (2 * z + core)
    square_at = iota((16, 1024), 1)
    square_block = 16 * (square_at // 64) + square_at % 16
    for n in range(4):
        mine = (block_row == 64 * col + iota((64, 1024), 0)) & (mine_too == n)
        rows = dot(jnp.where(mine, 1.0, 0.0).astype(BF), both)[:, :64].astype(BF)
        column = 64 * n + iota((64, 64), 1)
        take = (column == row_of_slot(iota((64, 64), 0), z, core, layer)).astype(BF)
        mt = mt + dot(take, rows, NT)
        own = (square_block == square_row) & ((square_at // 16) % 4 == n)
        rows = dot(jnp.where(own, 1.0, 0.0).astype(BF), both)[:, 64:].astype(BF)
        ms = ms + dot(dot(roll, rows).astype(BF), take, NT)
    mk_ref[...] = dot(mk, wide)
    mt_ref[...] = dot(mt.astype(BF), wide)
    ms_ref[...] = dot(ms.astype(BF), wide)
    mc_ref[...] = -2.0 * dot(dot(roll, cube_ref[...].astype(BF)).astype(BF), wide)


def load_pieces(piece_refs, mask_ref, block_row, out_ref):
    done = 0
    for ref in piece_refs:
        for block in range(ref.shape[0] // BLK):
            row = block_row + done // BLK
            keep = jnp.broadcast_to(mask_ref[pl.ds(row, 1), :], (BLK, 2048)).astype(BF)
            out_ref[pl.ds(done, BLK), :] = ref[pl.ds(BLK * block, BLK), :] * keep
            done += BLK


def product_one_kernel(slots, n_pieces, s_ref, left_ref, mt_ref, *refs):
    col = s_ref[2]
    pieces, (send_ref, own_ref, right) = refs[:n_pieces], refs[n_pieces:]
    load_pieces(pieces, mt_ref, 8 * slots[0], right)
    for start in range(0, right.shape[0], 256):
        block = dot(left_ref[...], right[pl.ds(start, 256), :], NT)
        own_ref[:, pl.ds(start, 256)] = block[:128]
        for quarter in range(4):
            rows = slice(128 * quarter, 128 * quarter + 128)
            send_ref[lax.rem(col + quarter, 4), :, pl.ds(start, 256)] = block[rows].astype(BF)


def square_kernel(slots, s_ref, ms_ref, own_ref, got_ref, out_ref):
    col = s_ref[2]
    total = own_ref[...]
    for quarter in range(1, 4):
        total = total + got_ref[lax.rem(col + quarter, 4)].astype(F32)
    for block in range(4):
        rows = slice(BLK * block, BLK * block + BLK)
        keep = ms_ref[pl.ds(block, 1), pl.ds(256 * slots[0], total.shape[1])]
        kept = (total[rows] * keep).astype(BF)
        for quarter in range(4):
            out_ref[quarter, rows, :] = kept


def product_two_kernel(chunks, n_pieces, first, last, s_ref, mk_ref, mc_ref, *refs):
    z, core, col, layer = s_ref[0], s_ref[1], s_ref[2], s_ref[3]
    refs = list(refs)
    total = refs.pop() if last else None
    right, square = refs[-2:]
    before = None if first else refs.pop(0)
    squares, refs = refs[: len(chunks)], refs[len(chunks) :]
    pieces, outs = refs[:n_pieces], refs[n_pieces:-2]
    slots = [slot for chunk in chunks for slot in CHUNKS[chunk]]
    load_pieces(pieces, mk_ref, 8 * slots[0], right)
    start = 0
    for n in range(len(chunks)):
        width = squares[n].shape[2]
        for quarter in range(4):
            square[pl.ds(128 * quarter, 128), pl.ds(start, width)] = squares[n][lax.rem(col + quarter, 4)]
        start += width
    if not last:
        total = outs[0]
    for cols in range(0, 2048, 256):
        block = dot(square[...], right[:, pl.ds(cols, 256)])
        for row in range(16):
            rows = slice(BLK * row, BLK * row + BLK)
            part = block[rows] * mc_ref[pl.ds(row, 1), pl.ds(cols, 256)]
            if not first:
                part = part + before[rows, pl.ds(cols, 256)]
            total[rows, pl.ds(cols, 256)] = part
    for n, slot in enumerate(slots):
        chip = lax.rem(z + SLOTS[slot] + 8, 8)

        @pl.when(chip // 2 == col)
        def _():
            for other in range(2):
                band = 2 * chip + lax.rem(core + other, 2) - 4 * col
                cols = pl.ds(pl.multiple_of(512 * band + 128 * layer, 128), 128)
                total[:, cols] += 3.0 * square[:, pl.ds(256 * n + 128 * other, 128)].astype(F32)

    if last:
        for share in range(4):
            outs[0][share] = total[:, pl.ds(512 * share, 512)].astype(BF)
        outs[1][...] = total[:, pl.ds(pl.multiple_of(512 * layer, 512), 512)]


def finish_kernel(s_ref, own_ref, got_ref, out_ref):
    col, layer = s_ref[2], s_ref[3]
    for quarter in range(4):
        rows = pl.ds(128 * quarter, 128)
        total = own_ref[rows, :]
        for share in range(1, 4):
            total = total + got_ref[lax.rem(layer + share, 4), rows, :].astype(F32)
        out_ref[pl.ds(pl.multiple_of(128 * lax.rem(col + quarter, 4), 128), 128), :] = total.astype(BF)


def shift(array, axis, step, size):
    return lax.ppermute(array, axis, [(i, (i + step) % size) for i in range(size)])


def swap(array):
    return lax.ppermute(array, "row", [(i, i ^ 1) for i in range(16)])


def exchange(parts, axis):
    return lax.all_to_all(parts, axis, 0, 0)


def gather_patterns(pattern_density, pattern_square):
    both = jnp.concatenate([pattern_density, pattern_square], 1).astype(BF)
    return exchange(jnp.broadcast_to(both, (64, 16, 128)), ("row", "col"))


def body(density, pattern_density, pattern_square, pattern_cube):
    row, col, layer = lax.axis_index("row"), lax.axis_index("col"), lax.axis_index("rep")
    where = jnp.stack([row // 2, row % 2, col, layer]).astype(jnp.int32)
    own = lax.dynamic_slice_in_dim(density, 128 * layer, 128, 0)

    up, down = [own], [own]
    for step in range(1, 5):
        first, second = up[-1], down[-1]
        if step == 4:
            first, second = first[:64], second[64:]
        up.append(shift(first, "row", 2, 16))
        down.append(shift(second, "row", -2, 16))
    held = {0: [own], 4: [up[4], down[4]]}
    for step in (1, 2, 3):
        held[-step], held[step] = [up[step]], [down[step]]
    pieces = []
    for offset in SLOTS:
        pieces.append(held[offset] + [swap(piece) for piece in held[offset]])

    both = gather_patterns(pattern_density, pattern_square)
    left, mk, mt, ms, mc = call(
        prep_kernel,
        (
            shape(512, 2048),
            shape(64, 2048, dtype=F32),
            shape(64, 2048, dtype=F32),
            shape(16, 2048, dtype=F32),
            shape(16, 2048, dtype=F32),
        ),
        5,
        flops=2 * 200 * 256 * 2048,
        byts=6 << 20,
    )(where, both, pattern_density, pattern_cube, density)

    squares = []
    for number, slots in enumerate(CHUNKS):
        width = 256 * len(slots)
        held = [piece for slot in slots for piece in pieces[slot]]
        send, mine = call(
            functools.partial(product_one_kernel, slots, len(held)),
            (shape(4, 128, width), shape(128, width, dtype=F32)),
            3 + len(held),
            [pltpu.VMEM((width, 2048), BF)],
            flops=2 * 512 * 2048 * width,
            byts=2 * 2048 * (512 + width),
        )(where, left, mt, *held)
        mine = call(
            functools.partial(square_kernel, slots),
            shape(4, 128, width),
            4,
            byts=2 * 128 * width * 6,
        )(where, ms, mine, exchange(send, "col"))
        squares.append(exchange(mine, "col"))

    total = []
    for number, chunks in enumerate(PHASES):
        first, last = number == 0, number == len(PHASES) - 1
        held = [piece for chunk in chunks for slot in CHUNKS[chunk] for piece in pieces[slot]]
        blocks = [squares[chunk] for chunk in chunks]
        width = sum(block.shape[2] for block in blocks)
        scratch = [pltpu.VMEM((width, 2048), BF), pltpu.VMEM((512, width), BF)]
        if last:
            out = (shape(4, 512, 512), shape(512, 512, dtype=F32))
            scratch.append(pltpu.VMEM((512, 2048), F32))
        else:
            out = (shape(512, 2048, dtype=F32),)
        total = call(
            functools.partial(product_two_kernel, chunks, len(held), first, last),
            out,
            3 + len(total) + len(blocks) + len(held),
            scratch,
            flops=2 * 512 * 2048 * width,
            byts=2 * 2048 * (1024 + width),
            aliases={} if first or last else {3: 0},
        )(where, mk, mc, *total, *blocks, *held)
    send, mine = total
    return call(finish_kernel, shape(512, 512), 3, byts=3 << 20)(where, mine, exchange(send, "rep"))


def solution(mesh):
    placed = (P("row", "col"), P("row", "col"), P("row", "col"), P("row", "col"))
    return jax.shard_map(
        body, mesh=mesh, in_specs=placed, out_specs=P("row", ("col", "rep")), check_vma=False
    )
```

profile of v0, /device:TPU:32, one launch (start us, length us, event | category | flops | bytes accessed | tf_op | source)
XLA Modules:
  0.0 189.5 jit_solution(15278716095924911887)
XLA Ops:
  0.0 1.9 constant_dynamic-slice_fusion.refs_0_.refs_2_
  1.9 1.9 %collective-permute-start.1 = (bf16[128,2048]{1,0:T(8,128)(2,1)}, bf16[128,2048]{1,0:T(8,128)(2,1)}, u32[]{:S(2)}, u32[]{:S(2)}) collective-permute-start(bf16[128,2048]{1,0:T(8,128)(2,1)} %constant_dynamic-slice_fusion.refs_0_.refs_2_), channel_id=1, source_target_pairs={{0,32},{16,48},{32,64},{48,80},{64,96},{80,112},{96,128},{112,144}... | collective-permute-start | bytes 1572872 | tf_op jit(solution)/shard_map/ppermute | solution.py:185
  3.9 0.7 convert.7
  4.6 0.7 convert.6
  5.4 0.7 broadcast_in_dim.3
  6.1 13.0 %all-to-all-start = ((bf16[64,16,128]{2,1,0:T(8,128)(2,1)}), bf16[64,16,128]{2,1,0:T(8,128)(2,1)S(1)}, u32[]{:S(2)}, u32[]{:S(2)}) async-start(bf16[64,16,128]{2,1,0:T(8,128)(2,1)} %broadcast_in_dim.3), calls=%async_computation | async-start | bytes 524288 | tf_op jit(solution)/shard_map/all_to_all | solution.py:193
  19.1 1.5 collective-permute-start.5
  21.8 10.5 %all-to-all-done.refs_0_ = bf16[64,16,128]{2,1,0:T(8,128)(2,1)S(1)} async-done(((bf16[64,16,128]{2,1,0:T(8,128)(2,1)}), bf16[64,16,128]{2,1,0:T(8,128)(2,1)S(1)}, u32[]{:S(2)}, u32[]{:S(2)}) %all-to-all-start) | async-done | bytes 262176 | tf_op jit(solution)/shard_map/all_to_all | solution.py:193
  32.3 0.7 copy-done.12
  33.0 1.6 copy-done.2
  34.6 0.9 copy-done.13
  35.6 0.7 copy-done.24
  36.3 0.7 copy-done.25
  37.0 3.1 %shard_map.46 = (bf16[512,2048]{1,0:T(8,128)(2,1)S(1)}, f32[64,2048]{1,0:T(8,128)S(1)}, f32[64,2048]{1,0:T(8,128)S(1)}, f32[16,2048]{1,0:T(8,128)S(1)}, f32[16,2048]{1,0:T(8,128)S(1)}) custom-call(s32[4]{0:T(128)S(1)} %pad_add_fusion.s_ref, bf16[64,16,128]{2,1,0:T(8,128)(2,1)S(1)} %copy-done.13, s32[16,64]{1,0:T(8,128)S(1)} %copy-done.24, ...), custom_call_target="tpu_custom_call" | custom-call | flops 209715200 | bytes 6291456 | tf_op jit(solution)/shard_map/pallas_call | solution.py:221
  40.7 3.7 %shard_map.47 = (bf16[4,128,768]{2,1,0:T(8,128)(2,1)S(1)}, f32[128,768]{1,0:T(8,128)S(1)}) custom-call(s32[4]{0:T(128)S(1)} %pad_add_fusion.s_ref, bf16[512,2048]{1,0:T(8,128)(2,1)S(1)} %get-tuple-element.23.left_ref, f32[64,2048]{1,0:T(8,128)S(1)} %get-tuple-element.24.mt_ref, bf16[128,2048]{1,0:T(8,128)(2,1)} %constant_dynamic-slice_fusion.refs_0_.refs_2_, ...), custom_call_target="tpu_custom_call" | custom-call | flops 1610612736 | bytes 5242880 | tf_op jit(solution)/shard_map/pallas_call | solution.py:239
  44.4 0.9 copy-done.14
  45.2 0.8 copy-done.17
  46.0 4.2 %all-to-all-start.1 = ((bf16[4,128,768]{2,1,0:T(8,128)(2,1)}), bf16[4,128,768]{2,1,0:T(8,128)(2,1)}, u32[]{:S(2)}, u32[]{:S(2)}) async-start(bf16[4,128,768]{2,1,0:T(8,128)(2,1)} %copy-done.14), calls=%async_computation.1 | async-start | bytes 1572864 | tf_op jit(solution)/shard_map/all_to_all | solution.py:193
  50.5 1.8 collective-permute-start.11
  52.3 2.8 %shard_map.49 = (bf16[4,128,512]{2,1,0:T(8,128)(2,1)S(1)}, f32[128,512]{1,0:T(8,128)S(1)}) custom-call(s32[4]{0:T(128)S(1)} %pad_add_fusion.s_ref, bf16[512,2048]{1,0:T(8,128)(2,1)S(1)} %get-tuple-element.23.left_ref, f32[64,2048]{1,0:T(8,128)S(1)} %get-tuple-element.24.mt_ref, bf16[128,2048]{1,0:T(8,128)(2,1)} %collective-permute-done.5.refs_0_.refs_8_, ...), custom_call_target="tpu_custom_call" | custom-call | flops 1073741824 | bytes 4194304 | tf_op jit(solution)/shard_map/pallas_call | solution.py:239
  55.2 0.8 copy-done.16
  56.0 0.7 copy-done.20
  56.7 6.4 %all-to-all-done.1.got_ref = bf16[4,128,768]{2,1,0:T(8,128)(2,1)} async-done(((bf16[4,128,768]{2,1,0:T(8,128)(2,1)}), bf16[4,128,768]{2,1,0:T(8,128)(2,1)}, u32[]{:S(2)}, u32[]{:S(2)}) %all-to-all-start.1) | async-done | bytes 786464 | tf_op jit(solution)/shard_map/all_to_all | solution.py:193
  63.1 4.2 %all-to-all-start.3 = ((bf16[4,128,512]{2,1,0:T(8,128)(2,1)}), bf16[4,128,512]{2,1,0:T(8,128)(2,1)}, u32[]{:S(2)}, u32[]{:S(2)}) async-start(bf16[4,128,512]{2,1,0:T(8,128)(2,1)} %copy-done.16), calls=%async_computation.3 | async-start | bytes 1048576 | tf_op jit(solution)/shard_map/all_to_all | solution.py:193
  67.3 1.0 copy-done.18
  68.3 1.3 shard_map.48
  69.5 0.9 copy-done.3
  70.4 6.1 %all-to-all-done.3.got_ref = bf16[4,128,512]{2,1,0:T(8,128)(2,1)} async-done(((bf16[4,128,512]{2,1,0:T(8,128)(2,1)}), bf16[4,128,512]{2,1,0:T(8,128)(2,1)}, u32[]{:S(2)}, u32[]{:S(2)}) %all-to-all-start.3) | async-done | bytes 524320 | tf_op jit(solution)/shard_map/all_to_all | solution.py:193
  76.5 4.2 %all-to-all-start.2 = ((bf16[4,128,768]{2,1,0:T(8,128)(2,1)}), bf16[4,128,768]{2,1,0:T(8,128)(2,1)}, u32[]{:S(2)}, u32[]{:S(2)}) async-start(bf16[4,128,768]{2,1,0:T(8,128)(2,1)} %copy-done.3), calls=%async_computation.2 | async-start | bytes 1572864 | tf_op jit(solution)/shard_map/all_to_all | solution.py:193
  80.7 1.0 slice.8
  82.0 1.0 slice.9
  83.0 1.9 %collective-permute-start.14 = (bf16[64,2048]{1,0:T(8,128)(2,1)S(1)}, bf16[64,2048]{1,0:T(8,128)(2,1)S(1)}, u32[]{:S(2)}, u32[]{:S(2)}) collective-permute-start(bf16[64,2048]{1,0:T(8,128)(2,1)S(1)} %slice.9), channel_id=1, source_target_pairs={{0,224},{16,240},{32,0},{48,16},{64,32},{80,48},{96,64},{112,80},{... | collective-permute-start | bytes 786440 | tf_op jit(solution)/shard_map/ppermute | solution.py:185
  85.4 2.8 %collective-permute-done.13.refs_0_.refs_2_ = bf16[64,2048]{1,0:T(8,128)(2,1)S(1)} collective-permute-done((bf16[64,2048]{1,0:T(8,128)(2,1)S(1)}, bf16[64,2048]{1,0:T(8,128)(2,1)S(1)}, u32[]{:S(2)}, u32[]{:S(2)}) %collective-permute-start.13) | collective-permute-done | bytes 262176 | tf_op jit(solution)/shard_map/ppermute | solution.py:185
  88.2 2.4 %collective-permute-done.14.refs_1_.refs_3_ = bf16[64,2048]{1,0:T(8,128)(2,1)S(1)} collective-permute-done((bf16[64,2048]{1,0:T(8,128)(2,1)S(1)}, bf16[64,2048]{1,0:T(8,128)(2,1)S(1)}, u32[]{:S(2)}, u32[]{:S(2)}) %collective-permute-start.14) | collective-permute-done | bytes 262176 | tf_op jit(solution)/shard_map/ppermute | solution.py:185
  90.5 1.5 collective-permute-done.16.refs_3_.refs_5_
  92.1 1.3 shard_map.55
  93.4 0.7 copy-done.4
  94.1 0.7 copy-done.6
  94.8 0.7 copy-done.8
  95.5 0.7 copy-done.10
  96.2 0.7 copy-done.19
  96.9 4.5 %all-to-all-start.7 = ((bf16[4,128,256]{2,1,0:T(8,128)(2,1)}), bf16[4,128,256]{2,1,0:T(8,128)(2,1)}, u32[]{:S(2)}, u32[]{:S(2)}) async-start(bf16[4,128,256]{2,1,0:T(8,128)(2,1)} %copy-done.19), calls=%async_computation.7 | async-start | bytes 524288 | tf_op jit(solution)/shard_map/all_to_all | solution.py:193
  101.4 2.8 %shard_map.52 = (bf16[4,128,512]{2,1,0:T(8,128)(2,1)S(1)}, f32[128,512]{1,0:T(8,128)S(1)}) custom-call(s32[4]{0:T(128)S(1)} %pad_add_fusion.s_ref, bf16[512,2048]{1,0:T(8,128)(2,1)S(1)} %get-tuple-element.23.left_ref, f32[64,2048]{1,0:T(8,128)S(1)} %get-tuple-element.24.mt_ref, bf16[128,2048]{1,0:T(8,128)(2,1)} %collective-permute-done.9.refs_0_.refs_2_, ...), custom_call_target="tpu_custom_call" | custom-call | flops 1073741824 | bytes 4194304 | tf_op jit(solution)/shard_map/pallas_call | solution.py:239
  104.2 0.8 copy-done.15
  105.0 0.7 copy-done.22
  105.7 2.7 %all-to-all-done.7.got_ref = bf16[4,128,256]{2,1,0:T(8,128)(2,1)} async-done(((bf16[4,128,256]{2,1,0:T(8,128)(2,1)}), bf16[4,128,256]{2,1,0:T(8,128)(2,1)}, u32[]{:S(2)}, u32[]{:S(2)}) %all-to-all-start.7) | async-done | bytes 262176 | tf_op jit(solution)/shard_map/all_to_all | solution.py:193
  108.5 3.6 %all-to-all-start.5 = ((bf16[4,128,512]{2,1,0:T(8,128)(2,1)}), bf16[4,128,512]{2,1,0:T(8,128)(2,1)S(1)}, u32[]{:S(2)}, u32[]{:S(2)}) async-start(bf16[4,128,512]{2,1,0:T(8,128)(2,1)} %copy-done.15), calls=%async_computation.5 | async-start | bytes 1048576 | tf_op jit(solution)/shard_map/all_to_all | solution.py:193
  112.1 0.9 copy-done.21
  113.0 1.9 %shard_map.50 = bf16[4,128,512]{2,1,0:T(8,128)(2,1)} custom-call(s32[4]{0:T(128)S(1)} %pad_add_fusion.s_ref, f32[16,2048]{1,0:T(8,128)S(1)} %get-tuple-element.22.ms_ref, f32[128,512]{1,0:T(8,128)S(1)} %copy-done.21, bf16[4,128,512]{2,1,0:T(8,128)(2,1)} %all-to-all-done.3.got_ref), custom_call_target="tpu_custom_call" | custom-call | bytes 786432 | tf_op jit(solution)/shard_map/pallas_call | solution.py:247
  114.9 5.7 %all-to-all-done.5.got_ref = bf16[4,128,512]{2,1,0:T(8,128)(2,1)S(1)} async-done(((bf16[4,128,512]{2,1,0:T(8,128)(2,1)}), bf16[4,128,512]{2,1,0:T(8,128)(2,1)S(1)}, u32[]{:S(2)}, u32[]{:S(2)}) %all-to-all-start.5) | async-done | bytes 524320 | tf_op jit(solution)/shard_map/all_to_all | solution.py:193
  120.6 3.5 %all-to-all-start.4 = ((bf16[4,128,512]{2,1,0:T(8,128)(2,1)}), bf16[4,128,512]{2,1,0:T(8,128)(2,1)S(1)}, u32[]{:S(2)}, u32[]{:S(2)}) async-start(bf16[4,128,512]{2,1,0:T(8,128)(2,1)} %shard_map.50), calls=%async_computation.4 | async-start | bytes 1048576 | tf_op jit(solution)/shard_map/all_to_all | solution.py:193
  124.1 1.4 shard_map.53
  125.5 6.6 %all-to-all-done.4.refs_1_ = bf16[4,128,512]{2,1,0:T(8,128)(2,1)S(1)} async-done(((bf16[4,128,512]{2,1,0:T(8,128)(2,1)}), bf16[4,128,512]{2,1,0:T(8,128)(2,1)S(1)}, u32[]{:S(2)}, u32[]{:S(2)}) %all-to-all-start.4) | async-done | bytes 524320 | tf_op jit(solution)/shard_map/all_to_all | solution.py:193
  132.2 3.5 %all-to-all-start.6 = ((bf16[4,128,512]{2,1,0:T(8,128)(2,1)}), bf16[4,128,512]{2,1,0:T(8,128)(2,1)S(1)}, u32[]{:S(2)}, u32[]{:S(2)}) async-start(bf16[4,128,512]{2,1,0:T(8,128)(2,1)} %shard_map.53), calls=%async_computation.6 | async-start | bytes 1048576 | tf_op jit(solution)/shard_map/all_to_all | solution.py:193
  135.6 1.7 shard_map.56
  137.4 6.3 %all-to-all-done.6.refs_1_ = bf16[4,128,512]{2,1,0:T(8,128)(2,1)S(1)} async-done(((bf16[4,128,512]{2,1,0:T(8,128)(2,1)}), bf16[4,128,512]{2,1,0:T(8,128)(2,1)S(1)}, u32[]{:S(2)}, u32[]{:S(2)}) %all-to-all-start.6) | async-done | bytes 524320 | tf_op jit(solution)/shard_map/all_to_all | solution.py:193
  143.7 3.4 %all-to-all-start.8 = ((bf16[4,128,256]{2,1,0:T(8,128)(2,1)}), bf16[4,128,256]{2,1,0:T(8,128)(2,1)S(1)}, u32[]{:S(2)}, u32[]{:S(2)}) async-start(bf16[4,128,256]{2,1,0:T(8,128)(2,1)} %shard_map.56), calls=%async_computation.8 | async-start | bytes 524288 | tf_op jit(solution)/shard_map/all_to_all | solution.py:193
  147.1 5.9 %shard_map.51.refs_0_ = f32[512,2048]{1,0:T(8,128)S(1)} custom-call(s32[4]{0:T(128)S(1)} %pad_add_fusion.s_ref, f32[64,2048]{1,0:T(8,128)S(1)} %get-tuple-element.20.mk_ref, f32[16,2048]{1,0:T(8,128)S(1)} %get-tuple-element.21.mc_ref, bf16[4,128,768]{2,1,0:T(8,128)(2,1)} %all-to-all-done.2.refs_0_, bf16[4,128,512]{2,1,0:T(8,128)(2,1)S(1)} %all-to-all-done.4.refs_1_, ...), custom_call_target="tpu_custom_call" | custom-call | flops 2684354560 | bytes 9437184 | tf_op jit(solution)/shard_map/pallas_call | solution.py:267
  153.1 3.3 %shard_map.54.refs_0_ = f32[512,2048]{1,0:T(8,128)S(1)} custom-call(s32[4]{0:T(128)S(1)} %pad_add_fusion.s_ref, f32[64,2048]{1,0:T(8,128)S(1)} %get-tuple-element.20.mk_ref, f32[16,2048]{1,0:T(8,128)S(1)} %get-tuple-element.21.mc_ref, f32[512,2048]{1,0:T(8,128)S(1)} %shard_map.51.refs_0_, ...), custom_call_target="tpu_custom_call", output_to_operand_aliasing={{}: (3, {})} | custom-call | flops 1073741824 | bytes 6291456 | tf_op jit(solution)/shard_map/pallas_call | solution.py:267
  156.4 2.0 %copy-done = f32[512,2048]{1,0:T(8,128)} copy-done((f32[512,2048]{1,0:T(8,128)}, f32[512,2048]{1,0:T(8,128)S(1)}, u32[]{:S(2)}) %copy-start) | copy-done | bytes 4194328
  158.4 2.2 %copy-done.1 = f32[512,2048]{1,0:T(8,128)S(1)} copy-done((f32[512,2048]{1,0:T(8,128)S(1)}, f32[512,2048]{1,0:T(8,128)}, u32[]{:S(2)}) %copy-start.1) | copy-done | bytes 4194328
  160.6 1.5 shard_map.57
  162.2 25.7 %all_to_all.50.got_ref = bf16[4,512,512]{2,1,0:T(8,128)(2,1)S(1)} all-to-all(bf16[4,512,512]{2,1,0:T(8,128)(2,1)S(1)} %get-tuple-element.34), channel_id=1, replica_groups=mesh['row'=16,'col'=4,'rep'=4] {'rep'}, dimensions={0} | all-to-all | bytes 4194304 | tf_op jit(solution)/shard_map/all_to_all | solution.py:193
  187.9 1.6 shard_map.58
  (62 shorter events, 3.0 us)
Async XLA Ops:
  1.9 17.2 %collective-permute-start.1 = (bf16[128,2048]{1,0:T(8,128)(2,1)}, bf16[128,2048]{1,0:T(8,128)(2,1)}, u32[]{:S(2)}, u32[]{:S(2)}) collective-permute-start(bf16[128,2048]{1,0:T(8,128)(2,1)} %constant_dynamic-slice_fusion.refs_0_.refs_2_), channel_id=1, source_target_pairs={{0,32},{16,48},{32,64},{48,80},{64,96},{80,112},{96,128},{112,144}... | collective-permute-start | bytes 1572872 | tf_op jit(solution)/shard_map/ppermute | solution.py:185
  3.8 16.9 %collective-permute-start.3 = (bf16[128,2048]{1,0:T(8,128)(2,1)}, bf16[128,2048]{1,0:T(8,128)(2,1)}, u32[]{:S(2)}, u32[]{:S(2)}) collective-permute-start(bf16[128,2048]{1,0:T(8,128)(2,1)} %constant_dynamic-slice_fusion.refs_0_.refs_2_), channel_id=1, source_target_pairs={{0,224},{16,240},{32,0},{48,16},{64,32},{80,48},{96,64},{112,80},{... | collective-permute-start | bytes 1572872 | tf_op jit(solution)/shard_map/ppermute | solution.py:185
  6.1 26.2 %all-to-all-start = ((bf16[64,16,128]{2,1,0:T(8,128)(2,1)}), bf16[64,16,128]{2,1,0:T(8,128)(2,1)S(1)}, u32[]{:S(2)}, u32[]{:S(2)}) async-start(bf16[64,16,128]{2,1,0:T(8,128)(2,1)} %broadcast_in_dim.3), calls=%async_computation | async-start | bytes 524288 | tf_op jit(solution)/shard_map/all_to_all | solution.py:193
  19.1 20.9 %collective-permute-start.5 = (bf16[128,2048]{1,0:T(8,128)(2,1)}, bf16[128,2048]{1,0:T(8,128)(2,1)}, u32[]{:S(2)}, u32[]{:S(2)}) collective-permute-start(bf16[128,2048]{1,0:T(8,128)(2,1)} %collective-permute-done.1.refs_2_.refs_4_), channel_id=1, source_target_pairs={{0,32},{16,48},{32,64},{48,80},{64,96},{80,112},{96,128},{112,144}... | collective-permute-start | bytes 1572872 | tf_op jit(solution)/shard_map/ppermute | solution.py:185
  20.7 19.5 %collective-permute-start.7 = (bf16[128,2048]{1,0:T(8,128)(2,1)}, bf16[128,2048]{1,0:T(8,128)(2,1)}, u32[]{:S(2)}, u32[]{:S(2)}) collective-permute-start(bf16[128,2048]{1,0:T(8,128)(2,1)} %collective-permute-done.3.refs_4_.refs_6_), channel_id=1, source_target_pairs={{0,224},{16,240},{32,0},{48,16},{64,32},{80,48},{96,64},{112,80},{... | collective-permute-start | bytes 1572872 | tf_op jit(solution)/shard_map/ppermute | solution.py:185
  21.2 19.4 %collective-permute-start = (bf16[128,2048]{1,0:T(8,128)(2,1)}, bf16[128,2048]{1,0:T(8,128)(2,1)}, u32[]{:S(2)}, u32[]{:S(2)}) collective-permute-start(bf16[128,2048]{1,0:T(8,128)(2,1)} %constant_dynamic-slice_fusion.refs_0_.refs_2_), channel_id=1, source_target_pairs={{0,16},{16,0},{32,48},{48,32},{64,80},{80,64},{96,112},{112,96},{1... | collective-permute-start | bytes 1572872 | tf_op jit(solution)/shard_map/ppermute | solution.py:189
  21.2 19.4 %collective-permute-start.2 = (bf16[128,2048]{1,0:T(8,128)(2,1)}, bf16[128,2048]{1,0:T(8,128)(2,1)}, u32[]{:S(2)}, u32[]{:S(2)}) collective-permute-start(bf16[128,2048]{1,0:T(8,128)(2,1)} %collective-permute-done.1.refs_2_.refs_4_), channel_id=1, source_target_pairs={{0,16},{16,0},{32,48},{48,32},{64,80},{80,64},{96,112},{112,96},{1... | collective-permute-start | bytes 1572872 | tf_op jit(solution)/shard_map/ppermute | solution.py:189
  21.7 18.9 %collective-permute-start.4 = (bf16[128,2048]{1,0:T(8,128)(2,1)}, bf16[128,2048]{1,0:T(8,128)(2,1)}, u32[]{:S(2)}, u32[]{:S(2)}) collective-permute-start(bf16[128,2048]{1,0:T(8,128)(2,1)} %collective-permute-done.3.refs_4_.refs_6_), channel_id=1, source_target_pairs={{0,16},{16,0},{32,48},{48,32},{64,80},{80,64},{96,112},{112,96},{1... | collective-permute-start | bytes 1572872 | tf_op jit(solution)/shard_map/ppermute | solution.py:189
  32.3 0.7 copy-start.12
  33.0 1.6 copy-start.2
  34.6 0.9 copy-start.13
  35.6 0.7 copy-start.24
  36.3 0.7 copy-start.25
  40.1 12.3 %collective-permute-start.6 = (bf16[128,2048]{1,0:T(8,128)(2,1)}, bf16[128,2048]{1,0:T(8,128)(2,1)}, u32[]{:S(2)}, u32[]{:S(2)}) collective-permute-start(bf16[128,2048]{1,0:T(8,128)(2,1)} %collective-permute-done.5.refs_0_.refs_8_), channel_id=1, source_target_pairs={{0,16},{16,0},{32,48},{48,32},{64,80},{80,64},{96,112},{112,96},{1... | collective-permute-start | bytes 1572872 | tf_op jit(solution)/shard_map/ppermute | solution.py:189
  40.2 12.2 %collective-permute-start.8 = (bf16[128,2048]{1,0:T(8,128)(2,1)}, bf16[128,2048]{1,0:T(8,128)(2,1)}, u32[]{:S(2)}, u32[]{:S(2)}) collective-permute-start(bf16[128,2048]{1,0:T(8,128)(2,1)} %collective-permute-done.7.refs_2_.refs_10_), channel_id=1, source_target_pairs={{0,16},{16,0},{32,48},{48,32},{64,80},{80,64},{96,112},{112,96},{1... | collective-permute-start | bytes 1572872 | tf_op jit(solution)/shard_map/ppermute | solution.py:189
  44.4 0.9 copy-start.14
  45.2 0.8 copy-start.17
  46.0 17.1 %all-to-all-start.1 = ((bf16[4,128,768]{2,1,0:T(8,128)(2,1)}), bf16[4,128,768]{2,1,0:T(8,128)(2,1)}, u32[]{:S(2)}, u32[]{:S(2)}) async-start(bf16[4,128,768]{2,1,0:T(8,128)(2,1)} %copy-done.14), calls=%async_computation.1 | async-start | bytes 1572864 | tf_op jit(solution)/shard_map/all_to_all | solution.py:193
  50.2 30.5 %collective-permute-start.9 = (bf16[128,2048]{1,0:T(8,128)(2,1)}, bf16[128,2048]{1,0:T(8,128)(2,1)}, u32[]{:S(2)}, u32[]{:S(2)}) collective-permute-start(bf16[128,2048]{1,0:T(8,128)(2,1)} %collective-permute-done.5.refs_0_.refs_8_), channel_id=1, source_target_pairs={{0,32},{16,48},{32,64},{48,80},{64,96},{80,112},{96,128},{112,144}... | collective-permute-start | bytes 1572872 | tf_op jit(solution)/shard_map/ppermute | solution.py:185
  50.5 31.5 %collective-permute-start.11 = (bf16[128,2048]{1,0:T(8,128)(2,1)}, bf16[128,2048]{1,0:T(8,128)(2,1)}, u32[]{:S(2)}, u32[]{:S(2)}) collective-permute-start(bf16[128,2048]{1,0:T(8,128)(2,1)} %collective-permute-done.7.refs_2_.refs_10_), channel_id=1, source_target_pairs={{0,224},{16,240},{32,0},{48,16},{64,32},{80,48},{96,64},{112,80},{... | collective-permute-start | bytes 1572872 | tf_op jit(solution)/shard_map/ppermute | solution.py:185
  55.2 0.8 copy-start.16
  56.0 0.7 copy-start.20
  63.1 13.4 %all-to-all-start.3 = ((bf16[4,128,512]{2,1,0:T(8,128)(2,1)}), bf16[4,128,512]{2,1,0:T(8,128)(2,1)}, u32[]{:S(2)}, u32[]{:S(2)}) async-start(bf16[4,128,512]{2,1,0:T(8,128)(2,1)} %copy-done.16), calls=%async_computation.3 | async-start | bytes 1048576 | tf_op jit(solution)/shard_map/all_to_all | solution.py:193
  67.3 1.0 copy-start.18
  69.5 0.9 copy-start.3
  76.5 20.4 %all-to-all-start.2 = ((bf16[4,128,768]{2,1,0:T(8,128)(2,1)}), bf16[4,128,768]{2,1,0:T(8,128)(2,1)}, u32[]{:S(2)}, u32[]{:S(2)}) async-start(bf16[4,128,768]{2,1,0:T(8,128)(2,1)} %copy-done.3), calls=%async_computation.2 | async-start | bytes 1572864 | tf_op jit(solution)/shard_map/all_to_all | solution.py:193
  81.7 6.4 %collective-permute-start.13 = (bf16[64,2048]{1,0:T(8,128)(2,1)S(1)}, bf16[64,2048]{1,0:T(8,128)(2,1)S(1)}, u32[]{:S(2)}, u32[]{:S(2)}) collective-permute-start(bf16[64,2048]{1,0:T(8,128)(2,1)S(1)} %slice.8), channel_id=1, source_target_pairs={{0,32},{16,48},{32,64},{48,80},{64,96},{80,112},{96,128},{112,144}... | collective-permute-start | bytes 786440 | tf_op jit(solution)/shard_map/ppermute | solution.py:185
  83.0 7.6 %collective-permute-start.14 = (bf16[64,2048]{1,0:T(8,128)(2,1)S(1)}, bf16[64,2048]{1,0:T(8,128)(2,1)S(1)}, u32[]{:S(2)}, u32[]{:S(2)}) collective-permute-start(bf16[64,2048]{1,0:T(8,128)(2,1)S(1)} %slice.9), channel_id=1, source_target_pairs={{0,224},{16,240},{32,0},{48,16},{64,32},{80,48},{96,64},{112,80},{... | collective-permute-start | bytes 786440 | tf_op jit(solution)/shard_map/ppermute | solution.py:185
  84.9 16.5 %collective-permute-start.10 = (bf16[128,2048]{1,0:T(8,128)(2,1)}, bf16[128,2048]{1,0:T(8,128)(2,1)}, u32[]{:S(2)}, u32[]{:S(2)}) collective-permute-start(bf16[128,2048]{1,0:T(8,128)(2,1)} %collective-permute-done.9.refs_0_.refs_2_), channel_id=1, source_target_pairs={{0,16},{16,0},{32,48},{48,32},{64,80},{80,64},{96,112},{112,96},{1... | collective-permute-start | bytes 1572872 | tf_op jit(solution)/shard_map/ppermute | solution.py:189
  84.9 16.5 %collective-permute-start.12 = (bf16[128,2048]{1,0:T(8,128)(2,1)}, bf16[128,2048]{1,0:T(8,128)(2,1)}, u32[]{:S(2)}, u32[]{:S(2)}) collective-permute-start(bf16[128,2048]{1,0:T(8,128)(2,1)} %collective-permute-done.11.refs_2_.refs_4_), channel_id=1, source_target_pairs={{0,16},{16,0},{32,48},{48,32},{64,80},{80,64},{96,112},{112,96},{1... | collective-permute-start | bytes 1572872 | tf_op jit(solution)/shard_map/ppermute | solution.py:189
  88.2 2.4 %collective-permute-start.15 = (bf16[64,2048]{1,0:T(8,128)(2,1)S(1)}, bf16[64,2048]{1,0:T(8,128)(2,1)S(1)}, u32[]{:S(2)}, u32[]{:S(2)}) collective-permute-start(bf16[64,2048]{1,0:T(8,128)(2,1)S(1)} %collective-permute-done.13.refs_0_.refs_2_), channel_id=1, source_target_pairs={{0,16},{16,0},{32,48},{48,32},{64,80},{80,64},{96,112},{112,96},{1... | collective-permute-start | bytes 786440 | tf_op jit(solution)/shard_map/ppermute | solution.py:189
  90.5 1.5 collective-permute-start.16
  93.4 0.7 copy-start.4
  94.1 0.7 copy-start.6
  94.8 0.7 copy-start.8
  95.5 0.7 copy-start.10
  96.2 0.7 copy-start.19
  96.9 11.5 %all-to-all-start.7 = ((bf16[4,128,256]{2,1,0:T(8,128)(2,1)}), bf16[4,128,256]{2,1,0:T(8,128)(2,1)}, u32[]{:S(2)}, u32[]{:S(2)}) async-start(bf16[4,128,256]{2,1,0:T(8,128)(2,1)} %copy-done.19), calls=%async_computation.7 | async-start | bytes 524288 | tf_op jit(solution)/shard_map/all_to_all | solution.py:193
  104.2 0.8 copy-start.15
  105.0 0.7 copy-start.22
  108.4 15.7 %copy-start.23 = (f32[128,512]{1,0:T(8,128)S(1)}, f32[128,512]{1,0:T(8,128)}, u32[]{:S(2)}) copy-start(f32[128,512]{1,0:T(8,128)} %copy-done.22) | copy-start | bytes 786436
  108.5 12.2 %all-to-all-start.5 = ((bf16[4,128,512]{2,1,0:T(8,128)(2,1)}), bf16[4,128,512]{2,1,0:T(8,128)(2,1)S(1)}, u32[]{:S(2)}, u32[]{:S(2)}) async-start(bf16[4,128,512]{2,1,0:T(8,128)(2,1)} %copy-done.15), calls=%async_computation.5 | async-start | bytes 1048576 | tf_op jit(solution)/shard_map/all_to_all | solution.py:193
  112.1 1.0 copy-start.21
  120.6 11.5 %all-to-all-start.4 = ((bf16[4,128,512]{2,1,0:T(8,128)(2,1)}), bf16[4,128,512]{2,1,0:T(8,128)(2,1)S(1)}, u32[]{:S(2)}, u32[]{:S(2)}) async-start(bf16[4,128,512]{2,1,0:T(8,128)(2,1)} %shard_map.50), calls=%async_computation.4 | async-start | bytes 1048576 | tf_op jit(solution)/shard_map/all_to_all | solution.py:193
  132.2 11.5 %all-to-all-start.6 = ((bf16[4,128,512]{2,1,0:T(8,128)(2,1)}), bf16[4,128,512]{2,1,0:T(8,128)(2,1)S(1)}, u32[]{:S(2)}, u32[]{:S(2)}) async-start(bf16[4,128,512]{2,1,0:T(8,128)(2,1)} %shard_map.53), calls=%async_computation.6 | async-start | bytes 1048576 | tf_op jit(solution)/shard_map/all_to_all | solution.py:193
  143.7 14.7 %all-to-all-start.8 = ((bf16[4,128,256]{2,1,0:T(8,128)(2,1)}), bf16[4,128,256]{2,1,0:T(8,128)(2,1)S(1)}, u32[]{:S(2)}, u32[]{:S(2)}) async-start(bf16[4,128,256]{2,1,0:T(8,128)(2,1)} %shard_map.56), calls=%async_computation.8 | async-start | bytes 524288 | tf_op jit(solution)/shard_map/all_to_all | solution.py:193
  153.0 5.4 %copy-start.5 = (bf16[64,2048]{1,0:T(8,128)(2,1)S(1)}, bf16[64,2048]{1,0:T(8,128)(2,1)}, u32[]{:S(2)}) copy-start(bf16[64,2048]{1,0:T(8,128)(2,1)} %copy-done.4) | copy-start | bytes 786436
  153.0 5.4 %copy-start.7 = (bf16[64,2048]{1,0:T(8,128)(2,1)S(1)}, bf16[64,2048]{1,0:T(8,128)(2,1)}, u32[]{:S(2)}) copy-start(bf16[64,2048]{1,0:T(8,128)(2,1)} %copy-done.6) | copy-start | bytes 786436
  153.1 5.4 %copy-start.9 = (bf16[64,2048]{1,0:T(8,128)(2,1)S(1)}, bf16[64,2048]{1,0:T(8,128)(2,1)}, u32[]{:S(2)}) copy-start(bf16[64,2048]{1,0:T(8,128)(2,1)} %copy-done.8) | copy-start | bytes 786436
  153.1 5.4 %copy-start.11 = (bf16[64,2048]{1,0:T(8,128)(2,1)S(1)}, bf16[64,2048]{1,0:T(8,128)(2,1)}, u32[]{:S(2)}) copy-start(bf16[64,2048]{1,0:T(8,128)(2,1)} %copy-done.10) | copy-start | bytes 786436
  156.4 2.0 %copy-start = (f32[512,2048]{1,0:T(8,128)}, f32[512,2048]{1,0:T(8,128)S(1)}, u32[]{:S(2)}) copy-start(f32[512,2048]{1,0:T(8,128)S(1)} %shard_map.54.refs_0_) | copy-start | bytes 12582916
  158.4 2.2 %copy-start.1 = (f32[512,2048]{1,0:T(8,128)S(1)}, f32[512,2048]{1,0:T(8,128)}, u32[]{:S(2)}) copy-start(f32[512,2048]{1,0:T(8,128)} %copy-done) | copy-start | bytes 12582916
where the time goes:
time: 192 us; the launch traced here: 189 us
  starting transfers between devices  53.9 us (28%)
  waiting for transfers between devices  51.2 us (27%)
  Pallas kernels  32.3 us (17%)
  blocking collectives  25.7 us (13%)
  local copies, waits for them, and re-layouts  24.4 us (13%)
    all_to_all x9, waiting for transfers between devices, exchange(): return lax.all_to_all(parts, axis, 0, 0)  44.5 us
    all_to_all x9, starting transfers between devices, exchange(): return lax.all_to_all(parts, axis, 0, 0)  43.9 us
    all_to_all x1, blocking collectives, exchange(): return lax.all_to_all(parts, axis, 0, 0)  25.7 us
    unnamed x52, local copies, waits for them, and re-layouts  19.9 us
    pallas_call x3, Pallas kernels, body(): call(functools.partial(product_two_kernel, chunks, len(held), first, last...  10.8 us
    pallas_call x4, Pallas kernels, body(): call(functools.partial(product_one_kernel, slots, len(held)), (shape(4, 1...  10.6 us
    ppermute x8, starting transfers between devices, shift(): lax.ppermute(array, axis, [(i, (i + step) % size) for i in range(size)])  8.41 us
    pallas_call x4, Pallas kernels, body(): call(functools.partial(square_kernel, slots), shape(4, 128, width), 4, by...  6.28 us
  transfers between devices with their start and end apart: 26, of which 10 were waited for; matrix products, arithmetic and copies ran while one was open for 2% of the time, Pallas kernels for 15%

commit v1 on v0

v1 whole, which is shorter than its diff:
```python
import functools

import jax
import jax.numpy as jnp
from jax import lax
from jax.experimental import pallas as pl
from jax.experimental.pallas import tpu as pltpu
from jax.sharding import PartitionSpec as P

BLK = 32
BF = jnp.bfloat16
F32 = jnp.float32
VMEM = pl.BlockSpec(memory_space=pltpu.VMEM)
SMEM = pl.BlockSpec(memory_space=pltpu.SMEM)
NT = (((1,), (1,)), ((), ()))
NN = (((1,), (0,)), ((), ()))

SLOTS = (0, -1, 1, -2, 2, -3, 3, 4)
EARLY = 3
HALVES = 2


def call(kernel, out_shape, n_in, scratch=(), flops=0, byts=0, mib=24, aliases={}):
    return pl.pallas_call(
        kernel,
        out_shape=out_shape,
        in_specs=[SMEM] + [VMEM] * (n_in - 1),
        out_specs=jax.tree.map(lambda _: VMEM, out_shape),
        scratch_shapes=list(scratch),
        input_output_aliases=aliases,
        compiler_params=pltpu.CompilerParams(vmem_limit_bytes=mib << 20),
        cost_estimate=pl.CostEstimate(flops=flops, bytes_accessed=byts, transcendentals=0),
    )


def shape(*dims, dtype=BF):
    return jax.ShapeDtypeStruct(dims, dtype)


def iota(dims, axis):
    return lax.broadcasted_iota(jnp.int32, dims, axis)


def dot(a, b, dims=NN):
    return lax.dot_general(a, b, dims, preferred_element_type=F32)


def row_of_slot(index, z, core, layer):
    slot = index // 8
    other = (index // 4) % 2
    offset = jnp.where(slot == 7, 4, jnp.where(slot % 2 == 1, -((slot + 1) // 2), slot // 2))
    chip = lax.rem(z + offset + 8, 8)
    band = 2 * chip + lax.rem(core + other, 2)
    return 16 * band + 4 * layer + index % 4


def prep_kernel(s_ref, *refs):
    both_ref, local_ref, cube_ref, density_ref, left_ref, mk_ref, mt_ref, ms_ref, mc_ref = refs
    z, core, col, layer = s_ref[0], s_ref[1], s_ref[2], s_ref[3]
    wide = (iota((64, 2048), 0) == iota((64, 2048), 1) // BLK).astype(BF)
    roll = (iota((16, 16), 1) == lax.rem(iota((16, 16), 0) + 4 * col, 16)).astype(BF)
    local = dot(dot(roll, local_ref[...].astype(BF)).astype(BF), wide).astype(BF)
    for quarter in range(4):
        start = pl.multiple_of(128 * lax.rem(col + quarter, 4), 128)
        for block in range(4):
            at = 4 * quarter + block
            left_ref[pl.ds(BLK * at, BLK), :] = (
                density_ref[pl.ds(start + BLK * block, BLK), :] * local[at : at + 1, :]
            )
    at = iota((64, 1024), 1)
    block_row = 16 * (at // 64) + at % 16
    mine_too = (at // 16) % 4
    share = row_of_slot(iota((64, 1024), 0), z, core, layer)
    pick = jnp.where((block_row == share) & (mine_too == col), 1.0, 0.0).astype(BF)
    both = both_ref[...].reshape(1024, 128)
    mk = dot(pick, both)[:, :64].astype(BF)
    mt = jnp.zeros((64, 64), F32)
    ms = jnp.zeros((16, 64), F32)
    square_row = iota((16, 1024), 0) + 16 * (2 * z + core)
    square_at = iota((16, 1024), 1)
    square_block = 16 * (square_at // 64) + square_at % 16
    for n in range(4):
        mine = (block_row == 64 * col + iota((64, 1024), 0)) & (mine_too == n)
        rows = dot(jnp.where(mine, 1.0, 0.0).astype(BF), both)[:, :64].astype(BF)
        column = 64 * n + iota((64, 64), 1)
        take = (column == row_of_slot(iota((64, 64), 0), z, core, layer)).astype(BF)
        mt = mt + dot(take, rows, NT)
        own = (square_block == square_row) & ((square_at // 16) % 4 == n)
        rows = dot(jnp.where(own, 1.0, 0.0).astype(BF), both)[:, 64:].astype(BF)
        ms = ms + dot(dot(roll, rows).astype(BF), take, NT)
    mk_ref[...] = dot(mk, wide)
    mt_ref[...] = dot(mt.astype(BF), wide)
    ms_ref[...] = dot(ms.astype(BF), wide)
    mc_ref[...] = -2.0 * dot(dot(roll, cube_ref[...].astype(BF)).astype(BF), wide)


def load_pieces(piece_refs, mask_ref, block_row, out_ref):
    done = 0
    for ref in piece_refs:
        for block in range(ref.shape[0] // BLK):
            row = block_row + done // BLK
            keep = jnp.broadcast_to(mask_ref[pl.ds(row, 1), :], (BLK, 2048)).astype(BF)
            out_ref[pl.ds(done, BLK), :] = ref[pl.ds(BLK * block, BLK), :] * keep
            done += BLK


def load_slots(slots, where, gathered_ref, mask_ref, out_ref):
    z, core = where
    for n, slot in enumerate(slots):
        chip = lax.rem(z + SLOTS[slot] + 8, 8)
        for other in range(2):
            start = pl.multiple_of(128 * (2 * chip + lax.rem(core + other, 2)), 128)
            for block in range(4):
                row = 8 * slot + 4 * other + block
                keep = jnp.broadcast_to(mask_ref[pl.ds(row, 1), :], (BLK, 2048)).astype(BF)
                out_ref[pl.ds(256 * n + 128 * other + BLK * block, BLK), :] = (
                    gathered_ref[pl.ds(start + BLK * block, BLK), :] * keep
                )


def product_one_kernel(slots, halves, n_pieces, s_ref, left_ref, mt_ref, *refs):
    pieces, outs, right = refs[:n_pieces], refs[n_pieces:-1], refs[-1]
    if n_pieces > 1:
        load_pieces(pieces, mt_ref, 8 * slots[0], right)
    else:
        load_slots(slots, (s_ref[0], s_ref[1]), pieces[0], mt_ref, right)
    height = 128 // halves
    for start in range(0, right.shape[0], 256):
        block = dot(left_ref[...], right[pl.ds(start, 256), :], NT)
        for half in range(halves):
            for quarter in range(4):
                row = 128 * quarter + height * half
                out = outs[4 * half + quarter]
                out[:, pl.ds(start, 256)] = block[row : row + height].astype(out.dtype)


def square_kernel(first_slot, first_block, s_ref, ms_ref, own_ref, a_ref, b_ref, c_ref, out_ref):
    height, width = out_ref.shape
    total = own_ref[...] + a_ref[...].astype(F32) + b_ref[...].astype(F32) + c_ref[...].astype(F32)
    for block in range(height // BLK):
        rows = slice(BLK * block, BLK * block + BLK)
        keep = ms_ref[pl.ds(first_block + block, 1), pl.ds(256 * first_slot, width)]
        out_ref[rows, :] = (total[rows] * keep).astype(BF)


def right_kernel(s_ref, mk_ref, gathered_ref, out_ref):
    load_slots(range(len(SLOTS)), (s_ref[0], s_ref[1]), gathered_ref, mk_ref, out_ref)


def product_two_kernel(half, n_early, s_ref, mc_ref, right_ref, *refs):
    z, core, col, layer = s_ref[0], s_ref[1], s_ref[2], s_ref[3]
    early, late, outs = refs[:n_early], refs[n_early : n_early + 4], refs[n_early + 4 : n_early + 8]
    square, total = refs[-2:]
    height = 128 // HALVES
    skip = 256 * EARLY if n_early else 0
    for quarter in range(4):
        rows = pl.ds(height * quarter, height)
        if n_early:
            square[rows, pl.ds(0, skip)] = early[quarter][pl.ds(height * half, height), :]
        square[rows, pl.ds(skip, 2048 - skip)] = late[quarter][...]
    for cols in range(0, 2048, 256):
        block = dot(square[...], right_ref[:, pl.ds(cols, 256)])
        for n in range(4 * height // BLK):
            row = 4 * (n // (height // BLK)) + height // BLK * half + n % (height // BLK)
            rows = slice(BLK * n, BLK * n + BLK)
            total[rows, pl.ds(cols, 256)] = block[rows] * mc_ref[pl.ds(row, 1), pl.ds(cols, 256)]
    for slot in range(len(SLOTS)):
        chip = lax.rem(z + SLOTS[slot] + 8, 8)

        @pl.when(chip // 2 == col)
        def _():
            for other in range(2):
                band = 2 * chip + lax.rem(core + other, 2) - 4 * col
                cols = pl.ds(pl.multiple_of(512 * band + 128 * layer, 128), 128)
                total[:, cols] += 3.0 * square[:, pl.ds(256 * slot + 128 * other, 128)].astype(F32)

    for share in range(4):
        cols = pl.ds(pl.multiple_of(512 * lax.rem(layer + share, 4), 512), 512)
        outs[share][...] = total[:, cols].astype(outs[share].dtype)


def finish_kernel(s_ref, *refs):
    col, out_ref = s_ref[2], refs[-1]
    height = 128 // HALVES
    for half in range(HALVES):
        own_ref, *got = refs[4 * half : 4 * half + 4]
        for quarter in range(4):
            rows = pl.ds(height * quarter, height)
            total = own_ref[rows, :]
            for ref in got:
                total = total + ref[rows, :].astype(F32)
            start = 128 * lax.rem(col + quarter, 4) + height * half
            out_ref[pl.ds(pl.multiple_of(start, height), height), :] = total.astype(BF)


def shift(array, axis, step, size):
    return lax.ppermute(array, axis, [(i, (i + step) % size) for i in range(size)])


def swap(array):
    return lax.ppermute(array, "row", [(i, i ^ 1) for i in range(16)])


def exchange(parts, axis):
    got = [shift(part, axis, step, 4) for part, step in zip(parts, (1, 2, 3))]
    return got[2], got[1], got[0]


def gather_patterns(pattern_density, pattern_square):
    both = jnp.concatenate([pattern_density, pattern_square], 1).astype(BF)
    return lax.all_to_all(jnp.broadcast_to(both, (64, 16, 128)), ("row", "col"), 0, 0)


def body(density, pattern_density, pattern_square, pattern_cube):
    row, col, layer = lax.axis_index("row"), lax.axis_index("col"), lax.axis_index("rep")
    where = jnp.stack([row // 2, row % 2, col, layer]).astype(jnp.int32)
    own = lax.dynamic_slice_in_dim(density, 128 * layer, 128, 0)

    gathered = lax.all_gather(own, "row", axis=0, tiled=True)
    near = [own, shift(own, "row", 2, 16), shift(own, "row", -2, 16)][:EARLY]
    early = [piece for one in near for piece in (one, swap(one))]

    both = gather_patterns(pattern_density, pattern_square)
    left, mk, mt, ms, mc = call(
        prep_kernel,
        (
            shape(512, 2048),
            shape(64, 2048, dtype=F32),
            shape(64, 2048, dtype=F32),
            shape(16, 2048, dtype=F32),
            shape(16, 2048, dtype=F32),
        ),
        5,
        flops=2 * 200 * 256 * 2048,
        byts=6 << 20,
    )(where, both, pattern_density, pattern_cube, density)

    def start(slots, halves, held):
        height, width = 128 // halves, 256 * len(slots)
        parts = call(
            functools.partial(product_one_kernel, slots, halves, len(held)),
            ((shape(height, width, dtype=F32),) + (shape(height, width),) * 3) * halves,
            3 + len(held),
            [pltpu.VMEM((width, 2048), BF)],
            flops=2 * 512 * 2048 * width,
            byts=2 * 2048 * (512 + width),
        )(where, left, mt, *held)
        squares = []
        for half in range(halves):
            mine, *others = parts[4 * half : 4 * half + 4]
            mine = call(
                functools.partial(square_kernel, slots[0], half * (4 // halves)),
                shape(height, width),
                6,
                byts=2 * height * width * 6,
            )(where, ms, mine, *exchange(others, "col"))
            squares.append((mine, *exchange([mine] * 3, "col")))
        return squares

    first = start(range(EARLY), 1, early)[0] if EARLY else ()
    first, gathered = lax.optimization_barrier((first, gathered))
    squares = start(range(EARLY, len(SLOTS)), HALVES, [gathered])
    right = call(right_kernel, shape(2048, 2048), 3, byts=16 << 20)(where, mk, gathered)
    results = []
    for half in range(HALVES):
        height = 512 // HALVES
        mine, *others = call(
            functools.partial(product_two_kernel, half, len(first)),
            (shape(height, 512, dtype=F32),) + (shape(height, 512),) * 3,
            3 + len(first) + 4,
            [pltpu.VMEM((height, 2048), BF), pltpu.VMEM((height, 2048), F32)],
            flops=2 * height * 2048 * 2048,
            byts=10 << 20,
        )(where, mc, right, *first, *squares[half])
        results += [mine, *exchange(others, "rep")]
    return call(finish_kernel, shape(512, 512), 1 + len(results), byts=3 << 20)(where, *results)


def solution(mesh):
    placed = (P("row", "col"), P("row", "col"), P("row", "col"), P("row", "col"))
    return jax.shard_map(
        body, mesh=mesh, in_specs=placed, out_specs=P("row", ("col", "rep")), check_vma=False
    )
```

time: 192 us -> 153 us (0.80); the launches traced: 189 us -> 153 us
  blocking collectives: 25.7 us -> 0 us
  local copies, waits for them, and re-layouts: 24.4 us -> 9.6 us
  between operations: 0.34 us -> 13.6 us
  Pallas kernels: 32.3 us -> 22.4 us
  waiting for transfers between devices: 51.2 us -> 59.8 us
  starting transfers between devices: 53.9 us -> 45.9 us
    ppermute x8 -> x26, waiting for transfers between devices: 5.15 us -> 45.1 us  [shift(): lax.ppermute(array, axis, [(i, (i + step) % size) for i in range(size)])]
    all_to_all x9 -> x1, starting transfers between devices: 43.9 us -> 13 us  [gather_patterns(): lax.all_to_all(jnp.broadcast_to(both, (64, 16, 128)), ('row', 'col'), 0, 0)]
    all_to_all x9 -> x1, waiting for transfers between devices: 44.5 us -> 14.6 us  [gather_patterns(): lax.all_to_all(jnp.broadcast_to(both, (64, 16, 128)), ('row', 'col'), 0, 0)]
    all_to_all x1 -> x0, blocking collectives: 25.7 us -> none  [exchange(): return lax.all_to_all(parts, axis, 0, 0)]
    ppermute x8 -> x26, starting transfers between devices: 8.41 us -> 32.2 us  [shift(): lax.ppermute(array, axis, [(i, (i + step) % size) for i in range(size)])]
    unnamed x52 -> x22, local copies, waits for them, and re-layouts: 19.9 us -> 6.83 us
    pallas_call x12 -> x9, Pallas kernels: 29.2 us -> 19.3 us  [the longest x2 8.04 us: start(): call(functools.partial(product_one_kernel, slots, halves, len(held)), ((s...]
    slice x2 -> x0, local copies, waits for them, and re-layouts: 1.94 us -> none  [body(): first, second = (first[:64], second[64:])]
  transfers between devices with their start and end apart: 26 -> 31, of which waited for: 10 -> 15; matrix products, arithmetic and copies ran while one was open for 2% -> 2% of each run, Pallas kernels for 15% -> 11%
where the time goes in v1:
time: 153 us
  waiting for transfers between devices  59.8 us (39%)
  starting transfers between devices  45.9 us (30%)
  Pallas kernels  22.4 us (15%)
  between operations  13.6 us (9%)
  local copies, waits for them, and re-layouts  9.6 us (6%)
  other arithmetic  1.56 us (1%)
    ppermute x26, waiting for transfers between devices, shift(): lax.ppermute(array, axis, [(i, (i + step) % size) for i in range(size)])  45.1 us
    ppermute x26, starting transfers between devices, shift(): lax.ppermute(array, axis, [(i, (i + step) % size) for i in range(size)])  32.2 us
    all_to_all x1, waiting for transfers between devices, gather_patterns(): lax.all_to_all(jnp.broadcast_to(both, (64, 16, 128)), ('row', 'col'), 0, 0)  14.6 us
    all_to_all x1, starting transfers between devices, gather_patterns(): lax.all_to_all(jnp.broadcast_to(both, (64, 16, 128)), ('row', 'col'), 0, 0)  13 us
    pallas_call x2, Pallas kernels, start(): call(functools.partial(product_one_kernel, slots, halves, len(held)), ((s...  8.04 us
    unnamed x22, local copies, waits for them, and re-layouts  6.83 us
    pallas_call x2, Pallas kernels, body(): call(functools.partial(product_two_kernel, half, len(first)), (shape(heig...  6.5 us
    pallas_call x1, Pallas kernels, body(): call(prep_kernel, (shape(512, 2048), shape(64, 2048, dtype=F32), shape(64...  3.07 us
  transfers between devices with their start and end apart: 31, of which 15 were waited for; matrix products, arithmetic and copies ran while one was open for 2% of the time, Pallas kernels for 11%

profile of v1, /device:TPU:32, one launch (start us, length us, event | category | flops | bytes accessed | tf_op | source)
XLA Modules:
  0.0 152.8 jit_solution(9985450235999747683)
XLA Ops:
  6.5 2.0 %constant_dynamic-slice_fusion.refs_0_ = bf16[128,2048]{1,0:T(8,128)(2,1)} fusion(bf16[512,2048]{1,0:T(8,128)(2,1)} %refs_3_.1, s32[]{:T(128)S(6)} %select_n.16), kind=kLoop, calls=%fused_computation.2 | loop fusion | bytes 1048580 | tf_op jit(solution)/shard_map/dynamic_slice | solution.py:217
  8.6 0.0 all-gather.2.cloned.1.call-update
  8.6 2.0 %collective-permute-start.1 = (bf16[128,2048]{1,0:T(8,128)(2,1)}, bf16[128,2048]{1,0:T(8,128)(2,1)}, u32[]{:S(2)}, u32[]{:S(2)}) collective-permute-start(bf16[128,2048]{1,0:T(8,128)(2,1)} %constant_dynamic-slice_fusion.refs_0_), channel_id=1, source_target_pairs={{0,32},{16,48},{32,64},{48,80},{64,96},{80,112},{96,128},{112,144}... | collective-permute-start | bytes 1572872 | tf_op jit(solution)/shard_map/ppermute | solution.py:197
  10.6 0.1 collective-permute-start.3
  10.7 0.7 convert.6
  11.4 0.7 convert.7
  12.1 0.1 pad_maximum_fusion
  12.2 0.7 broadcast_in_dim.3
  12.9 13.0 %all-to-all-start = ((bf16[64,16,128]{2,1,0:T(8,128)(2,1)}), bf16[64,16,128]{2,1,0:T(8,128)(2,1)S(1)}, u32[]{:S(2)}, u32[]{:S(2)}) async-start(bf16[64,16,128]{2,1,0:T(8,128)(2,1)} %broadcast_in_dim.3), calls=%async_computation | async-start | bytes 524288 | tf_op jit(solution)/shard_map/all_to_all | solution.py:211
  25.9 0.2 collective-permute-start
  26.1 0.4 collective-permute-start.2
  26.5 0.1 collective-permute-start.4
  26.7 0.1 pad_add_fusion.s_ref
  26.7 14.6 %all-to-all-done.refs_0_ = bf16[64,16,128]{2,1,0:T(8,128)(2,1)S(1)} async-done(((bf16[64,16,128]{2,1,0:T(8,128)(2,1)}), bf16[64,16,128]{2,1,0:T(8,128)(2,1)S(1)}, u32[]{:S(2)}, u32[]{:S(2)}) %all-to-all-start) | async-done | bytes 262176 | tf_op jit(solution)/shard_map/all_to_all | solution.py:211
  41.4 3.1 %shard_map.46 = (bf16[512,2048]{1,0:T(8,128)(2,1)S(1)}, f32[64,2048]{1,0:T(8,128)S(1)}, f32[64,2048]{1,0:T(8,128)S(1)}, f32[16,2048]{1,0:T(8,128)S(1)}, f32[16,2048]{1,0:T(8,128)S(1)}) custom-call(s32[4]{0:T(128)S(1)} %pad_add_fusion.s_ref, bf16[64,16,128]{2,1,0:T(8,128)(2,1)S(1)} %all-to-all-done.refs_0_, s32[16,64]{1,0:T(8,128)S(1)} %copy-done.9, ...), custom_call_target="tpu_custom_call" | custom-call | flops 209715200 | bytes 6291456 | tf_op jit(solution)/shard_map/pallas_call | solution.py:224
  44.5 0.8 copy-done.5
  45.3 4.6 %shard_map.47 = (f32[128,768]{1,0:T(8,128)S(1)}, bf16[128,768]{1,0:T(8,128)(2,1)S(1)}, bf16[128,768]{1,0:T(8,128)(2,1)S(1)}, bf16[128,768]{1,0:T(8,128)(2,1)S(1)}) custom-call(s32[4]{0:T(128)S(1)} %pad_add_fusion.s_ref, bf16[512,2048]{1,0:T(8,128)(2,1)S(1)} %get-tuple-element.38.left_ref, f32[64,2048]{1,0:T(8,128)S(1)} %get-tuple-element.39.mt_ref, ...), custom_call_target="tpu_custom_call" | custom-call | flops 1610612736 | bytes 5242880 | tf_op jit(solution)/shard_map/pallas_call | solution.py:240
  49.9 1.4 collective-permute-start.5
  51.3 1.3 collective-permute-start.6
  52.6 0.5 collective-permute-start.7
  53.1 4.7 %collective-permute-done.5.a_ref = bf16[128,768]{1,0:T(8,128)(2,1)S(1)} collective-permute-done((bf16[128,768]{1,0:T(8,128)(2,1)S(1)}, bf16[128,768]{1,0:T(8,128)(2,1)S(1)}, u32[]{:S(2)}, u32[]{:S(2)}) %collective-permute-start.5) | collective-permute-done | bytes 196640 | tf_op jit(solution)/shard_map/ppermute | solution.py:197
  57.8 2.8 %collective-permute-done.6.b_ref = bf16[128,768]{1,0:T(8,128)(2,1)S(1)} collective-permute-done((bf16[128,768]{1,0:T(8,128)(2,1)S(1)}, bf16[128,768]{1,0:T(8,128)(2,1)S(1)}, u32[]{:S(2)}, u32[]{:S(2)}) %collective-permute-start.6) | collective-permute-done | bytes 196640 | tf_op jit(solution)/shard_map/ppermute | solution.py:197
  60.6 3.0 %collective-permute-done.7.c_ref = bf16[128,768]{1,0:T(8,128)(2,1)S(1)} collective-permute-done((bf16[128,768]{1,0:T(8,128)(2,1)S(1)}, bf16[128,768]{1,0:T(8,128)(2,1)S(1)}, u32[]{:S(2)}, u32[]{:S(2)}) %collective-permute-start.7) | collective-permute-done | bytes 196640 | tf_op jit(solution)/shard_map/ppermute | solution.py:197
  63.6 0.7 shard_map.48.refs_0_
  64.3 0.1 collective-permute-start.10
  64.3 3.2 %collective-permute-start.8 = (bf16[128,768]{1,0:T(8,128)(2,1)S(1)}, bf16[128,768]{1,0:T(8,128)(2,1)S(1)}, u32[]{:S(2)}, u32[]{:S(2)}) collective-permute-start(bf16[128,768]{1,0:T(8,128)(2,1)S(1)} %shard_map.48.refs_0_), channel_id=1, source_target_pairs={{0,12},{4,0},{8,4},{12,8},{1,13},{5,1},{9,5},{13,9},{2,14},{6,2},{... | collective-permute-start | bytes 589832 | tf_op jit(solution)/shard_map/ppermute | solution.py:197
  67.6 0.2 collective-permute-start.9
  67.7 8.9 %collective-permute-done.10.refs_3_ = bf16[128,768]{1,0:T(8,128)(2,1)S(1)} collective-permute-done((bf16[128,768]{1,0:T(8,128)(2,1)S(1)}, bf16[128,768]{1,0:T(8,128)(2,1)S(1)}, u32[]{:S(2)}, u32[]{:S(2)}) %collective-permute-start.10) | collective-permute-done | bytes 196640 | tf_op jit(solution)/shard_map/ppermute | solution.py:197
  76.6 0.0 all-gather.2.cloned.1.call-done.gathered_ref.refs_0_
  76.6 3.4 %copy-done = bf16[2048,2048]{1,0:T(8,128)(2,1)S(1)} copy-done((bf16[2048,2048]{1,0:T(8,128)(2,1)S(1)}, bf16[2048,2048]{1,0:T(8,128)(2,1)}, u32[]{:S(2)}) %copy-start) | copy-done | bytes 8388632
  80.0 1.6 %copy-done.4 = bf16[512,2048]{1,0:T(8,128)(2,1)S(1)} copy-done((bf16[512,2048]{1,0:T(8,128)(2,1)S(1)}, bf16[512,2048]{1,0:T(8,128)(2,1)}, u32[]{:S(2)}) %copy-start.4) | copy-done | bytes 2097176
  81.6 1.0 copy-done.8
  82.6 3.5 %shard_map.50 = (f32[64,1280]{1,0:T(8,128)S(1)}, bf16[64,1280]{1,0:T(8,128)(2,1)S(1)}, bf16[64,1280]{1,0:T(8,128)(2,1)S(1)}, bf16[64,1280]{1,0:T(8,128)(2,1)S(1)...) custom-call(s32[4]{0:T(128)S(1)} %pad_add_fusion.s_ref, ...), custom_call_target="tpu_custom_call" | custom-call | flops 2684354560 | bytes 7340032 | tf_op jit(solution)/shard_map/pallas_call | solution.py:240
  86.1 3.0 %collective-permute-start.20 = (bf16[64,1280]{1,0:T(8,128)(2,1)S(1)}, bf16[64,1280]{1,0:T(8,128)(2,1)S(1)}, u32[]{:S(2)}, u32[]{:S(2)}) collective-permute-start(bf16[64,1280]{1,0:T(8,128)(2,1)S(1)} %get-tuple-element.58), channel_id=1, source_target_pairs={{0,12},{4,0},{8,4},{12,8},{1,13},{5,1},{9,5},{13,9},{2,14},{6,2},{... | collective-permute-start | bytes 491528 | tf_op jit(solution)/shard_map/ppermute | solution.py:197
  89.1 1.0 collective-permute-start.22
  90.1 2.3 %collective-permute-start.11 = (bf16[64,1280]{1,0:T(8,128)(2,1)S(1)}, bf16[64,1280]{1,0:T(8,128)(2,1)S(1)}, u32[]{:S(2)}, u32[]{:S(2)}) collective-permute-start(bf16[64,1280]{1,0:T(8,128)(2,1)S(1)} %get-tuple-element.50), channel_id=1, source_target_pairs={{0,12},{4,0},{8,4},{12,8},{1,13},{5,1},{9,5},{13,9},{2,14},{6,2},{... | collective-permute-start | bytes 491528 | tf_op jit(solution)/shard_map/ppermute | solution.py:197
  92.3 2.3 %collective-permute-start.12 = (bf16[64,1280]{1,0:T(8,128)(2,1)S(1)}, bf16[64,1280]{1,0:T(8,128)(2,1)S(1)}, u32[]{:S(2)}, u32[]{:S(2)}) collective-permute-start(bf16[64,1280]{1,0:T(8,128)(2,1)S(1)} %get-tuple-element.51), channel_id=1, source_target_pairs={{0,8},{4,12},{8,0},{12,4},{1,9},{5,13},{9,1},{13,5},{2,10},{6,14},... | collective-permute-start | bytes 491528 | tf_op jit(solution)/shard_map/ppermute | solution.py:197
  94.7 2.2 %collective-permute-done.20.a_ref = bf16[64,1280]{1,0:T(8,128)(2,1)S(1)} collective-permute-done((bf16[64,1280]{1,0:T(8,128)(2,1)S(1)}, bf16[64,1280]{1,0:T(8,128)(2,1)S(1)}, u32[]{:S(2)}, u32[]{:S(2)}) %collective-permute-start.20) | collective-permute-done | bytes 163872 | tf_op jit(solution)/shard_map/ppermute | solution.py:197
  96.8 1.0 collective-permute-done.21.b_ref
  97.8 3.2 %collective-permute-done.22.c_ref = bf16[64,1280]{1,0:T(8,128)(2,1)S(1)} collective-permute-done((bf16[64,1280]{1,0:T(8,128)(2,1)S(1)}, bf16[64,1280]{1,0:T(8,128)(2,1)S(1)}, u32[]{:S(2)}, u32[]{:S(2)}) %collective-permute-start.22) | collective-permute-done | bytes 163872 | tf_op jit(solution)/shard_map/ppermute | solution.py:197
  101.0 0.6 shard_map.53.refs_4_
  101.6 0.9 collective-permute-start.23
  102.5 1.6 %collective-permute-start.24 = (bf16[64,1280]{1,0:T(8,128)(2,1)S(1)}, bf16[64,1280]{1,0:T(8,128)(2,1)S(1)}, u32[]{:S(2)}, u32[]{:S(2)}) collective-permute-start(bf16[64,1280]{1,0:T(8,128)(2,1)S(1)} %shard_map.53.refs_4_), channel_id=1, source_target_pairs={{0,8},{4,12},{8,0},{12,4},{1,9},{5,13},{9,1},{13,5},{2,10},{6,14},... | collective-permute-start | bytes 491528 | tf_op jit(solution)/shard_map/ppermute | solution.py:197
  104.2 1.3 collective-permute-start.25
  105.5 1.3 shard_map.49.right_ref
  106.7 1.8 %collective-permute-done.13.c_ref = bf16[64,1280]{1,0:T(8,128)(2,1)S(1)} collective-permute-done((bf16[64,1280]{1,0:T(8,128)(2,1)S(1)}, bf16[64,1280]{1,0:T(8,128)(2,1)S(1)}, u32[]{:S(2)}, u32[]{:S(2)}) %collective-permute-start.13) | collective-permute-done | bytes 163872 | tf_op jit(solution)/shard_map/ppermute | solution.py:197
  108.5 0.6 shard_map.51.refs_4_
  109.2 0.2 collective-permute-start.14
  109.4 1.0 collective-permute-start.15
  110.4 1.3 collective-permute-start.16
  111.7 4.3 %collective-permute-done.25.refs_7_ = bf16[64,1280]{1,0:T(8,128)(2,1)S(1)} collective-permute-done((bf16[64,1280]{1,0:T(8,128)(2,1)S(1)}, bf16[64,1280]{1,0:T(8,128)(2,1)S(1)}, u32[]{:S(2)}, u32[]{:S(2)}) %collective-permute-start.25) | collective-permute-done | bytes 163872 | tf_op jit(solution)/shard_map/ppermute | solution.py:197
  116.1 3.3 %shard_map.54 = (f32[256,512]{1,0:T(8,128)S(1)}, bf16[256,512]{1,0:T(8,128)(2,1)S(1)}, bf16[256,512]{1,0:T(8,128)(2,1)S(1)}, bf16[256,512]{1,0:T(8,128)(2,1)S(1)}) custom-call(s32[4]{0:T(128)S(1)} %pad_add_fusion.s_ref, f32[16,2048]{1,0:T(8,128)S(1)} %get-tuple-element.35.mc_ref, bf16[2048,2048]{1,0:T(8,128)(2,1)S(1)} %shard_map.49.right_ref, ...), custom_call_target="tpu_custom_call" | custom-call | flops 2147483648 | bytes 10485760 | tf_op jit(solution)/shard_map/pallas_call | solution.py:267
  119.3 2.8 %collective-permute-start.26 = (bf16[256,512]{1,0:T(8,128)(2,1)S(1)}, bf16[256,512]{1,0:T(8,128)(2,1)S(1)}, u32[]{:S(2)}, u32[]{:S(2)}) collective-permute-start(bf16[256,512]{1,0:T(8,128)(2,1)S(1)} %get-tuple-element.62), channel_id=1, source_target_pairs={{0,3},{1,0},{2,1},{3,2},{4,7},{5,4},{6,5},{7,6},{8,11},{9,8},{10,9... | collective-permute-start | bytes 786440 | tf_op jit(solution)/shard_map/ppermute | solution.py:197
  122.2 0.8 collective-permute-start.27
  123.0 0.9 collective-permute-start.28
  123.8 3.2 %shard_map.52 = (f32[256,512]{1,0:T(8,128)S(1)}, bf16[256,512]{1,0:T(8,128)(2,1)S(1)}, bf16[256,512]{1,0:T(8,128)(2,1)S(1)}, bf16[256,512]{1,0:T(8,128)(2,1)S(1)}) custom-call(s32[4]{0:T(128)S(1)} %pad_add_fusion.s_ref, f32[16,2048]{1,0:T(8,128)S(1)} %get-tuple-element.35.mc_ref, bf16[2048,2048]{1,0:T(8,128)(2,1)S(1)} %shard_map.49.right_ref, ...), custom_call_target="tpu_custom_call" | custom-call | flops 2147483648 | bytes 10485760 | tf_op jit(solution)/shard_map/pallas_call | solution.py:267
  127.1 2.5 %collective-permute-start.17 = (bf16[256,512]{1,0:T(8,128)(2,1)S(1)}, bf16[256,512]{1,0:T(8,128)(2,1)S(1)}, u32[]{:S(2)}, u32[]{:S(2)}) collective-permute-start(bf16[256,512]{1,0:T(8,128)(2,1)S(1)} %get-tuple-element.54), channel_id=1, source_target_pairs={{0,3},{1,0},{2,1},{3,2},{4,7},{5,4},{6,5},{7,6},{8,11},{9,8},{10,9... | collective-permute-start | bytes 786440 | tf_op jit(solution)/shard_map/ppermute | solution.py:197
  129.6 1.5 collective-permute-start.18
  131.1 1.2 collective-permute-done.27.refs_6_
  132.2 7.2 %collective-permute-done.28.refs_7_ = bf16[256,512]{1,0:T(8,128)(2,1)S(1)} collective-permute-done((bf16[256,512]{1,0:T(8,128)(2,1)S(1)}, bf16[256,512]{1,0:T(8,128)(2,1)S(1)}, u32[]{:S(2)}, u32[]{:S(2)}) %collective-permute-start.28) | collective-permute-done | bytes 262176 | tf_op jit(solution)/shard_map/ppermute | solution.py:197
  139.5 1.2 collective-permute-done.17.refs_1_
  140.7 1.1 collective-permute-done.18.refs_2_
  141.7 2.6 %collective-permute-done.19.refs_3_ = bf16[256,512]{1,0:T(8,128)(2,1)S(1)} collective-permute-done((bf16[256,512]{1,0:T(8,128)(2,1)S(1)}, bf16[256,512]{1,0:T(8,128)(2,1)S(1)}, u32[]{:S(2)}, u32[]{:S(2)}) %collective-permute-start.19) | collective-permute-done | bytes 262176 | tf_op jit(solution)/shard_map/ppermute | solution.py:197
  144.4 1.6 %shard_map.55 = bf16[512,512]{1,0:T(8,128)(2,1)} custom-call(s32[4]{0:T(128)S(1)} %pad_add_fusion.s_ref, f32[256,512]{1,0:T(8,128)S(1)} %get-tuple-element.53.refs_0_, bf16[256,512]{1,0:T(8,128)(2,1)S(1)} %collective-permute-done.17.refs_1_, bf16[256,512]{1,0:T(8,128)(2,1)S(1)} %collective-permute-done.18.refs_2_, ...), custom_call_target="tpu_custom_call" | custom-call | bytes 3145728 | tf_op jit(solution)/shard_map/pallas_call | solution.py:276
  (37 shorter events, 0.1 us)
Async XLA Ops:
  6.5 34.8 %copy-start.1 = (bf16[512,2048]{1,0:T(8,128)(2,1)S(1)}, bf16[512,2048]{1,0:T(8,128)(2,1)}, u32[]{:S(2)}) copy-start(bf16[512,2048]{1,0:T(8,128)(2,1)} %refs_3_.1) | copy-start | bytes 6291460
  6.5 34.8 %copy-start.9 = (s32[16,64]{1,0:T(8,128)S(1)}, s32[16,64]{1,0:T(8,128)}, u32[]{:S(2)}) copy-start(s32[16,64]{1,0:T(8,128)} %refs_1_.1) | copy-start | bytes 12292
  6.5 34.8 %copy-start.10 = (s32[16,64]{1,0:T(8,128)S(1)}, s32[16,64]{1,0:T(8,128)}, u32[]{:S(2)}) copy-start(s32[16,64]{1,0:T(8,128)} %refs_2_.1) | copy-start | bytes 12292
  6.5 70.1 %all-gather.2.cloned.1.call-start = ((), (), s32[]{:S(2)}) async-start(), calls=%async_computation.1 | async-start | bytes 8912896 | tf_op jit(solution)/shard_map/all_gather | solution.py:219
  8.6 36.7 %copy-start.2 = (bf16[128,2048]{1,0:T(8,128)(2,1)S(1)}, bf16[128,2048]{1,0:T(8,128)(2,1)}, u32[]{:S(2)}) copy-start(bf16[128,2048]{1,0:T(8,128)(2,1)} %constant_dynamic-slice_fusion.refs_0_) | copy-start | bytes 1572868
  8.6 17.5 %collective-permute-start.1 = (bf16[128,2048]{1,0:T(8,128)(2,1)}, bf16[128,2048]{1,0:T(8,128)(2,1)}, u32[]{:S(2)}, u32[]{:S(2)}) collective-permute-start(bf16[128,2048]{1,0:T(8,128)(2,1)} %constant_dynamic-slice_fusion.refs_0_), channel_id=1, source_target_pairs={{0,32},{16,48},{32,64},{48,80},{64,96},{80,112},{96,128},{112,144}... | collective-permute-start | bytes 1572872 | tf_op jit(solution)/shard_map/ppermute | solution.py:197
  10.6 15.9 %collective-permute-start.3 = (bf16[128,2048]{1,0:T(8,128)(2,1)}, bf16[128,2048]{1,0:T(8,128)(2,1)}, u32[]{:S(2)}, u32[]{:S(2)}) collective-permute-start(bf16[128,2048]{1,0:T(8,128)(2,1)} %constant_dynamic-slice_fusion.refs_0_), channel_id=1, source_target_pairs={{0,224},{16,240},{32,0},{48,16},{64,32},{80,48},{96,64},{112,80},{... | collective-permute-start | bytes 1572872 | tf_op jit(solution)/shard_map/ppermute | solution.py:197
  12.9 28.4 %all-to-all-start = ((bf16[64,16,128]{2,1,0:T(8,128)(2,1)}), bf16[64,16,128]{2,1,0:T(8,128)(2,1)S(1)}, u32[]{:S(2)}, u32[]{:S(2)}) async-start(bf16[64,16,128]{2,1,0:T(8,128)(2,1)} %broadcast_in_dim.3), calls=%async_computation | async-start | bytes 524288 | tf_op jit(solution)/shard_map/all_to_all | solution.py:211
  25.9 19.4 %collective-permute-start = (bf16[128,2048]{1,0:T(8,128)(2,1)}, bf16[128,2048]{1,0:T(8,128)(2,1)}, u32[]{:S(2)}, u32[]{:S(2)}) collective-permute-start(bf16[128,2048]{1,0:T(8,128)(2,1)} %constant_dynamic-slice_fusion.refs_0_), channel_id=1, source_target_pairs={{0,16},{16,0},{32,48},{48,32},{64,80},{80,64},{96,112},{112,96},{1... | collective-permute-start | bytes 1572872 | tf_op jit(solution)/shard_map/ppermute | solution.py:201
  26.1 19.1 %collective-permute-start.2 = (bf16[128,2048]{1,0:T(8,128)(2,1)}, bf16[128,2048]{1,0:T(8,128)(2,1)}, u32[]{:S(2)}, u32[]{:S(2)}) collective-permute-start(bf16[128,2048]{1,0:T(8,128)(2,1)} %collective-permute-done.1.refs_2_), channel_id=1, source_target_pairs={{0,16},{16,0},{32,48},{48,32},{64,80},{80,64},{96,112},{112,96},{1... | collective-permute-start | bytes 1572872 | tf_op jit(solution)/shard_map/ppermute | solution.py:201
  26.5 18.8 %collective-permute-start.4 = (bf16[128,2048]{1,0:T(8,128)(2,1)}, bf16[128,2048]{1,0:T(8,128)(2,1)}, u32[]{:S(2)}, u32[]{:S(2)}) collective-permute-start(bf16[128,2048]{1,0:T(8,128)(2,1)} %collective-permute-done.3.refs_4_), channel_id=1, source_target_pairs={{0,16},{16,0},{32,48},{48,32},{64,80},{80,64},{96,112},{112,96},{1... | collective-permute-start | bytes 1572872 | tf_op jit(solution)/shard_map/ppermute | solution.py:201
  44.5 0.8 copy-start.5
  45.3 4.6 %copy-start.3 = (bf16[512,2048]{1,0:T(8,128)(2,1)}, bf16[512,2048]{1,0:T(8,128)(2,1)S(1)}, u32[]{:S(2)}) copy-start(bf16[512,2048]{1,0:T(8,128)(2,1)S(1)} %get-tuple-element.38.left_ref) | copy-start | bytes 6291460
  45.3 4.6 %copy-start.7 = (f32[64,2048]{1,0:T(8,128)}, f32[64,2048]{1,0:T(8,128)S(1)}, u32[]{:S(2)}) copy-start(f32[64,2048]{1,0:T(8,128)S(1)} %get-tuple-element.39.mt_ref) | copy-start | bytes 1572868
  49.9 7.9 %collective-permute-start.5 = (bf16[128,768]{1,0:T(8,128)(2,1)S(1)}, bf16[128,768]{1,0:T(8,128)(2,1)S(1)}, u32[]{:S(2)}, u32[]{:S(2)}) collective-permute-start(bf16[128,768]{1,0:T(8,128)(2,1)S(1)} %get-tuple-element.41), channel_id=1, source_target_pairs={{0,12},{4,0},{8,4},{12,8},{1,13},{5,1},{9,5},{13,9},{2,14},{6,2},{... | collective-permute-start | bytes 589832 | tf_op jit(solution)/shard_map/ppermute | solution.py:197
  51.3 9.3 %collective-permute-start.6 = (bf16[128,768]{1,0:T(8,128)(2,1)S(1)}, bf16[128,768]{1,0:T(8,128)(2,1)S(1)}, u32[]{:S(2)}, u32[]{:S(2)}) collective-permute-start(bf16[128,768]{1,0:T(8,128)(2,1)S(1)} %get-tuple-element.42), channel_id=1, source_target_pairs={{0,8},{4,12},{8,0},{12,4},{1,9},{5,13},{9,1},{13,5},{2,10},{6,14},... | collective-permute-start | bytes 589832 | tf_op jit(solution)/shard_map/ppermute | solution.py:197
  52.6 11.0 %collective-permute-start.7 = (bf16[128,768]{1,0:T(8,128)(2,1)S(1)}, bf16[128,768]{1,0:T(8,128)(2,1)S(1)}, u32[]{:S(2)}, u32[]{:S(2)}) collective-permute-start(bf16[128,768]{1,0:T(8,128)(2,1)S(1)} %get-tuple-element.43), channel_id=1, source_target_pairs={{0,4},{4,8},{8,12},{12,0},{1,5},{5,9},{9,13},{13,1},{2,6},{6,10},{... | collective-permute-start | bytes 589832 | tf_op jit(solution)/shard_map/ppermute | solution.py:197
  63.6 41.9 %copy-start.6 = (f32[64,2048]{1,0:T(8,128)S(1)}, f32[64,2048]{1,0:T(8,128)}, u32[]{:S(2)}) copy-start(f32[64,2048]{1,0:T(8,128)} %copy-done.5) | copy-start | bytes 1572868
  64.3 12.3 %collective-permute-start.10 = (bf16[128,768]{1,0:T(8,128)(2,1)S(1)}, bf16[128,768]{1,0:T(8,128)(2,1)S(1)}, u32[]{:S(2)}, u32[]{:S(2)}) collective-permute-start(bf16[128,768]{1,0:T(8,128)(2,1)S(1)} %shard_map.48.refs_0_), channel_id=1, source_target_pairs={{0,4},{4,8},{8,12},{12,0},{1,5},{5,9},{9,13},{13,1},{2,6},{6,10},{... | collective-permute-start | bytes 589832 | tf_op jit(solution)/shard_map/ppermute | solution.py:197
  64.3 12.2 %collective-permute-start.8 = (bf16[128,768]{1,0:T(8,128)(2,1)S(1)}, bf16[128,768]{1,0:T(8,128)(2,1)S(1)}, u32[]{:S(2)}, u32[]{:S(2)}) collective-permute-start(bf16[128,768]{1,0:T(8,128)(2,1)S(1)} %shard_map.48.refs_0_), channel_id=1, source_target_pairs={{0,12},{4,0},{8,4},{12,8},{1,13},{5,1},{9,5},{13,9},{2,14},{6,2},{... | collective-permute-start | bytes 589832 | tf_op jit(solution)/shard_map/ppermute | solution.py:197
  67.6 9.0 %collective-permute-start.9 = (bf16[128,768]{1,0:T(8,128)(2,1)S(1)}, bf16[128,768]{1,0:T(8,128)(2,1)S(1)}, u32[]{:S(2)}, u32[]{:S(2)}) collective-permute-start(bf16[128,768]{1,0:T(8,128)(2,1)S(1)} %shard_map.48.refs_0_), channel_id=1, source_target_pairs={{0,8},{4,12},{8,0},{12,4},{1,9},{5,13},{9,1},{13,5},{2,10},{6,14},... | collective-permute-start | bytes 589832 | tf_op jit(solution)/shard_map/ppermute | solution.py:197
  76.6 3.4 %copy-start = (bf16[2048,2048]{1,0:T(8,128)(2,1)S(1)}, bf16[2048,2048]{1,0:T(8,128)(2,1)}, u32[]{:S(2)}) copy-start(bf16[2048,2048]{1,0:T(8,128)(2,1)} %all-gather.2.cloned.1.call-done.gathered_ref.refs_0_) | copy-start | bytes 25165828
  80.0 1.6 %copy-start.4 = (bf16[512,2048]{1,0:T(8,128)(2,1)S(1)}, bf16[512,2048]{1,0:T(8,128)(2,1)}, u32[]{:S(2)}) copy-start(bf16[512,2048]{1,0:T(8,128)(2,1)} %copy-done.3) | copy-start | bytes 6291460
  81.6 1.0 copy-start.8
  86.1 10.7 %collective-permute-start.20 = (bf16[64,1280]{1,0:T(8,128)(2,1)S(1)}, bf16[64,1280]{1,0:T(8,128)(2,1)S(1)}, u32[]{:S(2)}, u32[]{:S(2)}) collective-permute-start(bf16[64,1280]{1,0:T(8,128)(2,1)S(1)} %get-tuple-element.58), channel_id=1, source_target_pairs={{0,12},{4,0},{8,4},{12,8},{1,13},{5,1},{9,5},{13,9},{2,14},{6,2},{... | collective-permute-start | bytes 491528 | tf_op jit(solution)/shard_map/ppermute | solution.py:197
  89.1 8.7 %collective-permute-start.21 = (bf16[64,1280]{1,0:T(8,128)(2,1)S(1)}, bf16[64,1280]{1,0:T(8,128)(2,1)S(1)}, u32[]{:S(2)}, u32[]{:S(2)}) collective-permute-start(bf16[64,1280]{1,0:T(8,128)(2,1)S(1)} %get-tuple-element.59), channel_id=1, source_target_pairs={{0,8},{4,12},{8,0},{12,4},{1,9},{5,13},{9,1},{13,5},{2,10},{6,14},... | collective-permute-start | bytes 491528 | tf_op jit(solution)/shard_map/ppermute | solution.py:197
  89.1 11.9 %collective-permute-start.22 = (bf16[64,1280]{1,0:T(8,128)(2,1)S(1)}, bf16[64,1280]{1,0:T(8,128)(2,1)S(1)}, u32[]{:S(2)}, u32[]{:S(2)}) collective-permute-start(bf16[64,1280]{1,0:T(8,128)(2,1)S(1)} %get-tuple-element.60), channel_id=1, source_target_pairs={{0,4},{4,8},{8,12},{12,0},{1,5},{5,9},{9,13},{13,1},{2,6},{6,10},{... | collective-permute-start | bytes 491528 | tf_op jit(solution)/shard_map/ppermute | solution.py:197
  90.1 14.1 %collective-permute-start.11 = (bf16[64,1280]{1,0:T(8,128)(2,1)S(1)}, bf16[64,1280]{1,0:T(8,128)(2,1)S(1)}, u32[]{:S(2)}, u32[]{:S(2)}) collective-permute-start(bf16[64,1280]{1,0:T(8,128)(2,1)S(1)} %get-tuple-element.50), channel_id=1, source_target_pairs={{0,12},{4,0},{8,4},{12,8},{1,13},{5,1},{9,5},{13,9},{2,14},{6,2},{... | collective-permute-start | bytes 491528 | tf_op jit(solution)/shard_map/ppermute | solution.py:197
  92.3 14.4 %collective-permute-start.12 = (bf16[64,1280]{1,0:T(8,128)(2,1)S(1)}, bf16[64,1280]{1,0:T(8,128)(2,1)S(1)}, u32[]{:S(2)}, u32[]{:S(2)}) collective-permute-start(bf16[64,1280]{1,0:T(8,128)(2,1)S(1)} %get-tuple-element.51), channel_id=1, source_target_pairs={{0,8},{4,12},{8,0},{12,4},{1,9},{5,13},{9,1},{13,5},{2,10},{6,14},... | collective-permute-start | bytes 491528 | tf_op jit(solution)/shard_map/ppermute | solution.py:197
  96.8 11.7 %collective-permute-start.13 = (bf16[64,1280]{1,0:T(8,128)(2,1)S(1)}, bf16[64,1280]{1,0:T(8,128)(2,1)S(1)}, u32[]{:S(2)}, u32[]{:S(2)}) collective-permute-start(bf16[64,1280]{1,0:T(8,128)(2,1)S(1)} %get-tuple-element.52), channel_id=1, source_target_pairs={{0,4},{4,8},{8,12},{12,0},{1,5},{5,9},{9,13},{13,1},{2,6},{6,10},{... | collective-permute-start | bytes 491528 | tf_op jit(solution)/shard_map/ppermute | solution.py:197
  101.6 8.8 %collective-permute-start.23 = (bf16[64,1280]{1,0:T(8,128)(2,1)S(1)}, bf16[64,1280]{1,0:T(8,128)(2,1)S(1)}, u32[]{:S(2)}, u32[]{:S(2)}) collective-permute-start(bf16[64,1280]{1,0:T(8,128)(2,1)S(1)} %shard_map.53.refs_4_), channel_id=1, source_target_pairs={{0,12},{4,0},{8,4},{12,8},{1,13},{5,1},{9,5},{13,9},{2,14},{6,2},{... | collective-permute-start | bytes 491528 | tf_op jit(solution)/shard_map/ppermute | solution.py:197
  102.5 9.2 %collective-permute-start.24 = (bf16[64,1280]{1,0:T(8,128)(2,1)S(1)}, bf16[64,1280]{1,0:T(8,128)(2,1)S(1)}, u32[]{:S(2)}, u32[]{:S(2)}) collective-permute-start(bf16[64,1280]{1,0:T(8,128)(2,1)S(1)} %shard_map.53.refs_4_), channel_id=1, source_target_pairs={{0,8},{4,12},{8,0},{12,4},{1,9},{5,13},{9,1},{13,5},{2,10},{6,14},... | collective-permute-start | bytes 491528 | tf_op jit(solution)/shard_map/ppermute | solution.py:197
  104.2 11.9 %collective-permute-start.25 = (bf16[64,1280]{1,0:T(8,128)(2,1)S(1)}, bf16[64,1280]{1,0:T(8,128)(2,1)S(1)}, u32[]{:S(2)}, u32[]{:S(2)}) collective-permute-start(bf16[64,1280]{1,0:T(8,128)(2,1)S(1)} %shard_map.53.refs_4_), channel_id=1, source_target_pairs={{0,4},{4,8},{8,12},{12,0},{1,5},{5,9},{9,13},{13,1},{2,6},{6,10},{... | collective-permute-start | bytes 491528 | tf_op jit(solution)/shard_map/ppermute | solution.py:197
  109.2 13.8 %collective-permute-start.14 = (bf16[64,1280]{1,0:T(8,128)(2,1)S(1)}, bf16[64,1280]{1,0:T(8,128)(2,1)S(1)}, u32[]{:S(2)}, u32[]{:S(2)}) collective-permute-start(bf16[64,1280]{1,0:T(8,128)(2,1)S(1)} %shard_map.51.refs_4_), channel_id=1, source_target_pairs={{0,12},{4,0},{8,4},{12,8},{1,13},{5,1},{9,5},{13,9},{2,14},{6,2},{... | collective-permute-start | bytes 491528 | tf_op jit(solution)/shard_map/ppermute | solution.py:197
  109.4 14.4 %collective-permute-start.15 = (bf16[64,1280]{1,0:T(8,128)(2,1)S(1)}, bf16[64,1280]{1,0:T(8,128)(2,1)S(1)}, u32[]{:S(2)}, u32[]{:S(2)}) collective-permute-start(bf16[64,1280]{1,0:T(8,128)(2,1)S(1)} %shard_map.51.refs_4_), channel_id=1, source_target_pairs={{0,8},{4,12},{8,0},{12,4},{1,9},{5,13},{9,1},{13,5},{2,10},{6,14},... | collective-permute-start | bytes 491528 | tf_op jit(solution)/shard_map/ppermute | solution.py:197
  110.4 13.4 %collective-permute-start.16 = (bf16[64,1280]{1,0:T(8,128)(2,1)S(1)}, bf16[64,1280]{1,0:T(8,128)(2,1)S(1)}, u32[]{:S(2)}, u32[]{:S(2)}) collective-permute-start(bf16[64,1280]{1,0:T(8,128)(2,1)S(1)} %shard_map.51.refs_4_), channel_id=1, source_target_pairs={{0,4},{4,8},{8,12},{12,0},{1,5},{5,9},{9,13},{13,1},{2,6},{6,10},{... | collective-permute-start | bytes 491528 | tf_op jit(solution)/shard_map/ppermute | solution.py:197
  119.3 11.8 %collective-permute-start.26 = (bf16[256,512]{1,0:T(8,128)(2,1)S(1)}, bf16[256,512]{1,0:T(8,128)(2,1)S(1)}, u32[]{:S(2)}, u32[]{:S(2)}) collective-permute-start(bf16[256,512]{1,0:T(8,128)(2,1)S(1)} %get-tuple-element.62), channel_id=1, source_target_pairs={{0,3},{1,0},{2,1},{3,2},{4,7},{5,4},{6,5},{7,6},{8,11},{9,8},{10,9... | collective-permute-start | bytes 786440 | tf_op jit(solution)/shard_map/ppermute | solution.py:197
  122.2 10.1 %collective-permute-start.27 = (bf16[256,512]{1,0:T(8,128)(2,1)S(1)}, bf16[256,512]{1,0:T(8,128)(2,1)S(1)}, u32[]{:S(2)}, u32[]{:S(2)}) collective-permute-start(bf16[256,512]{1,0:T(8,128)(2,1)S(1)} %get-tuple-element.63), channel_id=1, source_target_pairs={{0,2},{1,3},{2,0},{3,1},{4,6},{5,7},{6,4},{7,5},{8,10},{9,11},{10,... | collective-permute-start | bytes 786440 | tf_op jit(solution)/shard_map/ppermute | solution.py:197
  123.0 16.5 %collective-permute-start.28 = (bf16[256,512]{1,0:T(8,128)(2,1)S(1)}, bf16[256,512]{1,0:T(8,128)(2,1)S(1)}, u32[]{:S(2)}, u32[]{:S(2)}) collective-permute-start(bf16[256,512]{1,0:T(8,128)(2,1)S(1)} %get-tuple-element.64), channel_id=1, source_target_pairs={{0,1},{1,2},{2,3},{3,0},{4,5},{5,6},{6,7},{7,4},{8,9},{9,10},{10,1... | collective-permute-start | bytes 786440 | tf_op jit(solution)/shard_map/ppermute | solution.py:197
  127.1 13.6 %collective-permute-start.17 = (bf16[256,512]{1,0:T(8,128)(2,1)S(1)}, bf16[256,512]{1,0:T(8,128)(2,1)S(1)}, u32[]{:S(2)}, u32[]{:S(2)}) collective-permute-start(bf16[256,512]{1,0:T(8,128)(2,1)S(1)} %get-tuple-element.54), channel_id=1, source_target_pairs={{0,3},{1,0},{2,1},{3,2},{4,7},{5,4},{6,5},{7,6},{8,11},{9,8},{10,9... | collective-permute-start | bytes 786440 | tf_op jit(solution)/shard_map/ppermute | solution.py:197
  129.6 12.2 %collective-permute-start.18 = (bf16[256,512]{1,0:T(8,128)(2,1)S(1)}, bf16[256,512]{1,0:T(8,128)(2,1)S(1)}, u32[]{:S(2)}, u32[]{:S(2)}) collective-permute-start(bf16[256,512]{1,0:T(8,128)(2,1)S(1)} %get-tuple-element.55), channel_id=1, source_target_pairs={{0,2},{1,3},{2,0},{3,1},{4,6},{5,7},{6,4},{7,5},{8,10},{9,11},{10,... | collective-permute-start | bytes 786440 | tf_op jit(solution)/shard_map/ppermute | solution.py:197
  131.1 13.3 %collective-permute-start.19 = (bf16[256,512]{1,0:T(8,128)(2,1)S(1)}, bf16[256,512]{1,0:T(8,128)(2,1)S(1)}, u32[]{:S(2)}, u32[]{:S(2)}) collective-permute-start(bf16[256,512]{1,0:T(8,128)(2,1)S(1)} %get-tuple-element.56), channel_id=1, source_target_pairs={{0,1},{1,2},{2,3},{3,0},{4,5},{5,6},{6,7},{7,4},{8,9},{9,10},{10,1... | collective-permute-start | bytes 786440 | tf_op jit(solution)/shard_map/ppermute | solution.py:197
Sparse Core Ops, SparseCore 0:
  9.2 62.2 all-gather.1

commit v2 on v1

--- a/solution.py
+++ b/solution.py
@@ -20,7 +20,7 @@
 HALVES = 2
 
 
-def call(kernel, out_shape, n_in, scratch=(), flops=0, byts=0, mib=24, aliases={}):
+def call(kernel, out_shape, n_in, scratch=(), flops=0, byts=0, mib=20, aliases={}):
     return pl.pallas_call(
         kernel,
         out_shape=out_shape,
@@ -94,44 +94,41 @@
     mc_ref[...] = -2.0 * dot(dot(roll, cube_ref[...].astype(BF)).astype(BF), wide)
 
 
+def loop(count, step):
+    lax.fori_loop(0, count, lambda n, _: step(n), None)
+
+
+def block_of(n, size):
+    return pl.ds(pl.multiple_of(n * size, size), size)
+
+
 def load_pieces(piece_refs, mask_ref, block_row, out_ref):
     done = 0
     for ref in piece_refs:
-        for block in range(ref.shape[0] // BLK):
-            row = block_row + done // BLK
-            keep = jnp.broadcast_to(mask_ref[pl.ds(row, 1), :], (BLK, 2048)).astype(BF)
-            out_ref[pl.ds(done, BLK), :] = ref[pl.ds(BLK * block, BLK), :] * keep
-            done += BLK
-
-
-def load_slots(slots, where, gathered_ref, mask_ref, out_ref):
-    z, core = where
-    for n, slot in enumerate(slots):
-        chip = lax.rem(z + SLOTS[slot] + 8, 8)
-        for other in range(2):
-            start = pl.multiple_of(128 * (2 * chip + lax.rem(core + other, 2)), 128)
-            for block in range(4):
-                row = 8 * slot + 4 * other + block
-                keep = jnp.broadcast_to(mask_ref[pl.ds(row, 1), :], (BLK, 2048)).astype(BF)
-                out_ref[pl.ds(256 * n + 128 * other + BLK * block, BLK), :] = (
-                    gathered_ref[pl.ds(start + BLK * block, BLK), :] * keep
-                )
+
+        def step(n, ref=ref, done=done):
+            keep = mask_ref[pl.ds(block_row + done + n, 1), :]
+            keep = jnp.broadcast_to(keep, (BLK, 2048)).astype(BF)
+            out_ref[block_of(done + n, BLK), :] = ref[block_of(n, BLK), :] * keep
+
+        loop(ref.shape[0] // BLK, step)
+        done += ref.shape[0] // BLK
 
 
 def product_one_kernel(slots, halves, n_pieces, s_ref, left_ref, mt_ref, *refs):
     pieces, outs, right = refs[:n_pieces], refs[n_pieces:-1], refs[-1]
-    if n_pieces > 1:
-        load_pieces(pieces, mt_ref, 8 * slots[0], right)
-    else:
-        load_slots(slots, (s_ref[0], s_ref[1]), pieces[0], mt_ref, right)
+    load_pieces(pieces, mt_ref, 8 * slots[0], right)
     height = 128 // halves
-    for start in range(0, right.shape[0], 256):
-        block = dot(left_ref[...], right[pl.ds(start, 256), :], NT)
+
+    def step(n):
+        block = dot(left_ref[...], right[block_of(n, 256), :], NT)
         for half in range(halves):
             for quarter in range(4):
                 row = 128 * quarter + height * half
                 out = outs[4 * half + quarter]
-                out[:, pl.ds(start, 256)] = block[row : row + height].astype(out.dtype)
+                out[:, block_of(n, 256)] = block[row : row + height].astype(out.dtype)
+
+    loop(right.shape[0] // 256, step)
 
 
 def square_kernel(first_slot, first_block, s_ref, ms_ref, own_ref, a_ref, b_ref, c_ref, out_ref):
@@ -143,8 +140,8 @@
         out_ref[rows, :] = (total[rows] * keep).astype(BF)
 
 
-def right_kernel(s_ref, mk_ref, gathered_ref, out_ref):
-    load_slots(range(len(SLOTS)), (s_ref[0], s_ref[1]), gathered_ref, mk_ref, out_ref)
+def right_kernel(s_ref, mk_ref, *refs):
+    load_pieces(refs[:-1], mk_ref, 0, refs[-1])
 
 
 def product_two_kernel(half, n_early, s_ref, mc_ref, right_ref, *refs):
@@ -158,22 +155,26 @@
         if n_early:
             square[rows, pl.ds(0, skip)] = early[quarter][pl.ds(height * half, height), :]
         square[rows, pl.ds(skip, 2048 - skip)] = late[quarter][...]
-    for cols in range(0, 2048, 256):
-        block = dot(square[...], right_ref[:, pl.ds(cols, 256)])
+
+    def step(tile):
+        block = dot(square[...], right_ref[:, block_of(tile, 256)])
         for n in range(4 * height // BLK):
             row = 4 * (n // (height // BLK)) + height // BLK * half + n % (height // BLK)
             rows = slice(BLK * n, BLK * n + BLK)
-            total[rows, pl.ds(cols, 256)] = block[rows] * mc_ref[pl.ds(row, 1), pl.ds(cols, 256)]
-    for slot in range(len(SLOTS)):
-        chip = lax.rem(z + SLOTS[slot] + 8, 8)
-
-        @pl.when(chip // 2 == col)
+            total[rows, block_of(tile, 256)] = block[rows] * mc_ref[pl.ds(row, 1), block_of(tile, 256)]
+
+    loop(8, step)
+
+    def add(n):
+        block_row = row_of_slot(4 * n, z, core, layer)
+        band = block_row // 16 - 4 * col
+
+        @pl.when((band >= 0) & (band < 4))
         def _():
-            for other in range(2):
-                band = 2 * chip + lax.rem(core + other, 2) - 4 * col
-                cols = pl.ds(pl.multiple_of(512 * band + 128 * layer, 128), 128)
-                total[:, cols] += 3.0 * square[:, pl.ds(256 * slot + 128 * other, 128)].astype(F32)
-
+            cols = pl.ds(pl.multiple_of(512 * band + 128 * layer, 128), 128)
+            total[:, cols] += 3.0 * square[:, block_of(n, 128)].astype(F32)
+
+    loop(16, add)
     for share in range(4):
         cols = pl.ds(pl.multiple_of(512 * lax.rem(layer + share, 4), 512), 512)
         outs[share][...] = total[:, cols].astype(outs[share].dtype)
@@ -206,21 +207,24 @@
     return got[2], got[1], got[0]
 
 
-def gather_patterns(pattern_density, pattern_square):
-    both = jnp.concatenate([pattern_density, pattern_square], 1).astype(BF)
-    return lax.all_to_all(jnp.broadcast_to(both, (64, 16, 128)), ("row", "col"), 0, 0)
-
-
 def body(density, pattern_density, pattern_square, pattern_cube):
     row, col, layer = lax.axis_index("row"), lax.axis_index("col"), lax.axis_index("rep")
     where = jnp.stack([row // 2, row % 2, col, layer]).astype(jnp.int32)
     own = lax.dynamic_slice_in_dim(density, 128 * layer, 128, 0)
 
-    gathered = lax.all_gather(own, "row", axis=0, tiled=True)
-    near = [own, shift(own, "row", 2, 16), shift(own, "row", -2, 16)][:EARLY]
-    early = [piece for one in near for piece in (one, swap(one))]
-
-    both = gather_patterns(pattern_density, pattern_square)
+    both = jnp.concatenate([pattern_density, pattern_square], 1).astype(BF)
+    own, both = lax.optimization_barrier((own, jnp.broadcast_to(both, (64, 16, 128))))
+    both = lax.all_to_all(both, ("row", "col"), 0, 0)
+
+    def both_ways(up, down):
+        return shift(up, "row", 2, 16), shift(down, "row", -2, 16)
+
+    def with_swapped(held):
+        return [*held, *(swap(piece) for piece in held)]
+
+    first = both_ways(own, own)
+    *first, both = lax.optimization_barrier((*first, both))
+    second = both_ways(*first)
     left, mk, mt, ms, mc = call(
         prep_kernel,
         (
@@ -235,9 +239,9 @@
         byts=6 << 20,
     )(where, both, pattern_density, pattern_cube, density)
 
-    def start(slots, halves, held):
+    def multiply(slots, halves, held):
         height, width = 128 // halves, 256 * len(slots)
-        parts = call(
+        return call(
             functools.partial(product_one_kernel, slots, halves, len(held)),
             ((shape(height, width, dtype=F32),) + (shape(height, width),) * 3) * halves,
             3 + len(held),
@@ -245,33 +249,49 @@
             flops=2 * 512 * 2048 * width,
             byts=2 * 2048 * (512 + width),
         )(where, left, mt, *held)
-        squares = []
-        for half in range(halves):
-            mine, *others = parts[4 * half : 4 * half + 4]
-            mine = call(
-                functools.partial(square_kernel, slots[0], half * (4 // halves)),
-                shape(height, width),
-                6,
-                byts=2 * height * width * 6,
-            )(where, ms, mine, *exchange(others, "col"))
-            squares.append((mine, *exchange([mine] * 3, "col")))
-        return squares
-
-    first = start(range(EARLY), 1, early)[0] if EARLY else ()
-    first, gathered = lax.optimization_barrier((first, gathered))
-    squares = start(range(EARLY, len(SLOTS)), HALVES, [gathered])
-    right = call(right_kernel, shape(2048, 2048), 3, byts=16 << 20)(where, mk, gathered)
+
+    def finish_square(slots, halves, half, mine, got):
+        height, width = 128 // halves, 256 * len(slots)
+        mine = call(
+            functools.partial(square_kernel, slots[0], half * (4 // halves)),
+            shape(height, width),
+            6,
+            byts=2 * height * width * 6,
+        )(where, ms, mine, *got)
+        return mine, *exchange([mine] * 3, "col")
+
+    early = [piece for held in ([own], first[:1], first[1:]) for piece in with_swapped(held)]
+    parts = multiply(range(EARLY), 1, early)
+    *second, parts = lax.optimization_barrier((*second, parts))
+    third = both_ways(*second)
+    third, ends, got, second = lax.optimization_barrier(
+        (third, (third[0][:64], third[1][64:]), exchange(parts[1:], "col"), second)
+    )
+    fourth = both_ways(*ends)
+    late = [with_swapped(held) for held in (second[:1], second[1:])]
+    late, got = lax.optimization_barrier((late, got))
+    early_square = finish_square(range(EARLY), 1, 0, parts[0], got)
+    fourth, early_square = lax.optimization_barrier((fourth, early_square))
+    late += [with_swapped(held) for held in (third[:1], third[1:], fourth)]
+    late = [piece for held in late for piece in held]
+    slots = range(EARLY, len(SLOTS))
+    parts = multiply(slots, HALVES, late)
+    parts = [parts[4 * half : 4 * half + 4] for half in range(HALVES)]
+    squares = [
+        finish_square(slots, HALVES, half, mine, exchange(others, "col")) for half, (mine, *others) in enumerate(parts)
+    ]
+    right = call(right_kernel, shape(2048, 2048), 2 + len(early + late), byts=16 << 20)(where, mk, *early, *late)
     results = []
     for half in range(HALVES):
         height = 512 // HALVES
         mine, *others = call(
-            functools.partial(product_two_kernel, half, len(first)),
+            functools.partial(product_two_kernel, half, len(early_square)),
             (shape(height, 512, dtype=F32),) + (shape(height, 512),) * 3,
-            3 + len(first) + 4,
+            3 + len(early_square) + 4,
             [pltpu.VMEM((height, 2048), BF), pltpu.VMEM((height, 2048), F32)],
             flops=2 * height * 2048 * 2048,
             byts=10 << 20,
-        )(where, mc, right, *first, *squares[half])
+        )(where, mc, right, *early_square, *squares[half])
         results += [mine, *exchange(others, "rep")]
     return call(finish_kernel, shape(512, 512), 1 + len(results), byts=3 << 20)(where, *results)
 

time: 153 us -> 156 us (1.020); the launches traced: 153 us -> 153 us
  between operations: 13.6 us -> 0.18 us
  starting transfers between devices: 45.9 us -> 54.1 us
  Pallas kernels: 22.4 us -> 28.8 us
  local copies, waits for them, and re-layouts: 9.6 us -> 4.84 us
  waiting for transfers between devices: 59.8 us -> 63.1 us
    ppermute x26 -> x32, starting transfers between devices: 32.2 us -> 38.7 us  [shift(): lax.ppermute(array, axis, [(i, (i + step) % size) for i in range(size)])]
    pallas_call x8, Pallas kernels: 17.7 us -> 24.1 us  [the longest x2 10.7 us: body(): call(functools.partial(product_two_kernel, half, len(early_square)), (sha...]
    unnamed x22 -> x6, local copies, waits for them, and re-layouts: 6.83 us -> 2.98 us
    ppermute x26 -> x32, waiting for transfers between devices: 45.1 us -> 48.8 us  [shift(): lax.ppermute(array, axis, [(i, (i + step) % size) for i in range(size)])]
    all_to_all x1, waiting for transfers between devices: 14.6 us -> 12.9 us  [body(): both = lax.all_to_all(both, ('row', 'col'), 0, 0)]
    ppermute x3 -> x9, starting transfers between devices: 0.75 us -> 2.36 us  [swap(): return lax.ppermute(array, 'row', [(i, i ^ 1) for i in range(16)])]
  transfers between devices with their start and end apart: 31 -> 42, of which waited for: 15 -> 18; matrix products, arithmetic and copies ran while one was open for 2% -> 0% of each run, Pallas kernels for 11% -> 14%
where the time goes in v2:
time: 156 us; the launch traced here: 153 us
  waiting for transfers between devices  63.1 us (40%)
  starting transfers between devices  54.1 us (35%)
  Pallas kernels  28.8 us (18%)
  local copies, waits for them, and re-layouts  4.84 us (3%)
    ppermute x32, waiting for transfers between devices, shift(): lax.ppermute(array, axis, [(i, (i + step) % size) for i in range(size)])  48.8 us
    ppermute x32, starting transfers between devices, shift(): lax.ppermute(array, axis, [(i, (i + step) % size) for i in range(size)])  38.7 us
    all_to_all x1, starting transfers between devices, body(): both = lax.all_to_all(both, ('row', 'col'), 0, 0)  13 us
    all_to_all x1, waiting for transfers between devices, body(): both = lax.all_to_all(both, ('row', 'col'), 0, 0)  12.9 us
    pallas_call x2, Pallas kernels, body(): call(functools.partial(product_two_kernel, half, len(early_square)), (sha...  10.7 us
    pallas_call x2, Pallas kernels, multiply(): call(functools.partial(product_one_kernel, slots, halves, len(held)), ((s...  9.06 us
  transfers between devices with their start and end apart: 42, of which 18 were waited for; matrix products, arithmetic and copies ran while one was open for 0% of the time, Pallas kernels for 14%

profile of v2, /device:TPU:32, one launch (start us, length us, event | category | flops | bytes accessed | tf_op | source)
XLA Modules:
  0.0 152.5 jit_solution(10906115175481567853)
XLA Ops:
  0.0 0.7 convert.6
  0.7 0.7 convert.7
  1.4 1.1 constant_dynamic-slice_fusion.refs_0_
  2.6 0.7 broadcast_in_dim.3
  3.3 1.9 %collective-permute-start = (bf16[128,2048]{1,0:T(8,128)(2,1)S(1)}, bf16[128,2048]{1,0:T(8,128)(2,1)S(1)}, u32[]{:S(2)}, u32[]{:S(2)}) collective-permute-start(bf16[128,2048]{1,0:T(8,128)(2,1)S(1)} %constant_dynamic-slice_fusion.refs_0_), channel_id=1, source_target_pairs={{0,32},{16,48},{32,64},{48,80},{64,96},{80,112},{96,128},{112,144}... | collective-permute-start | bytes 1572872 | tf_op jit(solution)/shard_map/ppermute | solution.py:198
  5.3 13.0 %all-to-all-start = ((bf16[64,16,128]{2,1,0:T(8,128)(2,1)}), bf16[64,16,128]{2,1,0:T(8,128)(2,1)S(1)}, u32[]{:S(2)}, u32[]{:S(2)}) async-start(bf16[64,16,128]{2,1,0:T(8,128)(2,1)} %broadcast_in_dim.3), calls=%async_computation | async-start | bytes 524288 | tf_op jit(solution)/shard_map/all_to_all | solution.py:217
  18.5 12.9 %all-to-all-done.refs_0_ = bf16[64,16,128]{2,1,0:T(8,128)(2,1)S(1)} async-done(((bf16[64,16,128]{2,1,0:T(8,128)(2,1)}), bf16[64,16,128]{2,1,0:T(8,128)(2,1)S(1)}, u32[]{:S(2)}, u32[]{:S(2)}) %all-to-all-start) | async-done | bytes 262176 | tf_op jit(solution)/shard_map/all_to_all | solution.py:217
  32.1 1.9 %collective-permute-start.6 = (bf16[128,2048]{1,0:T(8,128)(2,1)S(1)}, bf16[128,2048]{1,0:T(8,128)(2,1)}, u32[]{:S(2)}, u32[]{:S(2)}) collective-permute-start(bf16[128,2048]{1,0:T(8,128)(2,1)S(1)} %collective-permute-done.1.refs_4_), channel_id=1, source_target_pairs={{0,224},{16,240},{32,0},{48,16},{64,32},{80,48},{96,64},{112,80},{... | collective-permute-start | bytes 1572872 | tf_op jit(solution)/shard_map/ppermute | solution.py:198
  34.1 1.6 %copy-done = bf16[512,2048]{1,0:T(8,128)(2,1)S(1)} copy-done((bf16[512,2048]{1,0:T(8,128)(2,1)S(1)}, bf16[512,2048]{1,0:T(8,128)(2,1)}, u32[]{:S(2)}) %copy-start) | copy-done | bytes 2097176
  35.7 0.7 copy-done.1
  36.4 0.7 copy-done.2
  37.1 3.1 %shard_map.46 = (bf16[512,2048]{1,0:T(8,128)(2,1)S(1)}, f32[64,2048]{1,0:T(8,128)S(1)}, f32[64,2048]{1,0:T(8,128)S(1)}, f32[16,2048]{1,0:T(8,128)S(1)}, f32[16,2048]{1,0:T(8,128)S(1)}) custom-call(s32[4]{0:T(128)S(1)} %pad_add_fusion.s_ref, bf16[64,16,128]{2,1,0:T(8,128)(2,1)S(1)} %all-to-all-done.refs_0_, s32[16,64]{1,0:T(8,128)S(1)} %copy-done.1, ...), custom_call_target="tpu_custom_call" | custom-call | flops 209715200 | bytes 6291456 | tf_op jit(solution)/shard_map/pallas_call | solution.py:228
  40.2 3.3 %shard_map.47 = (f32[128,768]{1,0:T(8,128)S(1)}, bf16[128,768]{1,0:T(8,128)(2,1)S(1)}, bf16[128,768]{1,0:T(8,128)(2,1)S(1)}, bf16[128,768]{1,0:T(8,128)(2,1)S(1)}) custom-call(s32[4]{0:T(128)S(1)} %pad_add_fusion.s_ref, bf16[512,2048]{1,0:T(8,128)(2,1)S(1)} %get-tuple-element.70.left_ref, f32[64,2048]{1,0:T(8,128)S(1)} %get-tuple-element.71.mt_ref, ...), custom_call_target="tpu_custom_call" | custom-call | flops 1610612736 | bytes 5242880 | tf_op jit(solution)/shard_map/pallas_call | solution.py:244
  43.4 2.6 %collective-permute-done.5.refs_6_.refs_0_ = bf16[128,2048]{1,0:T(8,128)(2,1)} collective-permute-done((bf16[128,2048]{1,0:T(8,128)(2,1)S(1)}, bf16[128,2048]{1,0:T(8,128)(2,1)}, u32[]{:S(2)}, u32[]{:S(2)}) %collective-permute-start.5) | collective-permute-done | bytes 524320 | tf_op jit(solution)/shard_map/ppermute | solution.py:198
  46.0 0.9 collective-permute-start.7
  46.9 1.4 collective-permute-start.8
  48.4 1.3 collective-permute-start.10
  49.7 0.5 collective-permute-start.11
  50.2 2.7 %collective-permute-start.9 = (bf16[128,768]{1,0:T(8,128)(2,1)S(1)}, bf16[128,768]{1,0:T(8,128)(2,1)S(1)}, u32[]{:S(2)}, u32[]{:S(2)}) collective-permute-start(bf16[128,768]{1,0:T(8,128)(2,1)S(1)} %get-tuple-element.78), channel_id=1, source_target_pairs={{0,12},{4,0},{8,4},{12,8},{1,13},{5,1},{9,5},{13,9},{2,14},{6,2},{... | collective-permute-start | bytes 589832 | tf_op jit(solution)/shard_map/ppermute | solution.py:198
  52.9 7.0 %collective-permute-done.7.refs_10_.refs_4_ = bf16[128,2048]{1,0:T(8,128)(2,1)S(1)} collective-permute-done((bf16[128,2048]{1,0:T(8,128)(2,1)}, bf16[128,2048]{1,0:T(8,128)(2,1)S(1)}, u32[]{:S(2)}, u32[]{:S(2)}) %collective-permute-start.7) | collective-permute-done | bytes 524320 | tf_op jit(solution)/shard_map/ppermute | solution.py:198
  60.2 0.5 collective-permute-start.13
  60.7 1.5 collective-permute-start.16
  62.2 1.4 collective-permute-start.17
  63.6 0.5 collective-permute-start.15
  64.1 0.6 shard_map.48.refs_0_
  64.7 1.1 collective-permute-start.18
  65.9 4.4 %collective-permute-done.16.refs_14_.refs_8_ = bf16[64,2048]{1,0:T(8,128)(2,1)S(1)} collective-permute-done((bf16[64,2048]{1,0:T(8,128)(2,1)S(1)}, bf16[64,2048]{1,0:T(8,128)(2,1)S(1)}, u32[]{:S(2)}, u32[]{:S(2)}) %collective-permute-start.16) | collective-permute-done | bytes 262176 | tf_op jit(solution)/shard_map/ppermute | solution.py:198
  70.3 1.3 collective-permute-start.19
  72.0 7.7 %collective-permute-done.19.refs_2_ = bf16[128,768]{1,0:T(8,128)(2,1)S(1)} collective-permute-done((bf16[128,768]{1,0:T(8,128)(2,1)S(1)}, bf16[128,768]{1,0:T(8,128)(2,1)S(1)}, u32[]{:S(2)}, u32[]{:S(2)}) %collective-permute-start.19) | collective-permute-done | bytes 196640 | tf_op jit(solution)/shard_map/ppermute | solution.py:198
  79.7 3.0 %collective-permute-done.20.refs_3_ = bf16[128,768]{1,0:T(8,128)(2,1)S(1)} collective-permute-done((bf16[128,768]{1,0:T(8,128)(2,1)S(1)}, bf16[128,768]{1,0:T(8,128)(2,1)S(1)}, u32[]{:S(2)}, u32[]{:S(2)}) %collective-permute-start.20) | collective-permute-done | bytes 196640 | tf_op jit(solution)/shard_map/ppermute | solution.py:198
  83.2 1.0 collective-permute-done.21.refs_16_.refs_10_
  84.5 5.8 %shard_map.50 = (f32[64,1280]{1,0:T(8,128)S(1)}, bf16[64,1280]{1,0:T(8,128)(2,1)S(1)}, bf16[64,1280]{1,0:T(8,128)(2,1)S(1)}, bf16[64,1280]{1,0:T(8,128)(2,1)S(1)...) custom-call(s32[4]{0:T(128)S(1)} %pad_add_fusion.s_ref, ...), custom_call_target="tpu_custom_call" | custom-call | flops 2684354560 | bytes 7340032 | tf_op jit(solution)/shard_map/pallas_call | solution.py:244
  90.4 0.7 collective-permute-start.32
  91.0 1.3 collective-permute-start.33
  92.3 0.8 collective-permute-start.34
  93.1 2.4 %collective-permute-start.23 = (bf16[64,1280]{1,0:T(8,128)(2,1)S(1)}, bf16[64,1280]{1,0:T(8,128)(2,1)S(1)}, u32[]{:S(2)}, u32[]{:S(2)}) collective-permute-start(bf16[64,1280]{1,0:T(8,128)(2,1)S(1)} %get-tuple-element.106), channel_id=1, source_target_pairs={{0,12},{4,0},{8,4},{12,8},{1,13},{5,1},{9,5},{13,9},{2,14},{6,2},{... | collective-permute-start | bytes 491528 | tf_op jit(solution)/shard_map/ppermute | solution.py:198
  95.6 1.0 collective-permute-start.24
  96.6 0.9 collective-permute-done.32.a_ref
  97.5 0.5 collective-permute-start.25
  98.0 1.6 %collective-permute-done.33.b_ref = bf16[64,1280]{1,0:T(8,128)(2,1)S(1)} collective-permute-done((bf16[64,1280]{1,0:T(8,128)(2,1)S(1)}, bf16[64,1280]{1,0:T(8,128)(2,1)S(1)}, u32[]{:S(2)}, u32[]{:S(2)}) %collective-permute-start.33) | collective-permute-done | bytes 163872 | tf_op jit(solution)/shard_map/ppermute | solution.py:198
  99.7 3.6 %collective-permute-done.34.c_ref = bf16[64,1280]{1,0:T(8,128)(2,1)S(1)} collective-permute-done((bf16[64,1280]{1,0:T(8,128)(2,1)S(1)}, bf16[64,1280]{1,0:T(8,128)(2,1)S(1)}, u32[]{:S(2)}, u32[]{:S(2)}) %collective-permute-start.34) | collective-permute-done | bytes 163872 | tf_op jit(solution)/shard_map/ppermute | solution.py:198
  103.2 0.6 shard_map.53.refs_4_
  103.9 0.6 collective-permute-start.35
  104.4 1.3 collective-permute-start.36
  105.7 0.9 collective-permute-start.37
  106.7 2.5 %shard_map.49.right_ref = bf16[2048,2048]{1,0:T(8,128)(2,1)S(1)} custom-call(s32[4]{0:T(128)S(1)} %pad_add_fusion.s_ref, f32[64,2048]{1,0:T(8,128)S(1)} %get-tuple-element.67.mk_ref, bf16[128,2048]{1,0:T(8,128)(2,1)S(1)} %constant_dynamic-slice_fusion.refs_0_, bf16[128,2048]{1,0:T(8,128)(2,1)S(1)} %collective-permute-done.2.refs_1_, ...), custom_call_target="tpu_custom_call" | custom-call | bytes 16777216 | tf_op jit(solution)/shard_map/pallas_call | solution.py:283
  109.2 0.8 collective-permute-done.25.c_ref
  110.0 0.6 shard_map.51.refs_4_
  110.7 1.6 %collective-permute-start.26 = (bf16[64,1280]{1,0:T(8,128)(2,1)S(1)}, bf16[64,1280]{1,0:T(8,128)(2,1)S(1)}, u32[]{:S(2)}, u32[]{:S(2)}) collective-permute-start(bf16[64,1280]{1,0:T(8,128)(2,1)S(1)} %shard_map.51.refs_4_), channel_id=1, source_target_pairs={{0,12},{4,0},{8,4},{12,8},{1,13},{5,1},{9,5},{13,9},{2,14},{6,2},{... | collective-permute-start | bytes 491528 | tf_op jit(solution)/shard_map/ppermute | solution.py:198
  112.2 1.2 collective-permute-start.27
  113.5 1.3 collective-permute-start.28
  114.8 3.9 %collective-permute-done.37.refs_7_ = bf16[64,1280]{1,0:T(8,128)(2,1)S(1)} collective-permute-done((bf16[64,1280]{1,0:T(8,128)(2,1)S(1)}, bf16[64,1280]{1,0:T(8,128)(2,1)S(1)}, u32[]{:S(2)}, u32[]{:S(2)}) %collective-permute-start.37) | collective-permute-done | bytes 163872 | tf_op jit(solution)/shard_map/ppermute | solution.py:198
  118.7 5.3 %shard_map.54 = (f32[256,512]{1,0:T(8,128)S(1)}, bf16[256,512]{1,0:T(8,128)(2,1)S(1)}, bf16[256,512]{1,0:T(8,128)(2,1)S(1)}, bf16[256,512]{1,0:T(8,128)(2,1)S(1)}) custom-call(s32[4]{0:T(128)S(1)} %pad_add_fusion.s_ref, f32[16,2048]{1,0:T(8,128)S(1)} %get-tuple-element.66.mc_ref, bf16[2048,2048]{1,0:T(8,128)(2,1)S(1)} %shard_map.49.right_ref, ...), custom_call_target="tpu_custom_call" | custom-call | flops 2147483648 | bytes 10485760 | tf_op jit(solution)/shard_map/pallas_call | solution.py:287
  124.0 2.8 %collective-permute-start.38 = (bf16[256,512]{1,0:T(8,128)(2,1)S(1)}, bf16[256,512]{1,0:T(8,128)(2,1)S(1)}, u32[]{:S(2)}, u32[]{:S(2)}) collective-permute-start(bf16[256,512]{1,0:T(8,128)(2,1)S(1)} %get-tuple-element.118), channel_id=1, source_target_pairs={{0,3},{1,0},{2,1},{3,2},{4,7},{5,4},{6,5},{7,6},{8,11},{9,8},{10,9... | collective-permute-start | bytes 786440 | tf_op jit(solution)/shard_map/ppermute | solution.py:198
  126.9 0.8 collective-permute-start.39
  127.7 0.9 collective-permute-start.40
  128.6 5.4 %shard_map.52 = (f32[256,512]{1,0:T(8,128)S(1)}, bf16[256,512]{1,0:T(8,128)(2,1)S(1)}, bf16[256,512]{1,0:T(8,128)(2,1)S(1)}, bf16[256,512]{1,0:T(8,128)(2,1)S(1)}) custom-call(s32[4]{0:T(128)S(1)} %pad_add_fusion.s_ref, f32[16,2048]{1,0:T(8,128)S(1)} %get-tuple-element.66.mc_ref, bf16[2048,2048]{1,0:T(8,128)(2,1)S(1)} %shard_map.49.right_ref, ...), custom_call_target="tpu_custom_call" | custom-call | flops 2147483648 | bytes 10485760 | tf_op jit(solution)/shard_map/pallas_call | solution.py:287
  133.9 2.4 %collective-permute-start.29 = (bf16[256,512]{1,0:T(8,128)(2,1)S(1)}, bf16[256,512]{1,0:T(8,128)(2,1)S(1)}, u32[]{:S(2)}, u32[]{:S(2)}) collective-permute-start(bf16[256,512]{1,0:T(8,128)(2,1)S(1)} %get-tuple-element.110), channel_id=1, source_target_pairs={{0,3},{1,0},{2,1},{3,2},{4,7},{5,4},{6,5},{7,6},{8,11},{9,8},{10,9... | collective-permute-start | bytes 786440 | tf_op jit(solution)/shard_map/ppermute | solution.py:198
  136.3 1.5 collective-permute-start.30
  137.9 6.8 %collective-permute-done.40.refs_7_ = bf16[256,512]{1,0:T(8,128)(2,1)S(1)} collective-permute-done((bf16[256,512]{1,0:T(8,128)(2,1)S(1)}, bf16[256,512]{1,0:T(8,128)(2,1)S(1)}, u32[]{:S(2)}, u32[]{:S(2)}) %collective-permute-start.40) | collective-permute-done | bytes 262176 | tf_op jit(solution)/shard_map/ppermute | solution.py:198
  144.7 2.6 %collective-permute-done.29.refs_1_ = bf16[256,512]{1,0:T(8,128)(2,1)S(1)} collective-permute-done((bf16[256,512]{1,0:T(8,128)(2,1)S(1)}, bf16[256,512]{1,0:T(8,128)(2,1)S(1)}, u32[]{:S(2)}, u32[]{:S(2)}) %collective-permute-start.29) | collective-permute-done | bytes 262176 | tf_op jit(solution)/shard_map/ppermute | solution.py:198
  147.3 0.7 collective-permute-done.30.refs_2_
  148.0 3.0 %collective-permute-done.31.refs_3_ = bf16[256,512]{1,0:T(8,128)(2,1)S(1)} collective-permute-done((bf16[256,512]{1,0:T(8,128)(2,1)S(1)}, bf16[256,512]{1,0:T(8,128)(2,1)S(1)}, u32[]{:S(2)}, u32[]{:S(2)}) %collective-permute-start.31) | collective-permute-done | bytes 262176 | tf_op jit(solution)/shard_map/ppermute | solution.py:198
  151.0 1.6 %shard_map.55 = bf16[512,512]{1,0:T(8,128)(2,1)} custom-call(s32[4]{0:T(128)S(1)} %pad_add_fusion.s_ref, f32[256,512]{1,0:T(8,128)S(1)} %get-tuple-element.109.refs_0_, bf16[256,512]{1,0:T(8,128)(2,1)S(1)} %collective-permute-done.29.refs_1_, bf16[256,512]{1,0:T(8,128)(2,1)S(1)} %collective-permute-done.30.refs_2_, ...), custom_call_target="tpu_custom_call" | custom-call | bytes 3145728 | tf_op jit(solution)/shard_map/pallas_call | solution.py:296
  (44 shorter events, 2.6 us)
Async XLA Ops:
  3.3 28.2 %collective-permute-start = (bf16[128,2048]{1,0:T(8,128)(2,1)S(1)}, bf16[128,2048]{1,0:T(8,128)(2,1)S(1)}, u32[]{:S(2)}, u32[]{:S(2)}) collective-permute-start(bf16[128,2048]{1,0:T(8,128)(2,1)S(1)} %constant_dynamic-slice_fusion.refs_0_), channel_id=1, source_target_pairs={{0,32},{16,48},{32,64},{48,80},{64,96},{80,112},{96,128},{112,144}... | collective-permute-start | bytes 1572872 | tf_op jit(solution)/shard_map/ppermute | solution.py:198
  5.2 26.3 %collective-permute-start.1 = (bf16[128,2048]{1,0:T(8,128)(2,1)S(1)}, bf16[128,2048]{1,0:T(8,128)(2,1)S(1)}, u32[]{:S(2)}, u32[]{:S(2)}) collective-permute-start(bf16[128,2048]{1,0:T(8,128)(2,1)S(1)} %constant_dynamic-slice_fusion.refs_0_), channel_id=1, source_target_pairs={{0,224},{16,240},{32,0},{48,16},{64,32},{80,48},{96,64},{112,80},{... | collective-permute-start | bytes 1572872 | tf_op jit(solution)/shard_map/ppermute | solution.py:198
  5.3 26.1 %all-to-all-start = ((bf16[64,16,128]{2,1,0:T(8,128)(2,1)}), bf16[64,16,128]{2,1,0:T(8,128)(2,1)S(1)}, u32[]{:S(2)}, u32[]{:S(2)}) async-start(bf16[64,16,128]{2,1,0:T(8,128)(2,1)} %broadcast_in_dim.3), calls=%async_computation | async-start | bytes 524288 | tf_op jit(solution)/shard_map/all_to_all | solution.py:217
  18.3 21.8 %collective-permute-start.2 = (bf16[128,2048]{1,0:T(8,128)(2,1)S(1)}, bf16[128,2048]{1,0:T(8,128)(2,1)S(1)}, u32[]{:S(2)}, u32[]{:S(2)}) collective-permute-start(bf16[128,2048]{1,0:T(8,128)(2,1)S(1)} %constant_dynamic-slice_fusion.refs_0_), channel_id=1, source_target_pairs={{0,16},{16,0},{32,48},{48,32},{64,80},{80,64},{96,112},{112,96},{1... | collective-permute-start | bytes 1572872 | tf_op jit(solution)/shard_map/ppermute | solution.py:202
  31.5 8.7 %collective-permute-start.3 = (bf16[128,2048]{1,0:T(8,128)(2,1)S(1)}, bf16[128,2048]{1,0:T(8,128)(2,1)S(1)}, u32[]{:S(2)}, u32[]{:S(2)}) collective-permute-start(bf16[128,2048]{1,0:T(8,128)(2,1)S(1)} %collective-permute-done.refs_2_), channel_id=1, source_target_pairs={{0,16},{16,0},{32,48},{48,32},{64,80},{80,64},{96,112},{112,96},{1... | collective-permute-start | bytes 1572872 | tf_op jit(solution)/shard_map/ppermute | solution.py:202
  31.6 8.6 %collective-permute-start.4 = (bf16[128,2048]{1,0:T(8,128)(2,1)S(1)}, bf16[128,2048]{1,0:T(8,128)(2,1)S(1)}, u32[]{:S(2)}, u32[]{:S(2)}) collective-permute-start(bf16[128,2048]{1,0:T(8,128)(2,1)S(1)} %collective-permute-done.1.refs_4_), channel_id=1, source_target_pairs={{0,16},{16,0},{32,48},{48,32},{64,80},{80,64},{96,112},{112,96},{1... | collective-permute-start | bytes 1572872 | tf_op jit(solution)/shard_map/ppermute | solution.py:202
  32.0 14.0 %collective-permute-start.5 = (bf16[128,2048]{1,0:T(8,128)(2,1)S(1)}, bf16[128,2048]{1,0:T(8,128)(2,1)}, u32[]{:S(2)}, u32[]{:S(2)}) collective-permute-start(bf16[128,2048]{1,0:T(8,128)(2,1)S(1)} %collective-permute-done.refs_2_), channel_id=1, source_target_pairs={{0,32},{16,48},{32,64},{48,80},{64,96},{80,112},{96,128},{112,144}... | collective-permute-start | bytes 1572872 | tf_op jit(solution)/shard_map/ppermute | solution.py:198
  32.1 13.9 %collective-permute-start.6 = (bf16[128,2048]{1,0:T(8,128)(2,1)S(1)}, bf16[128,2048]{1,0:T(8,128)(2,1)}, u32[]{:S(2)}, u32[]{:S(2)}) collective-permute-start(bf16[128,2048]{1,0:T(8,128)(2,1)S(1)} %collective-permute-done.1.refs_4_), channel_id=1, source_target_pairs={{0,224},{16,240},{32,0},{48,16},{64,32},{80,48},{96,64},{112,80},{... | collective-permute-start | bytes 1572872 | tf_op jit(solution)/shard_map/ppermute | solution.py:198
  34.1 1.6 %copy-start = (bf16[512,2048]{1,0:T(8,128)(2,1)S(1)}, bf16[512,2048]{1,0:T(8,128)(2,1)}, u32[]{:S(2)}) copy-start(bf16[512,2048]{1,0:T(8,128)(2,1)} %refs_3_.1) | copy-start | bytes 6291460
  35.7 0.7 copy-start.1
  36.4 0.7 copy-start.2
  46.0 13.9 %collective-permute-start.7 = (bf16[128,2048]{1,0:T(8,128)(2,1)}, bf16[128,2048]{1,0:T(8,128)(2,1)S(1)}, u32[]{:S(2)}, u32[]{:S(2)}) collective-permute-start(bf16[128,2048]{1,0:T(8,128)(2,1)} %collective-permute-done.5.refs_6_.refs_0_), channel_id=1, source_target_pairs={{0,32},{16,48},{32,64},{48,80},{64,96},{80,112},{96,128},{112,144}... | collective-permute-start | bytes 1572872 | tf_op jit(solution)/shard_map/ppermute | solution.py:198
  46.9 13.1 %collective-permute-start.8 = (bf16[128,2048]{1,0:T(8,128)(2,1)}, bf16[128,2048]{1,0:T(8,128)(2,1)S(1)}, u32[]{:S(2)}, u32[]{:S(2)}) collective-permute-start(bf16[128,2048]{1,0:T(8,128)(2,1)} %collective-permute-done.6.refs_8_.refs_2_), channel_id=1, source_target_pairs={{0,224},{16,240},{32,0},{48,16},{64,32},{80,48},{96,64},{112,80},{... | collective-permute-start | bytes 1572872 | tf_op jit(solution)/shard_map/ppermute | solution.py:198
  48.4 11.7 %collective-permute-start.10 = (bf16[128,768]{1,0:T(8,128)(2,1)S(1)}, bf16[128,768]{1,0:T(8,128)(2,1)S(1)}, u32[]{:S(2)}, u32[]{:S(2)}) collective-permute-start(bf16[128,768]{1,0:T(8,128)(2,1)S(1)} %get-tuple-element.79), channel_id=1, source_target_pairs={{0,8},{4,12},{8,0},{12,4},{1,9},{5,13},{9,1},{13,5},{2,10},{6,14},... | collective-permute-start | bytes 589832 | tf_op jit(solution)/shard_map/ppermute | solution.py:198
  49.7 10.4 %collective-permute-start.11 = (bf16[128,768]{1,0:T(8,128)(2,1)S(1)}, bf16[128,768]{1,0:T(8,128)(2,1)S(1)}, u32[]{:S(2)}, u32[]{:S(2)}) collective-permute-start(bf16[128,768]{1,0:T(8,128)(2,1)S(1)} %get-tuple-element.80), channel_id=1, source_target_pairs={{0,4},{4,8},{8,12},{12,0},{1,5},{5,9},{9,13},{13,1},{2,6},{6,10},{... | collective-permute-start | bytes 589832 | tf_op jit(solution)/shard_map/ppermute | solution.py:198
  50.2 9.9 %collective-permute-start.9 = (bf16[128,768]{1,0:T(8,128)(2,1)S(1)}, bf16[128,768]{1,0:T(8,128)(2,1)S(1)}, u32[]{:S(2)}, u32[]{:S(2)}) collective-permute-start(bf16[128,768]{1,0:T(8,128)(2,1)S(1)} %get-tuple-element.78), channel_id=1, source_target_pairs={{0,12},{4,0},{8,4},{12,8},{1,13},{5,1},{9,5},{13,9},{2,14},{6,2},{... | collective-permute-start | bytes 589832 | tf_op jit(solution)/shard_map/ppermute | solution.py:198
  60.1 3.5 %collective-permute-start.12 = (bf16[128,2048]{1,0:T(8,128)(2,1)}, bf16[128,2048]{1,0:T(8,128)(2,1)S(1)}, u32[]{:S(2)}, u32[]{:S(2)}) collective-permute-start(bf16[128,2048]{1,0:T(8,128)(2,1)} %collective-permute-done.5.refs_6_.refs_0_), channel_id=1, source_target_pairs={{0,16},{16,0},{32,48},{48,32},{64,80},{80,64},{96,112},{112,96},{1... | collective-permute-start | bytes 1572872 | tf_op jit(solution)/shard_map/ppermute | solution.py:202
  60.2 3.9 %collective-permute-start.13 = (bf16[128,2048]{1,0:T(8,128)(2,1)}, bf16[128,2048]{1,0:T(8,128)(2,1)S(1)}, u32[]{:S(2)}, u32[]{:S(2)}) collective-permute-start(bf16[128,2048]{1,0:T(8,128)(2,1)} %collective-permute-done.6.refs_8_.refs_2_), channel_id=1, source_target_pairs={{0,16},{16,0},{32,48},{48,32},{64,80},{80,64},{96,112},{112,96},{1... | collective-permute-start | bytes 1572872 | tf_op jit(solution)/shard_map/ppermute | solution.py:202
  60.7 9.7 %collective-permute-start.16 = (bf16[64,2048]{1,0:T(8,128)(2,1)S(1)}, bf16[64,2048]{1,0:T(8,128)(2,1)S(1)}, u32[]{:S(2)}, u32[]{:S(2)}) collective-permute-start(bf16[64,2048]{1,0:T(8,128)(2,1)S(1)} %slice.8), channel_id=1, source_target_pairs={{0,32},{16,48},{32,64},{48,80},{64,96},{80,112},{96,128},{112,144}... | collective-permute-start | bytes 786440 | tf_op jit(solution)/shard_map/ppermute | solution.py:198
  62.2 9.4 %collective-permute-start.17 = (bf16[64,2048]{1,0:T(8,128)(2,1)S(1)}, bf16[64,2048]{1,0:T(8,128)(2,1)S(1)}, u32[]{:S(2)}, u32[]{:S(2)}) collective-permute-start(bf16[64,2048]{1,0:T(8,128)(2,1)S(1)} %slice.9), channel_id=1, source_target_pairs={{0,224},{16,240},{32,0},{48,16},{64,32},{80,48},{96,64},{112,80},{... | collective-permute-start | bytes 786440 | tf_op jit(solution)/shard_map/ppermute | solution.py:198
  63.6 19.6 %collective-permute-start.14 = (bf16[128,2048]{1,0:T(8,128)(2,1)S(1)}, bf16[128,2048]{1,0:T(8,128)(2,1)S(1)}, u32[]{:S(2)}, u32[]{:S(2)}) collective-permute-start(bf16[128,2048]{1,0:T(8,128)(2,1)S(1)} %collective-permute-done.7.refs_10_.refs_4_), channel_id=1, source_target_pairs={{0,16},{16,0},{32,48},{48,32},{64,80},{80,64},{96,112},{112,96},{1... | collective-permute-start | bytes 1572872 | tf_op jit(solution)/shard_map/ppermute | solution.py:202
  63.6 19.6 %collective-permute-start.15 = (bf16[128,2048]{1,0:T(8,128)(2,1)S(1)}, bf16[128,2048]{1,0:T(8,128)(2,1)S(1)}, u32[]{:S(2)}, u32[]{:S(2)}) collective-permute-start(bf16[128,2048]{1,0:T(8,128)(2,1)S(1)} %collective-permute-done.8.refs_12_.refs_6_), channel_id=1, source_target_pairs={{0,16},{16,0},{32,48},{48,32},{64,80},{80,64},{96,112},{112,96},{1... | collective-permute-start | bytes 1572872 | tf_op jit(solution)/shard_map/ppermute | solution.py:202
  64.7 7.2 %collective-permute-start.18 = (bf16[128,768]{1,0:T(8,128)(2,1)S(1)}, bf16[128,768]{1,0:T(8,128)(2,1)S(1)}, u32[]{:S(2)}, u32[]{:S(2)}) collective-permute-start(bf16[128,768]{1,0:T(8,128)(2,1)S(1)} %shard_map.48.refs_0_), channel_id=1, source_target_pairs={{0,12},{4,0},{8,4},{12,8},{1,13},{5,1},{9,5},{13,9},{2,14},{6,2},{... | collective-permute-start | bytes 589832 | tf_op jit(solution)/shard_map/ppermute | solution.py:198
  70.3 9.3 %collective-permute-start.19 = (bf16[128,768]{1,0:T(8,128)(2,1)S(1)}, bf16[128,768]{1,0:T(8,128)(2,1)S(1)}, u32[]{:S(2)}, u32[]{:S(2)}) collective-permute-start(bf16[128,768]{1,0:T(8,128)(2,1)S(1)} %shard_map.48.refs_0_), channel_id=1, source_target_pairs={{0,8},{4,12},{8,0},{12,4},{1,9},{5,13},{9,1},{13,5},{2,10},{6,14},... | collective-permute-start | bytes 589832 | tf_op jit(solution)/shard_map/ppermute | solution.py:198
  71.6 11.0 %collective-permute-start.20 = (bf16[128,768]{1,0:T(8,128)(2,1)S(1)}, bf16[128,768]{1,0:T(8,128)(2,1)S(1)}, u32[]{:S(2)}, u32[]{:S(2)}) collective-permute-start(bf16[128,768]{1,0:T(8,128)(2,1)S(1)} %shard_map.48.refs_0_), channel_id=1, source_target_pairs={{0,4},{4,8},{8,12},{12,0},{1,5},{5,9},{9,13},{13,1},{2,6},{6,10},{... | collective-permute-start | bytes 589832 | tf_op jit(solution)/shard_map/ppermute | solution.py:198
  82.6 1.5 %collective-permute-start.21 = (bf16[64,2048]{1,0:T(8,128)(2,1)S(1)}, bf16[64,2048]{1,0:T(8,128)(2,1)S(1)}, u32[]{:S(2)}, u32[]{:S(2)}) collective-permute-start(bf16[64,2048]{1,0:T(8,128)(2,1)S(1)} %collective-permute-done.16.refs_14_.refs_8_), channel_id=1, source_target_pairs={{0,16},{16,0},{32,48},{48,32},{64,80},{80,64},{96,112},{112,96},{1... | collective-permute-start | bytes 786440 | tf_op jit(solution)/shard_map/ppermute | solution.py:202
  82.7 1.9 %collective-permute-start.22 = (bf16[64,2048]{1,0:T(8,128)(2,1)S(1)}, bf16[64,2048]{1,0:T(8,128)(2,1)S(1)}, u32[]{:S(2)}, u32[]{:S(2)}) collective-permute-start(bf16[64,2048]{1,0:T(8,128)(2,1)S(1)} %collective-permute-done.17.refs_15_.refs_9_), channel_id=1, source_target_pairs={{0,16},{16,0},{32,48},{48,32},{64,80},{80,64},{96,112},{112,96},{1... | collective-permute-start | bytes 786440 | tf_op jit(solution)/shard_map/ppermute | solution.py:202
  90.4 7.1 %collective-permute-start.32 = (bf16[64,1280]{1,0:T(8,128)(2,1)S(1)}, bf16[64,1280]{1,0:T(8,128)(2,1)S(1)}, u32[]{:S(2)}, u32[]{:S(2)}) collective-permute-start(bf16[64,1280]{1,0:T(8,128)(2,1)S(1)} %get-tuple-element.114), channel_id=1, source_target_pairs={{0,12},{4,0},{8,4},{12,8},{1,13},{5,1},{9,5},{13,9},{2,14},{6,2},{... | collective-permute-start | bytes 491528 | tf_op jit(solution)/shard_map/ppermute | solution.py:198
  91.0 8.6 %collective-permute-start.33 = (bf16[64,1280]{1,0:T(8,128)(2,1)S(1)}, bf16[64,1280]{1,0:T(8,128)(2,1)S(1)}, u32[]{:S(2)}, u32[]{:S(2)}) collective-permute-start(bf16[64,1280]{1,0:T(8,128)(2,1)S(1)} %get-tuple-element.115), channel_id=1, source_target_pairs={{0,8},{4,12},{8,0},{12,4},{1,9},{5,13},{9,1},{13,5},{2,10},{6,14},... | collective-permute-start | bytes 491528 | tf_op jit(solution)/shard_map/ppermute | solution.py:198
  92.3 10.9 %collective-permute-start.34 = (bf16[64,1280]{1,0:T(8,128)(2,1)S(1)}, bf16[64,1280]{1,0:T(8,128)(2,1)S(1)}, u32[]{:S(2)}, u32[]{:S(2)}) collective-permute-start(bf16[64,1280]{1,0:T(8,128)(2,1)S(1)} %get-tuple-element.116), channel_id=1, source_target_pairs={{0,4},{4,8},{8,12},{12,0},{1,5},{5,9},{9,13},{13,1},{2,6},{6,10},{... | collective-permute-start | bytes 491528 | tf_op jit(solution)/shard_map/ppermute | solution.py:198
  93.1 12.6 %collective-permute-start.23 = (bf16[64,1280]{1,0:T(8,128)(2,1)S(1)}, bf16[64,1280]{1,0:T(8,128)(2,1)S(1)}, u32[]{:S(2)}, u32[]{:S(2)}) collective-permute-start(bf16[64,1280]{1,0:T(8,128)(2,1)S(1)} %get-tuple-element.106), channel_id=1, source_target_pairs={{0,12},{4,0},{8,4},{12,8},{1,13},{5,1},{9,5},{13,9},{2,14},{6,2},{... | collective-permute-start | bytes 491528 | tf_op jit(solution)/shard_map/ppermute | solution.py:198
  95.6 13.6 %collective-permute-start.24 = (bf16[64,1280]{1,0:T(8,128)(2,1)S(1)}, bf16[64,1280]{1,0:T(8,128)(2,1)S(1)}, u32[]{:S(2)}, u32[]{:S(2)}) collective-permute-start(bf16[64,1280]{1,0:T(8,128)(2,1)S(1)} %get-tuple-element.107), channel_id=1, source_target_pairs={{0,8},{4,12},{8,0},{12,4},{1,9},{5,13},{9,1},{13,5},{2,10},{6,14},... | collective-permute-start | bytes 491528 | tf_op jit(solution)/shard_map/ppermute | solution.py:198
  97.5 12.5 %collective-permute-start.25 = (bf16[64,1280]{1,0:T(8,128)(2,1)S(1)}, bf16[64,1280]{1,0:T(8,128)(2,1)S(1)}, u32[]{:S(2)}, u32[]{:S(2)}) collective-permute-start(bf16[64,1280]{1,0:T(8,128)(2,1)S(1)} %get-tuple-element.108), channel_id=1, source_target_pairs={{0,4},{4,8},{8,12},{12,0},{1,5},{5,9},{9,13},{13,1},{2,6},{6,10},{... | collective-permute-start | bytes 491528 | tf_op jit(solution)/shard_map/ppermute | solution.py:198
  103.9 9.6 %collective-permute-start.35 = (bf16[64,1280]{1,0:T(8,128)(2,1)S(1)}, bf16[64,1280]{1,0:T(8,128)(2,1)S(1)}, u32[]{:S(2)}, u32[]{:S(2)}) collective-permute-start(bf16[64,1280]{1,0:T(8,128)(2,1)S(1)} %shard_map.53.refs_4_), channel_id=1, source_target_pairs={{0,12},{4,0},{8,4},{12,8},{1,13},{5,1},{9,5},{13,9},{2,14},{6,2},{... | collective-permute-start | bytes 491528 | tf_op jit(solution)/shard_map/ppermute | solution.py:198
  104.4 10.4 %collective-permute-start.36 = (bf16[64,1280]{1,0:T(8,128)(2,1)S(1)}, bf16[64,1280]{1,0:T(8,128)(2,1)S(1)}, u32[]{:S(2)}, u32[]{:S(2)}) collective-permute-start(bf16[64,1280]{1,0:T(8,128)(2,1)S(1)} %shard_map.53.refs_4_), channel_id=1, source_target_pairs={{0,8},{4,12},{8,0},{12,4},{1,9},{5,13},{9,1},{13,5},{2,10},{6,14},... | collective-permute-start | bytes 491528 | tf_op jit(solution)/shard_map/ppermute | solution.py:198
  105.7 13.0 %collective-permute-start.37 = (bf16[64,1280]{1,0:T(8,128)(2,1)S(1)}, bf16[64,1280]{1,0:T(8,128)(2,1)S(1)}, u32[]{:S(2)}, u32[]{:S(2)}) collective-permute-start(bf16[64,1280]{1,0:T(8,128)(2,1)S(1)} %shard_map.53.refs_4_), channel_id=1, source_target_pairs={{0,4},{4,8},{8,12},{12,0},{1,5},{5,9},{9,13},{13,1},{2,6},{6,10},{... | collective-permute-start | bytes 491528 | tf_op jit(solution)/shard_map/ppermute | solution.py:198
  110.7 17.0 %collective-permute-start.26 = (bf16[64,1280]{1,0:T(8,128)(2,1)S(1)}, bf16[64,1280]{1,0:T(8,128)(2,1)S(1)}, u32[]{:S(2)}, u32[]{:S(2)}) collective-permute-start(bf16[64,1280]{1,0:T(8,128)(2,1)S(1)} %shard_map.51.refs_4_), channel_id=1, source_target_pairs={{0,12},{4,0},{8,4},{12,8},{1,13},{5,1},{9,5},{13,9},{2,14},{6,2},{... | collective-permute-start | bytes 491528 | tf_op jit(solution)/shard_map/ppermute | solution.py:198
  112.2 16.4 %collective-permute-start.27 = (bf16[64,1280]{1,0:T(8,128)(2,1)S(1)}, bf16[64,1280]{1,0:T(8,128)(2,1)S(1)}, u32[]{:S(2)}, u32[]{:S(2)}) collective-permute-start(bf16[64,1280]{1,0:T(8,128)(2,1)S(1)} %shard_map.51.refs_4_), channel_id=1, source_target_pairs={{0,8},{4,12},{8,0},{12,4},{1,9},{5,13},{9,1},{13,5},{2,10},{6,14},... | collective-permute-start | bytes 491528 | tf_op jit(solution)/shard_map/ppermute | solution.py:198
  113.5 15.1 %collective-permute-start.28 = (bf16[64,1280]{1,0:T(8,128)(2,1)S(1)}, bf16[64,1280]{1,0:T(8,128)(2,1)S(1)}, u32[]{:S(2)}, u32[]{:S(2)}) collective-permute-start(bf16[64,1280]{1,0:T(8,128)(2,1)S(1)} %shard_map.51.refs_4_), channel_id=1, source_target_pairs={{0,4},{4,8},{8,12},{12,0},{1,5},{5,9},{9,13},{13,1},{2,6},{6,10},{... | collective-permute-start | bytes 491528 | tf_op jit(solution)/shard_map/ppermute | solution.py:198
  124.0 13.8 %collective-permute-start.38 = (bf16[256,512]{1,0:T(8,128)(2,1)S(1)}, bf16[256,512]{1,0:T(8,128)(2,1)S(1)}, u32[]{:S(2)}, u32[]{:S(2)}) collective-permute-start(bf16[256,512]{1,0:T(8,128)(2,1)S(1)} %get-tuple-element.118), channel_id=1, source_target_pairs={{0,3},{1,0},{2,1},{3,2},{4,7},{5,4},{6,5},{7,6},{8,11},{9,8},{10,9... | collective-permute-start | bytes 786440 | tf_op jit(solution)/shard_map/ppermute | solution.py:198
  126.9 11.0 %collective-permute-start.39 = (bf16[256,512]{1,0:T(8,128)(2,1)S(1)}, bf16[256,512]{1,0:T(8,128)(2,1)S(1)}, u32[]{:S(2)}, u32[]{:S(2)}) collective-permute-start(bf16[256,512]{1,0:T(8,128)(2,1)S(1)} %get-tuple-element.119), channel_id=1, source_target_pairs={{0,2},{1,3},{2,0},{3,1},{4,6},{5,7},{6,4},{7,5},{8,10},{9,11},{10,... | collective-permute-start | bytes 786440 | tf_op jit(solution)/shard_map/ppermute | solution.py:198
  127.7 17.0 %collective-permute-start.40 = (bf16[256,512]{1,0:T(8,128)(2,1)S(1)}, bf16[256,512]{1,0:T(8,128)(2,1)S(1)}, u32[]{:S(2)}, u32[]{:S(2)}) collective-permute-start(bf16[256,512]{1,0:T(8,128)(2,1)S(1)} %get-tuple-element.120), channel_id=1, source_target_pairs={{0,1},{1,2},{2,3},{3,0},{4,5},{5,6},{6,7},{7,4},{8,9},{9,10},{10,1... | collective-permute-start | bytes 786440 | tf_op jit(solution)/shard_map/ppermute | solution.py:198
  133.9 13.4 %collective-permute-start.29 = (bf16[256,512]{1,0:T(8,128)(2,1)S(1)}, bf16[256,512]{1,0:T(8,128)(2,1)S(1)}, u32[]{:S(2)}, u32[]{:S(2)}) collective-permute-start(bf16[256,512]{1,0:T(8,128)(2,1)S(1)} %get-tuple-element.110), channel_id=1, source_target_pairs={{0,3},{1,0},{2,1},{3,2},{4,7},{5,4},{6,5},{7,6},{8,11},{9,8},{10,9... | collective-permute-start | bytes 786440 | tf_op jit(solution)/shard_map/ppermute | solution.py:198
  136.3 11.7 %collective-permute-start.30 = (bf16[256,512]{1,0:T(8,128)(2,1)S(1)}, bf16[256,512]{1,0:T(8,128)(2,1)S(1)}, u32[]{:S(2)}, u32[]{:S(2)}) collective-permute-start(bf16[256,512]{1,0:T(8,128)(2,1)S(1)} %get-tuple-element.111), channel_id=1, source_target_pairs={{0,2},{1,3},{2,0},{3,1},{4,6},{5,7},{6,4},{7,5},{8,10},{9,11},{10,... | collective-permute-start | bytes 786440 | tf_op jit(solution)/shard_map/ppermute | solution.py:198
  137.9 13.1 %collective-permute-start.31 = (bf16[256,512]{1,0:T(8,128)(2,1)S(1)}, bf16[256,512]{1,0:T(8,128)(2,1)S(1)}, u32[]{:S(2)}, u32[]{:S(2)}) collective-permute-start(bf16[256,512]{1,0:T(8,128)(2,1)S(1)} %get-tuple-element.112), channel_id=1, source_target_pairs={{0,1},{1,2},{2,3},{3,0},{4,5},{5,6},{6,7},{7,4},{8,9},{9,10},{10,1... | collective-permute-start | bytes 786440 | tf_op jit(solution)/shard_map/ppermute | solution.py:198

commit v3 on v1

--- a/solution.py
+++ b/solution.py
@@ -20,14 +20,13 @@
 HALVES = 2
 
 
-def call(kernel, out_shape, n_in, scratch=(), flops=0, byts=0, mib=24, aliases={}):
+def call(kernel, out_shape, n_in, scratch=(), flops=0, byts=0, far=False, mib=24):
     return pl.pallas_call(
         kernel,
         out_shape=out_shape,
-        in_specs=[SMEM] + [VMEM] * (n_in - 1),
+        in_specs=[SMEM] + [VMEM] * (n_in - 1 - far) + [pl.BlockSpec(memory_space=pl.ANY)] * far,
         out_specs=jax.tree.map(lambda _: VMEM, out_shape),
         scratch_shapes=list(scratch),
-        input_output_aliases=aliases,
         compiler_params=pltpu.CompilerParams(vmem_limit_bytes=mib << 20),
         cost_estimate=pl.CostEstimate(flops=flops, bytes_accessed=byts, transcendentals=0),
     )
@@ -104,34 +103,48 @@
             done += BLK
 
 
-def load_slots(slots, where, gathered_ref, mask_ref, out_ref):
+def fetch_slots(slots, where, gathered_ref, mask_ref, out_ref, sems):
     z, core = where
+    copies = []
     for n, slot in enumerate(slots):
         chip = lax.rem(z + SLOTS[slot] + 8, 8)
         for other in range(2):
             start = pl.multiple_of(128 * (2 * chip + lax.rem(core + other, 2)), 128)
-            for block in range(4):
-                row = 8 * slot + 4 * other + block
-                keep = jnp.broadcast_to(mask_ref[pl.ds(row, 1), :], (BLK, 2048)).astype(BF)
-                out_ref[pl.ds(256 * n + 128 * other + BLK * block, BLK), :] = (
-                    gathered_ref[pl.ds(start + BLK * block, BLK), :] * keep
-                )
+            copy = pltpu.make_async_copy(
+                gathered_ref.at[pl.ds(start, 128), :],
+                out_ref.at[pl.ds(256 * n + 128 * other, 128), :],
+                sems.at[2 * n + other],
+            )
+            copy.start()
+            copies.append(copy)
+
+    def mask(n):
+        copies[2 * n].wait()
+        copies[2 * n + 1].wait()
+        for block in range(8):
+            keep = mask_ref[pl.ds(8 * slots[n] + block, 1), :]
+            rows = pl.ds(256 * n + BLK * block, BLK)
+            out_ref[rows, :] = out_ref[rows, :] * jnp.broadcast_to(keep, (BLK, 2048)).astype(BF)
+
+    return mask
 
 
 def product_one_kernel(slots, halves, n_pieces, s_ref, left_ref, mt_ref, *refs):
-    pieces, outs, right = refs[:n_pieces], refs[n_pieces:-1], refs[-1]
+    pieces, outs, (right, sems) = refs[:n_pieces], refs[n_pieces:-2], refs[-2:]
     if n_pieces > 1:
         load_pieces(pieces, mt_ref, 8 * slots[0], right)
+        mask = lambda n: None
     else:
-        load_slots(slots, (s_ref[0], s_ref[1]), pieces[0], mt_ref, right)
+        mask = fetch_slots(slots, (s_ref[0], s_ref[1]), pieces[0], mt_ref, right, sems)
     height = 128 // halves
-    for start in range(0, right.shape[0], 256):
-        block = dot(left_ref[...], right[pl.ds(start, 256), :], NT)
+    for n in range(len(slots)):
+        mask(n)
+        block = dot(left_ref[...], right[pl.ds(256 * n, 256), :], NT)
         for half in range(halves):
             for quarter in range(4):
                 row = 128 * quarter + height * half
                 out = outs[4 * half + quarter]
-                out[:, pl.ds(start, 256)] = block[row : row + height].astype(out.dtype)
+                out[:, pl.ds(256 * n, 256)] = block[row : row + height].astype(out.dtype)
 
 
 def square_kernel(first_slot, first_block, s_ref, ms_ref, own_ref, a_ref, b_ref, c_ref, out_ref):
@@ -143,8 +156,11 @@
         out_ref[rows, :] = (total[rows] * keep).astype(BF)
 
 
-def right_kernel(s_ref, mk_ref, gathered_ref, out_ref):
-    load_slots(range(len(SLOTS)), (s_ref[0], s_ref[1]), gathered_ref, mk_ref, out_ref)
+def right_kernel(s_ref, mk_ref, gathered_ref, out_ref, sems):
+    slots = range(len(SLOTS))
+    mask = fetch_slots(slots, (s_ref[0], s_ref[1]), gathered_ref, mk_ref, out_ref, sems)
+    for n in slots:
+        mask(n)
 
 
 def product_two_kernel(half, n_early, s_ref, mc_ref, right_ref, *refs):
@@ -241,9 +257,11 @@
             functools.partial(product_one_kernel, slots, halves, len(held)),
             ((shape(height, width, dtype=F32),) + (shape(height, width),) * 3) * halves,
             3 + len(held),
-            [pltpu.VMEM((width, 2048), BF)],
+            [pltpu.VMEM((width, 2048), BF), pltpu.SemaphoreType.DMA((2 * len(slots),))],
             flops=2 * 512 * 2048 * width,
             byts=2 * 2048 * (512 + width),
+            far=len(held) == 1,
+            mib=54 if len(held) == 1 else 24,
         )(where, left, mt, *held)
         squares = []
         for half in range(halves):
@@ -260,7 +278,9 @@
     first = start(range(EARLY), 1, early)[0] if EARLY else ()
     first, gathered = lax.optimization_barrier((first, gathered))
     squares = start(range(EARLY, len(SLOTS)), HALVES, [gathered])
-    right = call(right_kernel, shape(2048, 2048), 3, byts=16 << 20)(where, mk, gathered)
+    right = call(
+        right_kernel, shape(2048, 2048), 3, [pltpu.SemaphoreType.DMA((2 * len(SLOTS),))], byts=16 << 20, far=True, mib=46
+    )(where, mk, gathered)
     results = []
     for half in range(HALVES):
         height = 512 // HALVES

time: 153 us -> 160 us (1.046)
  Pallas kernels: 22.4 us -> 35.1 us
  waiting for transfers between devices: 59.8 us -> 54.1 us
  starting transfers between devices: 45.9 us -> 47.8 us
  local copies, waits for them, and re-layouts: 9.6 us -> 7.95 us
    pallas_call x2, Pallas kernels: 8.04 us -> 14.6 us  [start(): call(functools.partial(product_one_kernel, slots, halves, len(held)), ((s...]
    pallas_call x1, Pallas kernels: 1.25 us -> 7.42 us  [body(): call(right_kernel, shape(2048, 2048), 3, [pltpu.SemaphoreType.DMA((2 * le...]
    ppermute x26, waiting for transfers between devices: 45.1 us -> 39.4 us  [shift(): lax.ppermute(array, axis, [(i, (i + step) % size) for i in range(size)])]
    ppermute x26, starting transfers between devices: 32.2 us -> 34 us  [shift(): lax.ppermute(array, axis, [(i, (i + step) % size) for i in range(size)])]
    unnamed x22 -> x26, local copies, waits for them, and re-layouts: 6.83 us -> 5.19 us
  transfers between devices with their start and end apart: 31 -> 31, of which waited for: 15 -> 13; matrix products, arithmetic and copies ran while one was open for 2% -> 1% of each run, Pallas kernels for 11% -> 15%
where the time goes in v3:
time: 160 us
  waiting for transfers between devices  54.1 us (34%)
  starting transfers between devices  47.8 us (30%)
  Pallas kernels  35.1 us (22%)
  between operations  13.6 us (8%)
  local copies, waits for them, and re-layouts  7.95 us (5%)
    ppermute x26, waiting for transfers between devices, shift(): lax.ppermute(array, axis, [(i, (i + step) % size) for i in range(size)])  39.4 us
    ppermute x26, starting transfers between devices, shift(): lax.ppermute(array, axis, [(i, (i + step) % size) for i in range(size)])  34 us
    all_to_all x1, waiting for transfers between devices, gather_patterns(): lax.all_to_all(jnp.broadcast_to(both, (64, 16, 128)), ('row', 'col'), 0, 0)  14.6 us
    pallas_call x2, Pallas kernels, start(): call(functools.partial(product_one_kernel, slots, halves, len(held)), ((s...  14.6 us
    all_to_all x1, starting transfers between devices, gather_patterns(): lax.all_to_all(jnp.broadcast_to(both, (64, 16, 128)), ('row', 'col'), 0, 0)  13 us
    pallas_call x1, Pallas kernels, body(): call(right_kernel, shape(2048, 2048), 3, [pltpu.SemaphoreType.DMA((2 * le...  7.42 us
    pallas_call x2, Pallas kernels, body(): call(functools.partial(product_two_kernel, half, len(first)), (shape(heig...  6.51 us
    unnamed x26, local copies, waits for them, and re-layouts  5.19 us
  transfers between devices with their start and end apart: 31, of which 13 were waited for; matrix products, arithmetic and copies ran while one was open for 1% of the time, Pallas kernels for 15%

profile of v3, /device:TPU:32, one launch (start us, length us, event | category | flops | bytes accessed | tf_op | source)
XLA Modules:
  0.0 160.1 jit_solution(4773383142013580407)
XLA Ops:
  6.5 2.0 %constant_dynamic-slice_fusion.refs_0_ = bf16[128,2048]{1,0:T(8,128)(2,1)} fusion(bf16[512,2048]{1,0:T(8,128)(2,1)} %refs_3_.1, s32[]{:T(128)S(6)} %select_n.16), kind=kLoop, calls=%fused_computation.2 | loop fusion | bytes 1048580 | tf_op jit(solution)/shard_map/dynamic_slice | solution.py:233
  8.6 0.0 all-gather.2.cloned.1.call-update
  8.6 2.0 %collective-permute-start.1 = (bf16[128,2048]{1,0:T(8,128)(2,1)}, bf16[128,2048]{1,0:T(8,128)(2,1)}, u32[]{:S(2)}, u32[]{:S(2)}) collective-permute-start(bf16[128,2048]{1,0:T(8,128)(2,1)} %constant_dynamic-slice_fusion.refs_0_), channel_id=1, source_target_pairs={{0,32},{16,48},{32,64},{48,80},{64,96},{80,112},{96,128},{112,144}... | collective-permute-start | bytes 1572872 | tf_op jit(solution)/shard_map/ppermute | solution.py:213
  10.6 0.1 collective-permute-start.3
  10.7 0.7 convert.6
  11.4 0.7 convert.7
  12.1 0.1 pad_maximum_fusion
  12.2 0.7 broadcast_in_dim.3
  12.9 13.0 %all-to-all-start = ((bf16[64,16,128]{2,1,0:T(8,128)(2,1)}), bf16[64,16,128]{2,1,0:T(8,128)(2,1)S(1)}, u32[]{:S(2)}, u32[]{:S(2)}) async-start(bf16[64,16,128]{2,1,0:T(8,128)(2,1)} %broadcast_in_dim.3), calls=%async_computation | async-start | bytes 524288 | tf_op jit(solution)/shard_map/all_to_all | solution.py:227
  25.9 0.2 collective-permute-start
  26.1 0.0 collective-permute-done.1.refs_2_
  26.1 0.4 collective-permute-start.2
  26.5 0.1 collective-permute-start.4
  26.6 0.1 pad_add_fusion.s_ref
  26.7 14.6 %all-to-all-done.refs_0_ = bf16[64,16,128]{2,1,0:T(8,128)(2,1)S(1)} async-done(((bf16[64,16,128]{2,1,0:T(8,128)(2,1)}), bf16[64,16,128]{2,1,0:T(8,128)(2,1)S(1)}, u32[]{:S(2)}, u32[]{:S(2)}) %all-to-all-start) | async-done | bytes 262176 | tf_op jit(solution)/shard_map/all_to_all | solution.py:227
  41.4 3.1 %shard_map.46 = (bf16[512,2048]{1,0:T(8,128)(2,1)S(1)}, f32[64,2048]{1,0:T(8,128)S(1)}, f32[64,2048]{1,0:T(8,128)S(1)}, f32[16,2048]{1,0:T(8,128)S(1)}, f32[16,2048]{1,0:T(8,128)S(1)}) custom-call(s32[4]{0:T(128)S(1)} %pad_add_fusion.s_ref, bf16[64,16,128]{2,1,0:T(8,128)(2,1)S(1)} %all-to-all-done.refs_0_, s32[16,64]{1,0:T(8,128)S(1)} %copy-done.11, ...), custom_call_target="tpu_custom_call" | custom-call | flops 209715200 | bytes 6291456 | tf_op jit(solution)/shard_map/pallas_call | solution.py:240
  44.4 0.8 copy-done.4
  45.3 4.6 %shard_map.47 = (f32[128,768]{1,0:T(8,128)S(1)}, bf16[128,768]{1,0:T(8,128)(2,1)S(1)}, bf16[128,768]{1,0:T(8,128)(2,1)S(1)}, bf16[128,768]{1,0:T(8,128)(2,1)S(1)}) custom-call(s32[4]{0:T(128)S(1)} %pad_add_fusion.s_ref, bf16[512,2048]{1,0:T(8,128)(2,1)S(1)} %get-tuple-element.38.left_ref, f32[64,2048]{1,0:T(8,128)S(1)} %get-tuple-element.39.mt_ref, ...), custom_call_target="tpu_custom_call" | custom-call | flops 1610612736 | bytes 5242880 | tf_op jit(solution)/shard_map/pallas_call | solution.py:256
  49.9 1.4 collective-permute-start.5
  51.3 1.3 collective-permute-start.6
  52.6 0.5 collective-permute-start.7
  53.2 4.6 %collective-permute-done.5.a_ref = bf16[128,768]{1,0:T(8,128)(2,1)S(1)} collective-permute-done((bf16[128,768]{1,0:T(8,128)(2,1)S(1)}, bf16[128,768]{1,0:T(8,128)(2,1)S(1)}, u32[]{:S(2)}, u32[]{:S(2)}) %collective-permute-start.5) | collective-permute-done | bytes 196640 | tf_op jit(solution)/shard_map/ppermute | solution.py:213
  57.8 2.9 %collective-permute-done.6.b_ref = bf16[128,768]{1,0:T(8,128)(2,1)S(1)} collective-permute-done((bf16[128,768]{1,0:T(8,128)(2,1)S(1)}, bf16[128,768]{1,0:T(8,128)(2,1)S(1)}, u32[]{:S(2)}, u32[]{:S(2)}) %collective-permute-start.6) | collective-permute-done | bytes 196640 | tf_op jit(solution)/shard_map/ppermute | solution.py:213
  60.7 2.9 %collective-permute-done.7.c_ref = bf16[128,768]{1,0:T(8,128)(2,1)S(1)} collective-permute-done((bf16[128,768]{1,0:T(8,128)(2,1)S(1)}, bf16[128,768]{1,0:T(8,128)(2,1)S(1)}, u32[]{:S(2)}, u32[]{:S(2)}) %collective-permute-start.7) | collective-permute-done | bytes 196640 | tf_op jit(solution)/shard_map/ppermute | solution.py:213
  63.6 0.7 shard_map.48.refs_0_
  64.3 0.0 copy-start.5
  64.3 0.1 collective-permute-start.10
  64.4 3.2 %collective-permute-start.8 = (bf16[128,768]{1,0:T(8,128)(2,1)S(1)}, bf16[128,768]{1,0:T(8,128)(2,1)S(1)}, u32[]{:S(2)}, u32[]{:S(2)}) collective-permute-start(bf16[128,768]{1,0:T(8,128)(2,1)S(1)} %shard_map.48.refs_0_), channel_id=1, source_target_pairs={{0,12},{4,0},{8,4},{12,8},{1,13},{5,1},{9,5},{13,9},{2,14},{6,2},{... | collective-permute-start | bytes 589832 | tf_op jit(solution)/shard_map/ppermute | solution.py:213
  67.6 0.2 collective-permute-start.9
  67.8 8.8 %collective-permute-done.10.refs_3_ = bf16[128,768]{1,0:T(8,128)(2,1)S(1)} collective-permute-done((bf16[128,768]{1,0:T(8,128)(2,1)S(1)}, bf16[128,768]{1,0:T(8,128)(2,1)S(1)}, u32[]{:S(2)}, u32[]{:S(2)}) %collective-permute-start.10) | collective-permute-done | bytes 196640 | tf_op jit(solution)/shard_map/ppermute | solution.py:213
  76.6 0.0 all-gather.2.cloned.1.call-done.gathered_ref.refs_0_
  76.6 10.0 %shard_map.50 = (f32[64,1280]{1,0:T(8,128)}, bf16[64,1280]{1,0:T(8,128)(2,1)}, bf16[64,1280]{1,0:T(8,128)(2,1)}, bf16[64,1280]{1,0:T(8,128)(2,1)}, f32[64,1280]{...) custom-call(s32[4]{0:T(128)} %copy-done.9, ...), custom_call_target="tpu_custom_call" | custom-call | flops 2684354560 | bytes 7340032 | tf_op jit(solution)/shard_map/pallas_call | solution.py:256
  86.6 3.0 %collective-permute-start.20 = (bf16[64,1280]{1,0:T(8,128)(2,1)}, bf16[64,1280]{1,0:T(8,128)(2,1)S(1)}, u32[]{:S(2)}, u32[]{:S(2)}) collective-permute-start(bf16[64,1280]{1,0:T(8,128)(2,1)} %get-tuple-element.58), channel_id=1, source_target_pairs={{0,12},{4,0},{8,4},{12,8},{1,13},{5,1},{9,5},{13,9},{2,14},{6,2},{... | collective-permute-start | bytes 491528 | tf_op jit(solution)/shard_map/ppermute | solution.py:213
  89.7 1.0 collective-permute-start.22
  90.6 2.3 %collective-permute-start.11 = (bf16[64,1280]{1,0:T(8,128)(2,1)}, bf16[64,1280]{1,0:T(8,128)(2,1)S(1)}, u32[]{:S(2)}, u32[]{:S(2)}) collective-permute-start(bf16[64,1280]{1,0:T(8,128)(2,1)} %get-tuple-element.50), channel_id=1, source_target_pairs={{0,12},{4,0},{8,4},{12,8},{1,13},{5,1},{9,5},{13,9},{2,14},{6,2},{... | collective-permute-start | bytes 491528 | tf_op jit(solution)/shard_map/ppermute | solution.py:213
  92.9 2.3 %collective-permute-start.12 = (bf16[64,1280]{1,0:T(8,128)(2,1)}, bf16[64,1280]{1,0:T(8,128)(2,1)S(1)}, u32[]{:S(2)}, u32[]{:S(2)}) collective-permute-start(bf16[64,1280]{1,0:T(8,128)(2,1)} %get-tuple-element.51), channel_id=1, source_target_pairs={{0,8},{4,12},{8,0},{12,4},{1,9},{5,13},{9,1},{13,5},{2,10},{6,14},... | collective-permute-start | bytes 491528 | tf_op jit(solution)/shard_map/ppermute | solution.py:213
  95.2 2.5 %collective-permute-done.20.a_ref = bf16[64,1280]{1,0:T(8,128)(2,1)S(1)} collective-permute-done((bf16[64,1280]{1,0:T(8,128)(2,1)}, bf16[64,1280]{1,0:T(8,128)(2,1)S(1)}, u32[]{:S(2)}, u32[]{:S(2)}) %collective-permute-start.20) | collective-permute-done | bytes 163872 | tf_op jit(solution)/shard_map/ppermute | solution.py:213
  97.7 0.9 collective-permute-done.21.b_ref
  98.6 3.2 %collective-permute-done.22.c_ref = bf16[64,1280]{1,0:T(8,128)(2,1)S(1)} collective-permute-done((bf16[64,1280]{1,0:T(8,128)(2,1)}, bf16[64,1280]{1,0:T(8,128)(2,1)S(1)}, u32[]{:S(2)}, u32[]{:S(2)}) %collective-permute-start.22) | collective-permute-done | bytes 163872 | tf_op jit(solution)/shard_map/ppermute | solution.py:213
  101.7 1.0 copy-done.8
  102.7 0.6 shard_map.53.refs_4_
  103.3 0.9 collective-permute-start.23
  104.3 1.6 %collective-permute-start.24 = (bf16[64,1280]{1,0:T(8,128)(2,1)S(1)}, bf16[64,1280]{1,0:T(8,128)(2,1)S(1)}, u32[]{:S(2)}, u32[]{:S(2)}) collective-permute-start(bf16[64,1280]{1,0:T(8,128)(2,1)S(1)} %shard_map.53.refs_4_), channel_id=1, source_target_pairs={{0,8},{4,12},{8,0},{12,4},{1,9},{5,13},{9,1},{13,5},{2,10},{6,14},... | collective-permute-start | bytes 491528 | tf_op jit(solution)/shard_map/ppermute | solution.py:213
  105.9 1.3 collective-permute-start.25
  107.2 7.4 %shard_map.49.right_ref = bf16[2048,2048]{1,0:T(8,128)(2,1)} custom-call(s32[4]{0:T(128)S(1)} %copy-done.10, f32[64,2048]{1,0:T(8,128)S(1)} %copy-done.5, bf16[2048,2048]{1,0:T(8,128)(2,1)} %all-gather.2.cloned.1.call-done.gathered_ref.refs_0_), custom_call_target="tpu_custom_call" | custom-call | bytes 16777216 | tf_op jit(solution)/shard_map/pallas_call | solution.py:281
  114.7 0.6 shard_map.51.refs_4_
  115.3 2.0 %collective-permute-start.14 = (bf16[64,1280]{1,0:T(8,128)(2,1)S(1)}, bf16[64,1280]{1,0:T(8,128)(2,1)S(1)}, u32[]{:S(2)}, u32[]{:S(2)}) collective-permute-start(bf16[64,1280]{1,0:T(8,128)(2,1)S(1)} %shard_map.51.refs_4_), channel_id=1, source_target_pairs={{0,12},{4,0},{8,4},{12,8},{1,13},{5,1},{9,5},{13,9},{2,14},{6,2},{... | collective-permute-start | bytes 491528 | tf_op jit(solution)/shard_map/ppermute | solution.py:213
  117.3 0.8 collective-permute-start.15
  118.1 1.1 collective-permute-start.16
  119.2 3.4 %copy-done = bf16[2048,2048]{1,0:T(8,128)(2,1)S(1)} copy-done((bf16[2048,2048]{1,0:T(8,128)(2,1)S(1)}, bf16[2048,2048]{1,0:T(8,128)(2,1)}, u32[]{:S(2)}) %copy-start) | copy-done | bytes 8388632
  122.6 3.3 %shard_map.54 = (f32[256,512]{1,0:T(8,128)S(1)}, bf16[256,512]{1,0:T(8,128)(2,1)S(1)}, bf16[256,512]{1,0:T(8,128)(2,1)S(1)}, bf16[256,512]{1,0:T(8,128)(2,1)S(1)}) custom-call(s32[4]{0:T(128)S(1)} %copy-done.10, f32[16,2048]{1,0:T(8,128)S(1)} %get-tuple-element.35.mc_ref, bf16[2048,2048]{1,0:T(8,128)(2,1)S(1)} %copy-done, ...), custom_call_target="tpu_custom_call" | custom-call | flops 2147483648 | bytes 10485760 | tf_op jit(solution)/shard_map/pallas_call | solution.py:287
  125.9 2.9 %collective-permute-start.26 = (bf16[256,512]{1,0:T(8,128)(2,1)S(1)}, bf16[256,512]{1,0:T(8,128)(2,1)S(1)}, u32[]{:S(2)}, u32[]{:S(2)}) collective-permute-start(bf16[256,512]{1,0:T(8,128)(2,1)S(1)} %get-tuple-element.62), channel_id=1, source_target_pairs={{0,3},{1,0},{2,1},{3,2},{4,7},{5,4},{6,5},{7,6},{8,11},{9,8},{10,9... | collective-permute-start | bytes 786440 | tf_op jit(solution)/shard_map/ppermute | solution.py:213
  128.7 0.8 collective-permute-start.27
  129.5 0.9 collective-permute-start.28
  130.4 3.3 %shard_map.52 = (f32[256,512]{1,0:T(8,128)S(1)}, bf16[256,512]{1,0:T(8,128)(2,1)S(1)}, bf16[256,512]{1,0:T(8,128)(2,1)S(1)}, bf16[256,512]{1,0:T(8,128)(2,1)S(1)}) custom-call(s32[4]{0:T(128)S(1)} %copy-done.10, f32[16,2048]{1,0:T(8,128)S(1)} %get-tuple-element.35.mc_ref, bf16[2048,2048]{1,0:T(8,128)(2,1)S(1)} %copy-done, ...), custom_call_target="tpu_custom_call" | custom-call | flops 2147483648 | bytes 10485760 | tf_op jit(solution)/shard_map/pallas_call | solution.py:287
  133.7 2.4 %collective-permute-start.17 = (bf16[256,512]{1,0:T(8,128)(2,1)S(1)}, bf16[256,512]{1,0:T(8,128)(2,1)S(1)}, u32[]{:S(2)}, u32[]{:S(2)}) collective-permute-start(bf16[256,512]{1,0:T(8,128)(2,1)S(1)} %get-tuple-element.54), channel_id=1, source_target_pairs={{0,3},{1,0},{2,1},{3,2},{4,7},{5,4},{6,5},{7,6},{8,11},{9,8},{10,9... | collective-permute-start | bytes 786440 | tf_op jit(solution)/shard_map/ppermute | solution.py:213
  136.1 1.5 collective-permute-start.18
  137.6 0.4 collective-permute-start.19
  138.0 1.5 collective-permute-done.27.refs_6_
  139.6 6.1 %collective-permute-done.28.refs_7_ = bf16[256,512]{1,0:T(8,128)(2,1)S(1)} collective-permute-done((bf16[256,512]{1,0:T(8,128)(2,1)S(1)}, bf16[256,512]{1,0:T(8,128)(2,1)S(1)}, u32[]{:S(2)}, u32[]{:S(2)}) %collective-permute-start.28) | collective-permute-done | bytes 262176 | tf_op jit(solution)/shard_map/ppermute | solution.py:213
  145.6 2.4 %collective-permute-done.17.refs_1_ = bf16[256,512]{1,0:T(8,128)(2,1)S(1)} collective-permute-done((bf16[256,512]{1,0:T(8,128)(2,1)S(1)}, bf16[256,512]{1,0:T(8,128)(2,1)S(1)}, u32[]{:S(2)}, u32[]{:S(2)}) %collective-permute-start.17) | collective-permute-done | bytes 262176 | tf_op jit(solution)/shard_map/ppermute | solution.py:213
  148.0 1.1 collective-permute-done.18.refs_2_
  149.0 2.6 %collective-permute-done.19.refs_3_ = bf16[256,512]{1,0:T(8,128)(2,1)S(1)} collective-permute-done((bf16[256,512]{1,0:T(8,128)(2,1)S(1)}, bf16[256,512]{1,0:T(8,128)(2,1)S(1)}, u32[]{:S(2)}, u32[]{:S(2)}) %collective-permute-start.19) | collective-permute-done | bytes 262176 | tf_op jit(solution)/shard_map/ppermute | solution.py:213
  151.6 1.6 shard_map.55
  (41 shorter events, 0.1 us)
Async XLA Ops:
  6.5 34.8 %copy-start.1 = (bf16[512,2048]{1,0:T(8,128)(2,1)S(1)}, bf16[512,2048]{1,0:T(8,128)(2,1)}, u32[]{:S(2)}) copy-start(bf16[512,2048]{1,0:T(8,128)(2,1)} %refs_3_.1) | copy-start | bytes 6291460
  6.5 34.8 %copy-start.11 = (s32[16,64]{1,0:T(8,128)S(1)}, s32[16,64]{1,0:T(8,128)}, u32[]{:S(2)}) copy-start(s32[16,64]{1,0:T(8,128)} %refs_1_.1) | copy-start | bytes 12292
  6.5 34.8 %copy-start.12 = (s32[16,64]{1,0:T(8,128)S(1)}, s32[16,64]{1,0:T(8,128)}, u32[]{:S(2)}) copy-start(s32[16,64]{1,0:T(8,128)} %refs_2_.1) | copy-start | bytes 12292
  6.5 70.1 %all-gather.2.cloned.1.call-start = ((), (), s32[]{:S(2)}) async-start(), calls=%async_computation.1 | async-start | bytes 8912896 | tf_op jit(solution)/shard_map/all_gather | solution.py:235
  8.6 36.7 %copy-start.2 = (bf16[128,2048]{1,0:T(8,128)(2,1)S(1)}, bf16[128,2048]{1,0:T(8,128)(2,1)}, u32[]{:S(2)}) copy-start(bf16[128,2048]{1,0:T(8,128)(2,1)} %constant_dynamic-slice_fusion.refs_0_) | copy-start | bytes 1572868
  8.6 17.5 %collective-permute-start.1 = (bf16[128,2048]{1,0:T(8,128)(2,1)}, bf16[128,2048]{1,0:T(8,128)(2,1)}, u32[]{:S(2)}, u32[]{:S(2)}) collective-permute-start(bf16[128,2048]{1,0:T(8,128)(2,1)} %constant_dynamic-slice_fusion.refs_0_), channel_id=1, source_target_pairs={{0,32},{16,48},{32,64},{48,80},{64,96},{80,112},{96,128},{112,144}... | collective-permute-start | bytes 1572872 | tf_op jit(solution)/shard_map/ppermute | solution.py:213
  10.6 15.9 %collective-permute-start.3 = (bf16[128,2048]{1,0:T(8,128)(2,1)}, bf16[128,2048]{1,0:T(8,128)(2,1)}, u32[]{:S(2)}, u32[]{:S(2)}) collective-permute-start(bf16[128,2048]{1,0:T(8,128)(2,1)} %constant_dynamic-slice_fusion.refs_0_), channel_id=1, source_target_pairs={{0,224},{16,240},{32,0},{48,16},{64,32},{80,48},{96,64},{112,80},{... | collective-permute-start | bytes 1572872 | tf_op jit(solution)/shard_map/ppermute | solution.py:213
  12.9 28.4 %all-to-all-start = ((bf16[64,16,128]{2,1,0:T(8,128)(2,1)}), bf16[64,16,128]{2,1,0:T(8,128)(2,1)S(1)}, u32[]{:S(2)}, u32[]{:S(2)}) async-start(bf16[64,16,128]{2,1,0:T(8,128)(2,1)} %broadcast_in_dim.3), calls=%async_computation | async-start | bytes 524288 | tf_op jit(solution)/shard_map/all_to_all | solution.py:227
  25.9 19.4 %collective-permute-start = (bf16[128,2048]{1,0:T(8,128)(2,1)}, bf16[128,2048]{1,0:T(8,128)(2,1)}, u32[]{:S(2)}, u32[]{:S(2)}) collective-permute-start(bf16[128,2048]{1,0:T(8,128)(2,1)} %constant_dynamic-slice_fusion.refs_0_), channel_id=1, source_target_pairs={{0,16},{16,0},{32,48},{48,32},{64,80},{80,64},{96,112},{112,96},{1... | collective-permute-start | bytes 1572872 | tf_op jit(solution)/shard_map/ppermute | solution.py:217
  26.1 19.1 %collective-permute-start.2 = (bf16[128,2048]{1,0:T(8,128)(2,1)}, bf16[128,2048]{1,0:T(8,128)(2,1)}, u32[]{:S(2)}, u32[]{:S(2)}) collective-permute-start(bf16[128,2048]{1,0:T(8,128)(2,1)} %collective-permute-done.1.refs_2_), channel_id=1, source_target_pairs={{0,16},{16,0},{32,48},{48,32},{64,80},{80,64},{96,112},{112,96},{1... | collective-permute-start | bytes 1572872 | tf_op jit(solution)/shard_map/ppermute | solution.py:217
  26.5 18.8 %collective-permute-start.4 = (bf16[128,2048]{1,0:T(8,128)(2,1)}, bf16[128,2048]{1,0:T(8,128)(2,1)}, u32[]{:S(2)}, u32[]{:S(2)}) collective-permute-start(bf16[128,2048]{1,0:T(8,128)(2,1)} %collective-permute-done.3.refs_4_), channel_id=1, source_target_pairs={{0,16},{16,0},{32,48},{48,32},{64,80},{80,64},{96,112},{112,96},{1... | collective-permute-start | bytes 1572872 | tf_op jit(solution)/shard_map/ppermute | solution.py:217
  26.7 36.9 %copy-start.9 = (s32[4]{0:T(128)}, s32[4]{0:T(128)S(1)}, u32[]{:S(2)}) copy-start(s32[4]{0:T(128)S(1)} %pad_add_fusion.s_ref) | copy-start | bytes 52
  44.4 0.8 copy-start.4
  45.2 4.7 %copy-start.3 = (bf16[512,2048]{1,0:T(8,128)(2,1)}, bf16[512,2048]{1,0:T(8,128)(2,1)S(1)}, u32[]{:S(2)}) copy-start(bf16[512,2048]{1,0:T(8,128)(2,1)S(1)} %get-tuple-element.38.left_ref) | copy-start | bytes 6291460
  45.2 4.7 %copy-start.6 = (f32[64,2048]{1,0:T(8,128)}, f32[64,2048]{1,0:T(8,128)S(1)}, u32[]{:S(2)}) copy-start(f32[64,2048]{1,0:T(8,128)S(1)} %get-tuple-element.39.mt_ref) | copy-start | bytes 1572868
  49.9 7.9 %collective-permute-start.5 = (bf16[128,768]{1,0:T(8,128)(2,1)S(1)}, bf16[128,768]{1,0:T(8,128)(2,1)S(1)}, u32[]{:S(2)}, u32[]{:S(2)}) collective-permute-start(bf16[128,768]{1,0:T(8,128)(2,1)S(1)} %get-tuple-element.41), channel_id=1, source_target_pairs={{0,12},{4,0},{8,4},{12,8},{1,13},{5,1},{9,5},{13,9},{2,14},{6,2},{... | collective-permute-start | bytes 589832 | tf_op jit(solution)/shard_map/ppermute | solution.py:213
  51.3 9.3 %collective-permute-start.6 = (bf16[128,768]{1,0:T(8,128)(2,1)S(1)}, bf16[128,768]{1,0:T(8,128)(2,1)S(1)}, u32[]{:S(2)}, u32[]{:S(2)}) collective-permute-start(bf16[128,768]{1,0:T(8,128)(2,1)S(1)} %get-tuple-element.42), channel_id=1, source_target_pairs={{0,8},{4,12},{8,0},{12,4},{1,9},{5,13},{9,1},{13,5},{2,10},{6,14},... | collective-permute-start | bytes 589832 | tf_op jit(solution)/shard_map/ppermute | solution.py:213
  52.6 11.0 %collective-permute-start.7 = (bf16[128,768]{1,0:T(8,128)(2,1)S(1)}, bf16[128,768]{1,0:T(8,128)(2,1)S(1)}, u32[]{:S(2)}, u32[]{:S(2)}) collective-permute-start(bf16[128,768]{1,0:T(8,128)(2,1)S(1)} %get-tuple-element.43), channel_id=1, source_target_pairs={{0,4},{4,8},{8,12},{12,0},{1,5},{5,9},{9,13},{13,1},{2,6},{6,10},{... | collective-permute-start | bytes 589832 | tf_op jit(solution)/shard_map/ppermute | solution.py:213
  64.3 37.5 %copy-start.10 = (s32[4]{0:T(128)S(1)}, s32[4]{0:T(128)}, u32[]{:S(2)}) copy-start(s32[4]{0:T(128)} %copy-done.9) | copy-start | bytes 52
  64.3 42.9 %copy-start.5 = (f32[64,2048]{1,0:T(8,128)S(1)}, f32[64,2048]{1,0:T(8,128)}, u32[]{:S(2)}) copy-start(f32[64,2048]{1,0:T(8,128)} %copy-done.4) | copy-start | bytes 1572868
  64.3 12.3 %collective-permute-start.10 = (bf16[128,768]{1,0:T(8,128)(2,1)S(1)}, bf16[128,768]{1,0:T(8,128)(2,1)S(1)}, u32[]{:S(2)}, u32[]{:S(2)}) collective-permute-start(bf16[128,768]{1,0:T(8,128)(2,1)S(1)} %shard_map.48.refs_0_), channel_id=1, source_target_pairs={{0,4},{4,8},{8,12},{12,0},{1,5},{5,9},{9,13},{13,1},{2,6},{6,10},{... | collective-permute-start | bytes 589832 | tf_op jit(solution)/shard_map/ppermute | solution.py:213
  64.4 12.2 %collective-permute-start.8 = (bf16[128,768]{1,0:T(8,128)(2,1)S(1)}, bf16[128,768]{1,0:T(8,128)(2,1)S(1)}, u32[]{:S(2)}, u32[]{:S(2)}) collective-permute-start(bf16[128,768]{1,0:T(8,128)(2,1)S(1)} %shard_map.48.refs_0_), channel_id=1, source_target_pairs={{0,12},{4,0},{8,4},{12,8},{1,13},{5,1},{9,5},{13,9},{2,14},{6,2},{... | collective-permute-start | bytes 589832 | tf_op jit(solution)/shard_map/ppermute | solution.py:213
  67.6 9.0 %collective-permute-start.9 = (bf16[128,768]{1,0:T(8,128)(2,1)S(1)}, bf16[128,768]{1,0:T(8,128)(2,1)S(1)}, u32[]{:S(2)}, u32[]{:S(2)}) collective-permute-start(bf16[128,768]{1,0:T(8,128)(2,1)S(1)} %shard_map.48.refs_0_), channel_id=1, source_target_pairs={{0,8},{4,12},{8,0},{12,4},{1,9},{5,13},{9,1},{13,5},{2,10},{6,14},... | collective-permute-start | bytes 589832 | tf_op jit(solution)/shard_map/ppermute | solution.py:213
  86.6 11.1 %collective-permute-start.20 = (bf16[64,1280]{1,0:T(8,128)(2,1)}, bf16[64,1280]{1,0:T(8,128)(2,1)S(1)}, u32[]{:S(2)}, u32[]{:S(2)}) collective-permute-start(bf16[64,1280]{1,0:T(8,128)(2,1)} %get-tuple-element.58), channel_id=1, source_target_pairs={{0,12},{4,0},{8,4},{12,8},{1,13},{5,1},{9,5},{13,9},{2,14},{6,2},{... | collective-permute-start | bytes 491528 | tf_op jit(solution)/shard_map/ppermute | solution.py:213
  89.7 8.9 %collective-permute-start.21 = (bf16[64,1280]{1,0:T(8,128)(2,1)}, bf16[64,1280]{1,0:T(8,128)(2,1)S(1)}, u32[]{:S(2)}, u32[]{:S(2)}) collective-permute-start(bf16[64,1280]{1,0:T(8,128)(2,1)} %get-tuple-element.59), channel_id=1, source_target_pairs={{0,8},{4,12},{8,0},{12,4},{1,9},{5,13},{9,1},{13,5},{2,10},{6,14},... | collective-permute-start | bytes 491528 | tf_op jit(solution)/shard_map/ppermute | solution.py:213
  89.7 12.1 %collective-permute-start.22 = (bf16[64,1280]{1,0:T(8,128)(2,1)}, bf16[64,1280]{1,0:T(8,128)(2,1)S(1)}, u32[]{:S(2)}, u32[]{:S(2)}) collective-permute-start(bf16[64,1280]{1,0:T(8,128)(2,1)} %get-tuple-element.60), channel_id=1, source_target_pairs={{0,4},{4,8},{8,12},{12,0},{1,5},{5,9},{9,13},{13,1},{2,6},{6,10},{... | collective-permute-start | bytes 491528 | tf_op jit(solution)/shard_map/ppermute | solution.py:213
  90.6 15.3 %collective-permute-start.11 = (bf16[64,1280]{1,0:T(8,128)(2,1)}, bf16[64,1280]{1,0:T(8,128)(2,1)S(1)}, u32[]{:S(2)}, u32[]{:S(2)}) collective-permute-start(bf16[64,1280]{1,0:T(8,128)(2,1)} %get-tuple-element.50), channel_id=1, source_target_pairs={{0,12},{4,0},{8,4},{12,8},{1,13},{5,1},{9,5},{13,9},{2,14},{6,2},{... | collective-permute-start | bytes 491528 | tf_op jit(solution)/shard_map/ppermute | solution.py:213
  92.9 21.8 %collective-permute-start.12 = (bf16[64,1280]{1,0:T(8,128)(2,1)}, bf16[64,1280]{1,0:T(8,128)(2,1)S(1)}, u32[]{:S(2)}, u32[]{:S(2)}) collective-permute-start(bf16[64,1280]{1,0:T(8,128)(2,1)} %get-tuple-element.51), channel_id=1, source_target_pairs={{0,8},{4,12},{8,0},{12,4},{1,9},{5,13},{9,1},{13,5},{2,10},{6,14},... | collective-permute-start | bytes 491528 | tf_op jit(solution)/shard_map/ppermute | solution.py:213
  97.7 17.0 %collective-permute-start.13 = (bf16[64,1280]{1,0:T(8,128)(2,1)}, bf16[64,1280]{1,0:T(8,128)(2,1)S(1)}, u32[]{:S(2)}, u32[]{:S(2)}) collective-permute-start(bf16[64,1280]{1,0:T(8,128)(2,1)} %get-tuple-element.52), channel_id=1, source_target_pairs={{0,4},{4,8},{8,12},{12,0},{1,5},{5,9},{9,13},{13,1},{2,6},{6,10},{... | collective-permute-start | bytes 491528 | tf_op jit(solution)/shard_map/ppermute | solution.py:213
  101.7 1.0 copy-start.8
  103.3 14.7 %collective-permute-start.23 = (bf16[64,1280]{1,0:T(8,128)(2,1)S(1)}, bf16[64,1280]{1,0:T(8,128)(2,1)S(1)}, u32[]{:S(2)}, u32[]{:S(2)}) collective-permute-start(bf16[64,1280]{1,0:T(8,128)(2,1)S(1)} %shard_map.53.refs_4_), channel_id=1, source_target_pairs={{0,12},{4,0},{8,4},{12,8},{1,13},{5,1},{9,5},{13,9},{2,14},{6,2},{... | collective-permute-start | bytes 491528 | tf_op jit(solution)/shard_map/ppermute | solution.py:213
  104.3 14.9 %collective-permute-start.24 = (bf16[64,1280]{1,0:T(8,128)(2,1)S(1)}, bf16[64,1280]{1,0:T(8,128)(2,1)S(1)}, u32[]{:S(2)}, u32[]{:S(2)}) collective-permute-start(bf16[64,1280]{1,0:T(8,128)(2,1)S(1)} %shard_map.53.refs_4_), channel_id=1, source_target_pairs={{0,8},{4,12},{8,0},{12,4},{1,9},{5,13},{9,1},{13,5},{2,10},{6,14},... | collective-permute-start | bytes 491528 | tf_op jit(solution)/shard_map/ppermute | solution.py:213
  105.9 13.3 %collective-permute-start.25 = (bf16[64,1280]{1,0:T(8,128)(2,1)S(1)}, bf16[64,1280]{1,0:T(8,128)(2,1)S(1)}, u32[]{:S(2)}, u32[]{:S(2)}) collective-permute-start(bf16[64,1280]{1,0:T(8,128)(2,1)S(1)} %shard_map.53.refs_4_), channel_id=1, source_target_pairs={{0,4},{4,8},{8,12},{12,0},{1,5},{5,9},{9,13},{13,1},{2,6},{6,10},{... | collective-permute-start | bytes 491528 | tf_op jit(solution)/shard_map/ppermute | solution.py:213
  107.2 7.5 %copy-start.7 = (f32[64,1280]{1,0:T(8,128)S(1)}, f32[64,1280]{1,0:T(8,128)}, u32[]{:S(2)}) copy-start(f32[64,1280]{1,0:T(8,128)} %get-tuple-element.49.own_ref) | copy-start | bytes 983044
  115.3 14.2 %collective-permute-start.14 = (bf16[64,1280]{1,0:T(8,128)(2,1)S(1)}, bf16[64,1280]{1,0:T(8,128)(2,1)S(1)}, u32[]{:S(2)}, u32[]{:S(2)}) collective-permute-start(bf16[64,1280]{1,0:T(8,128)(2,1)S(1)} %shard_map.51.refs_4_), channel_id=1, source_target_pairs={{0,12},{4,0},{8,4},{12,8},{1,13},{5,1},{9,5},{13,9},{2,14},{6,2},{... | collective-permute-start | bytes 491528 | tf_op jit(solution)/shard_map/ppermute | solution.py:213
  117.3 13.1 %collective-permute-start.15 = (bf16[64,1280]{1,0:T(8,128)(2,1)S(1)}, bf16[64,1280]{1,0:T(8,128)(2,1)S(1)}, u32[]{:S(2)}, u32[]{:S(2)}) collective-permute-start(bf16[64,1280]{1,0:T(8,128)(2,1)S(1)} %shard_map.51.refs_4_), channel_id=1, source_target_pairs={{0,8},{4,12},{8,0},{12,4},{1,9},{5,13},{9,1},{13,5},{2,10},{6,14},... | collective-permute-start | bytes 491528 | tf_op jit(solution)/shard_map/ppermute | solution.py:213
  118.1 12.3 %collective-permute-start.16 = (bf16[64,1280]{1,0:T(8,128)(2,1)S(1)}, bf16[64,1280]{1,0:T(8,128)(2,1)S(1)}, u32[]{:S(2)}, u32[]{:S(2)}) collective-permute-start(bf16[64,1280]{1,0:T(8,128)(2,1)S(1)} %shard_map.51.refs_4_), channel_id=1, source_target_pairs={{0,4},{4,8},{8,12},{12,0},{1,5},{5,9},{9,13},{13,1},{2,6},{6,10},{... | collective-permute-start | bytes 491528 | tf_op jit(solution)/shard_map/ppermute | solution.py:213
  119.2 3.4 %copy-start = (bf16[2048,2048]{1,0:T(8,128)(2,1)S(1)}, bf16[2048,2048]{1,0:T(8,128)(2,1)}, u32[]{:S(2)}) copy-start(bf16[2048,2048]{1,0:T(8,128)(2,1)} %shard_map.49.right_ref) | copy-start | bytes 25165828
  125.9 11.8 %collective-permute-start.26 = (bf16[256,512]{1,0:T(8,128)(2,1)S(1)}, bf16[256,512]{1,0:T(8,128)(2,1)S(1)}, u32[]{:S(2)}, u32[]{:S(2)}) collective-permute-start(bf16[256,512]{1,0:T(8,128)(2,1)S(1)} %get-tuple-element.62), channel_id=1, source_target_pairs={{0,3},{1,0},{2,1},{3,2},{4,7},{5,4},{6,5},{7,6},{8,11},{9,8},{10,9... | collective-permute-start | bytes 786440 | tf_op jit(solution)/shard_map/ppermute | solution.py:213
  128.7 10.9 %collective-permute-start.27 = (bf16[256,512]{1,0:T(8,128)(2,1)S(1)}, bf16[256,512]{1,0:T(8,128)(2,1)S(1)}, u32[]{:S(2)}, u32[]{:S(2)}) collective-permute-start(bf16[256,512]{1,0:T(8,128)(2,1)S(1)} %get-tuple-element.63), channel_id=1, source_target_pairs={{0,2},{1,3},{2,0},{3,1},{4,6},{5,7},{6,4},{7,5},{8,10},{9,11},{10,... | collective-permute-start | bytes 786440 | tf_op jit(solution)/shard_map/ppermute | solution.py:213
  129.5 16.1 %collective-permute-start.28 = (bf16[256,512]{1,0:T(8,128)(2,1)S(1)}, bf16[256,512]{1,0:T(8,128)(2,1)S(1)}, u32[]{:S(2)}, u32[]{:S(2)}) collective-permute-start(bf16[256,512]{1,0:T(8,128)(2,1)S(1)} %get-tuple-element.64), channel_id=1, source_target_pairs={{0,1},{1,2},{2,3},{3,0},{4,5},{5,6},{6,7},{7,4},{8,9},{9,10},{10,1... | collective-permute-start | bytes 786440 | tf_op jit(solution)/shard_map/ppermute | solution.py:213
  133.7 14.3 %collective-permute-start.17 = (bf16[256,512]{1,0:T(8,128)(2,1)S(1)}, bf16[256,512]{1,0:T(8,128)(2,1)S(1)}, u32[]{:S(2)}, u32[]{:S(2)}) collective-permute-start(bf16[256,512]{1,0:T(8,128)(2,1)S(1)} %get-tuple-element.54), channel_id=1, source_target_pairs={{0,3},{1,0},{2,1},{3,2},{4,7},{5,4},{6,5},{7,6},{8,11},{9,8},{10,9... | collective-permute-start | bytes 786440 | tf_op jit(solution)/shard_map/ppermute | solution.py:213
  136.1 12.9 %collective-permute-start.18 = (bf16[256,512]{1,0:T(8,128)(2,1)S(1)}, bf16[256,512]{1,0:T(8,128)(2,1)S(1)}, u32[]{:S(2)}, u32[]{:S(2)}) collective-permute-start(bf16[256,512]{1,0:T(8,128)(2,1)S(1)} %get-tuple-element.55), channel_id=1, source_target_pairs={{0,2},{1,3},{2,0},{3,1},{4,6},{5,7},{6,4},{7,5},{8,10},{9,11},{10,... | collective-permute-start | bytes 786440 | tf_op jit(solution)/shard_map/ppermute | solution.py:213
  137.6 14.0 %collective-permute-start.19 = (bf16[256,512]{1,0:T(8,128)(2,1)S(1)}, bf16[256,512]{1,0:T(8,128)(2,1)S(1)}, u32[]{:S(2)}, u32[]{:S(2)}) collective-permute-start(bf16[256,512]{1,0:T(8,128)(2,1)S(1)} %get-tuple-element.56), channel_id=1, source_target_pairs={{0,1},{1,2},{2,3},{3,0},{4,5},{5,6},{6,7},{7,4},{8,9},{9,10},{10,1... | collective-permute-start | bytes 786440 | tf_op jit(solution)/shard_map/ppermute | solution.py:213
Sparse Core Ops, SparseCore 0:
  9.2 62.2 all-gather.1

commit v4 on v1

--- a/solution.py
+++ b/solution.py
@@ -134,7 +134,8 @@
                 out[:, pl.ds(start, 256)] = block[row : row + height].astype(out.dtype)
 
 
-def square_kernel(first_slot, first_block, s_ref, ms_ref, own_ref, a_ref, b_ref, c_ref, out_ref):
+def square_kernel(first_slot, first_block, s_ref, ms_ref, own_ref, a_ref, b_ref, c_ref, *refs):
+    out_ref = refs[-1]
     height, width = out_ref.shape
     total = own_ref[...] + a_ref[...].astype(F32) + b_ref[...].astype(F32) + c_ref[...].astype(F32)
     for block in range(height // BLK):
@@ -251,9 +252,9 @@
             mine = call(
                 functools.partial(square_kernel, slots[0], half * (4 // halves)),
                 shape(height, width),
-                6,
+                8 if halves == 1 else 6,
                 byts=2 * height * width * 6,
-            )(where, ms, mine, *exchange(others, "col"))
+            )(where, ms, mine, *exchange(others, "col"), *((left, mt) if halves == 1 else ()))
             squares.append((mine, *exchange([mine] * 3, "col")))
         return squares
 

time: 153 us -> 152 us (level)
  no operation moved by 1% of the time
where the time goes in v4:
time: 152 us; the launch traced here: 151 us
  waiting for transfers between devices  59.2 us (39%)
  starting transfers between devices  46.3 us (30%)
  Pallas kernels  21.5 us (14%)
  between operations  13.6 us (9%)
  local copies, waits for them, and re-layouts  9.06 us (6%)
  other arithmetic  1.56 us (1%)
    ppermute x26, waiting for transfers between devices, shift(): lax.ppermute(array, axis, [(i, (i + step) % size) for i in range(size)])  44.5 us
    ppermute x26, starting transfers between devices, shift(): lax.ppermute(array, axis, [(i, (i + step) % size) for i in range(size)])  32.6 us
    all_to_all x1, waiting for transfers between devices, gather_patterns(): lax.all_to_all(jnp.broadcast_to(both, (64, 16, 128)), ('row', 'col'), 0, 0)  14.7 us
    all_to_all x1, starting transfers between devices, gather_patterns(): lax.all_to_all(jnp.broadcast_to(both, (64, 16, 128)), ('row', 'col'), 0, 0)  13 us
    pallas_call x2, Pallas kernels, start(): call(functools.partial(product_one_kernel, slots, halves, len(held)), ((s...  7.23 us
    pallas_call x2, Pallas kernels, body(): call(functools.partial(product_two_kernel, half, len(first)), (shape(heig...  6.5 us
    unnamed x22, local copies, waits for them, and re-layouts  6.41 us
    pallas_call x1, Pallas kernels, body(): call(prep_kernel, (shape(512, 2048), shape(64, 2048, dtype=F32), shape(64...  3.07 us
  transfers between devices with their start and end apart: 31, of which 15 were waited for; matrix products, arithmetic and copies ran while one was open for 2% of the time, Pallas kernels for 11%

profile of v4, /device:TPU:32, one launch (start us, length us, event | category | flops | bytes accessed | tf_op | source)
XLA Modules:
  0.0 151.2 jit_solution(18076351815342168022)
XLA Ops:
  6.5 1.9 %constant_dynamic-slice_fusion.refs_0_ = bf16[128,2048]{1,0:T(8,128)(2,1)} fusion(bf16[512,2048]{1,0:T(8,128)(2,1)} %refs_3_.1, s32[]{:T(128)S(6)} %select_n.16), kind=kLoop, calls=%fused_computation.2 | loop fusion | bytes 1048580 | tf_op jit(solution)/shard_map/dynamic_slice | solution.py:218
  8.5 0.0 all-gather.2.cloned.1.call-update
  8.5 2.0 %collective-permute-start.1 = (bf16[128,2048]{1,0:T(8,128)(2,1)}, bf16[128,2048]{1,0:T(8,128)(2,1)}, u32[]{:S(2)}, u32[]{:S(2)}) collective-permute-start(bf16[128,2048]{1,0:T(8,128)(2,1)} %constant_dynamic-slice_fusion.refs_0_), channel_id=1, source_target_pairs={{0,32},{16,48},{32,64},{48,80},{64,96},{80,112},{96,128},{112,144}... | collective-permute-start | bytes 1572872 | tf_op jit(solution)/shard_map/ppermute | solution.py:198
  10.5 0.1 collective-permute-start.3
  10.6 0.7 convert.6
  11.3 0.7 convert.7
  12.0 0.1 pad_maximum_fusion
  12.1 0.7 broadcast_in_dim.3
  12.8 13.0 %all-to-all-start = ((bf16[64,16,128]{2,1,0:T(8,128)(2,1)}), bf16[64,16,128]{2,1,0:T(8,128)(2,1)S(1)}, u32[]{:S(2)}, u32[]{:S(2)}) async-start(bf16[64,16,128]{2,1,0:T(8,128)(2,1)} %broadcast_in_dim.3), calls=%async_computation | async-start | bytes 524288 | tf_op jit(solution)/shard_map/all_to_all | solution.py:212
  25.8 0.2 collective-permute-start
  26.0 0.4 collective-permute-start.2
  26.4 0.1 collective-permute-start.4
  26.5 0.1 pad_add_fusion.s_ref
  26.6 14.7 %all-to-all-done.refs_0_ = bf16[64,16,128]{2,1,0:T(8,128)(2,1)S(1)} async-done(((bf16[64,16,128]{2,1,0:T(8,128)(2,1)}), bf16[64,16,128]{2,1,0:T(8,128)(2,1)S(1)}, u32[]{:S(2)}, u32[]{:S(2)}) %all-to-all-start) | async-done | bytes 262176 | tf_op jit(solution)/shard_map/all_to_all | solution.py:212
  41.3 1.6 %copy-done.1 = bf16[512,2048]{1,0:T(8,128)(2,1)S(1)} copy-done((bf16[512,2048]{1,0:T(8,128)(2,1)S(1)}, bf16[512,2048]{1,0:T(8,128)(2,1)}, u32[]{:S(2)}) %copy-start.1) | copy-done | bytes 2097176
  43.0 0.7 copy-done.10
  43.6 3.1 %shard_map.46 = (bf16[512,2048]{1,0:T(8,128)(2,1)S(1)}, f32[64,2048]{1,0:T(8,128)S(1)}, f32[64,2048]{1,0:T(8,128)S(1)}, f32[16,2048]{1,0:T(8,128)S(1)}, f32[16,2048]{1,0:T(8,128)S(1)}) custom-call(s32[4]{0:T(128)S(1)} %pad_add_fusion.s_ref, bf16[64,16,128]{2,1,0:T(8,128)(2,1)S(1)} %all-to-all-done.refs_0_, s32[16,64]{1,0:T(8,128)S(1)} %copy-done.9, ...), custom_call_target="tpu_custom_call" | custom-call | flops 209715200 | bytes 6291456 | tf_op jit(solution)/shard_map/pallas_call | solution.py:225
  46.7 0.0 copy-start.7
  46.8 3.8 %shard_map.47 = (f32[128,768]{1,0:T(8,128)S(1)}, bf16[128,768]{1,0:T(8,128)(2,1)S(1)}, bf16[128,768]{1,0:T(8,128)(2,1)S(1)}, bf16[128,768]{1,0:T(8,128)(2,1)S(1)}) custom-call(s32[4]{0:T(128)S(1)} %pad_add_fusion.s_ref, bf16[512,2048]{1,0:T(8,128)(2,1)S(1)} %get-tuple-element.38.left_ref.refs_0_, f32[64,2048]{1,0:T(8,128)S(1)} %get-tuple-element.39.mt_ref.refs_1_, ...), custom_call_target="tpu_custom_call" | custom-call | flops 1610612736 | bytes 5242880 | tf_op jit(solution)/shard_map/pallas_call | solution.py:241
  50.6 1.3 collective-permute-start.5
  51.9 1.4 collective-permute-start.6
  53.3 0.5 collective-permute-start.7
  53.8 4.7 %collective-permute-done.5.a_ref = bf16[128,768]{1,0:T(8,128)(2,1)S(1)} collective-permute-done((bf16[128,768]{1,0:T(8,128)(2,1)S(1)}, bf16[128,768]{1,0:T(8,128)(2,1)S(1)}, u32[]{:S(2)}, u32[]{:S(2)}) %collective-permute-start.5) | collective-permute-done | bytes 196640 | tf_op jit(solution)/shard_map/ppermute | solution.py:198
  58.5 2.8 %collective-permute-done.6.b_ref = bf16[128,768]{1,0:T(8,128)(2,1)S(1)} collective-permute-done((bf16[128,768]{1,0:T(8,128)(2,1)S(1)}, bf16[128,768]{1,0:T(8,128)(2,1)S(1)}, u32[]{:S(2)}, u32[]{:S(2)}) %collective-permute-start.6) | collective-permute-done | bytes 196640 | tf_op jit(solution)/shard_map/ppermute | solution.py:198
  61.3 2.6 %collective-permute-done.7.c_ref = bf16[128,768]{1,0:T(8,128)(2,1)S(1)} collective-permute-done((bf16[128,768]{1,0:T(8,128)(2,1)S(1)}, bf16[128,768]{1,0:T(8,128)(2,1)S(1)}, u32[]{:S(2)}, u32[]{:S(2)}) %collective-permute-start.7) | collective-permute-done | bytes 196640 | tf_op jit(solution)/shard_map/ppermute | solution.py:198
  63.9 0.7 shard_map.48.refs_0_
  64.5 0.2 collective-permute-start.10
  64.7 3.1 %collective-permute-start.8 = (bf16[128,768]{1,0:T(8,128)(2,1)S(1)}, bf16[128,768]{1,0:T(8,128)(2,1)S(1)}, u32[]{:S(2)}, u32[]{:S(2)}) collective-permute-start(bf16[128,768]{1,0:T(8,128)(2,1)S(1)} %shard_map.48.refs_0_), channel_id=1, source_target_pairs={{0,12},{4,0},{8,4},{12,8},{1,13},{5,1},{9,5},{13,9},{2,14},{6,2},{... | collective-permute-start | bytes 589832 | tf_op jit(solution)/shard_map/ppermute | solution.py:198
  67.9 0.4 collective-permute-start.9
  68.2 8.7 %collective-permute-done.10.refs_3_ = bf16[128,768]{1,0:T(8,128)(2,1)S(1)} collective-permute-done((bf16[128,768]{1,0:T(8,128)(2,1)S(1)}, bf16[128,768]{1,0:T(8,128)(2,1)S(1)}, u32[]{:S(2)}, u32[]{:S(2)}) %collective-permute-start.10) | collective-permute-done | bytes 196640 | tf_op jit(solution)/shard_map/ppermute | solution.py:198
  76.9 0.7 copy-done.3
  77.6 3.4 %copy-done = bf16[2048,2048]{1,0:T(8,128)(2,1)S(1)} copy-done((bf16[2048,2048]{1,0:T(8,128)(2,1)S(1)}, bf16[2048,2048]{1,0:T(8,128)(2,1)}, u32[]{:S(2)}) %copy-start) | copy-done | bytes 8388632
  81.0 3.5 %shard_map.50 = (f32[64,1280]{1,0:T(8,128)S(1)}, bf16[64,1280]{1,0:T(8,128)(2,1)S(1)}, bf16[64,1280]{1,0:T(8,128)(2,1)S(1)}, bf16[64,1280]{1,0:T(8,128)(2,1)S(1)...) custom-call(s32[4]{0:T(128)S(1)} %pad_add_fusion.s_ref, ...), custom_call_target="tpu_custom_call" | custom-call | flops 2684354560 | bytes 7340032 | tf_op jit(solution)/shard_map/pallas_call | solution.py:241
  84.4 3.0 %collective-permute-start.20 = (bf16[64,1280]{1,0:T(8,128)(2,1)S(1)}, bf16[64,1280]{1,0:T(8,128)(2,1)S(1)}, u32[]{:S(2)}, u32[]{:S(2)}) collective-permute-start(bf16[64,1280]{1,0:T(8,128)(2,1)S(1)} %get-tuple-element.58), channel_id=1, source_target_pairs={{0,12},{4,0},{8,4},{12,8},{1,13},{5,1},{9,5},{13,9},{2,14},{6,2},{... | collective-permute-start | bytes 491528 | tf_op jit(solution)/shard_map/ppermute | solution.py:198
  87.5 1.0 collective-permute-start.22
  88.4 2.3 %collective-permute-start.11 = (bf16[64,1280]{1,0:T(8,128)(2,1)S(1)}, bf16[64,1280]{1,0:T(8,128)(2,1)S(1)}, u32[]{:S(2)}, u32[]{:S(2)}) collective-permute-start(bf16[64,1280]{1,0:T(8,128)(2,1)S(1)} %get-tuple-element.50), channel_id=1, source_target_pairs={{0,12},{4,0},{8,4},{12,8},{1,13},{5,1},{9,5},{13,9},{2,14},{6,2},{... | collective-permute-start | bytes 491528 | tf_op jit(solution)/shard_map/ppermute | solution.py:198
  90.7 2.3 %collective-permute-start.12 = (bf16[64,1280]{1,0:T(8,128)(2,1)S(1)}, bf16[64,1280]{1,0:T(8,128)(2,1)S(1)}, u32[]{:S(2)}, u32[]{:S(2)}) collective-permute-start(bf16[64,1280]{1,0:T(8,128)(2,1)S(1)} %get-tuple-element.51), channel_id=1, source_target_pairs={{0,8},{4,12},{8,0},{12,4},{1,9},{5,13},{9,1},{13,5},{2,10},{6,14},... | collective-permute-start | bytes 491528 | tf_op jit(solution)/shard_map/ppermute | solution.py:198
  93.0 2.2 %collective-permute-done.20.a_ref = bf16[64,1280]{1,0:T(8,128)(2,1)S(1)} collective-permute-done((bf16[64,1280]{1,0:T(8,128)(2,1)S(1)}, bf16[64,1280]{1,0:T(8,128)(2,1)S(1)}, u32[]{:S(2)}, u32[]{:S(2)}) %collective-permute-start.20) | collective-permute-done | bytes 163872 | tf_op jit(solution)/shard_map/ppermute | solution.py:198
  95.2 0.9 collective-permute-done.21.b_ref
  96.1 3.2 %collective-permute-done.22.c_ref = bf16[64,1280]{1,0:T(8,128)(2,1)S(1)} collective-permute-done((bf16[64,1280]{1,0:T(8,128)(2,1)S(1)}, bf16[64,1280]{1,0:T(8,128)(2,1)S(1)}, u32[]{:S(2)}, u32[]{:S(2)}) %collective-permute-start.22) | collective-permute-done | bytes 163872 | tf_op jit(solution)/shard_map/ppermute | solution.py:198
  99.3 0.6 shard_map.53.refs_4_
  99.9 0.9 collective-permute-start.23
  100.9 1.6 %collective-permute-start.24 = (bf16[64,1280]{1,0:T(8,128)(2,1)S(1)}, bf16[64,1280]{1,0:T(8,128)(2,1)S(1)}, u32[]{:S(2)}, u32[]{:S(2)}) collective-permute-start(bf16[64,1280]{1,0:T(8,128)(2,1)S(1)} %shard_map.53.refs_4_), channel_id=1, source_target_pairs={{0,8},{4,12},{8,0},{12,4},{1,9},{5,13},{9,1},{13,5},{2,10},{6,14},... | collective-permute-start | bytes 491528 | tf_op jit(solution)/shard_map/ppermute | solution.py:198
  102.5 1.3 collective-permute-start.25
  103.8 1.3 shard_map.49.right_ref
  105.1 1.8 %collective-permute-done.13.c_ref = bf16[64,1280]{1,0:T(8,128)(2,1)S(1)} collective-permute-done((bf16[64,1280]{1,0:T(8,128)(2,1)S(1)}, bf16[64,1280]{1,0:T(8,128)(2,1)S(1)}, u32[]{:S(2)}, u32[]{:S(2)}) %collective-permute-start.13) | collective-permute-done | bytes 163872 | tf_op jit(solution)/shard_map/ppermute | solution.py:198
  106.9 0.6 shard_map.51.refs_4_
  107.5 0.2 collective-permute-start.14
  107.7 1.0 collective-permute-start.15
  108.8 1.3 collective-permute-start.16
  110.1 4.3 %collective-permute-done.25.refs_7_ = bf16[64,1280]{1,0:T(8,128)(2,1)S(1)} collective-permute-done((bf16[64,1280]{1,0:T(8,128)(2,1)S(1)}, bf16[64,1280]{1,0:T(8,128)(2,1)S(1)}, u32[]{:S(2)}, u32[]{:S(2)}) %collective-permute-start.25) | collective-permute-done | bytes 163872 | tf_op jit(solution)/shard_map/ppermute | solution.py:198
  114.4 3.2 %shard_map.54 = (f32[256,512]{1,0:T(8,128)S(1)}, bf16[256,512]{1,0:T(8,128)(2,1)S(1)}, bf16[256,512]{1,0:T(8,128)(2,1)S(1)}, bf16[256,512]{1,0:T(8,128)(2,1)S(1)}) custom-call(s32[4]{0:T(128)S(1)} %pad_add_fusion.s_ref, f32[16,2048]{1,0:T(8,128)S(1)} %copy-done.6, bf16[2048,2048]{1,0:T(8,128)(2,1)S(1)} %shard_map.49.right_ref, ...), custom_call_target="tpu_custom_call" | custom-call | flops 2147483648 | bytes 10485760 | tf_op jit(solution)/shard_map/pallas_call | solution.py:268
  117.7 3.0 %collective-permute-start.26 = (bf16[256,512]{1,0:T(8,128)(2,1)S(1)}, bf16[256,512]{1,0:T(8,128)(2,1)S(1)}, u32[]{:S(2)}, u32[]{:S(2)}) collective-permute-start(bf16[256,512]{1,0:T(8,128)(2,1)S(1)} %get-tuple-element.62), channel_id=1, source_target_pairs={{0,3},{1,0},{2,1},{3,2},{4,7},{5,4},{6,5},{7,6},{8,11},{9,8},{10,9... | collective-permute-start | bytes 786440 | tf_op jit(solution)/shard_map/ppermute | solution.py:198
  120.7 0.7 collective-permute-start.27
  121.4 0.9 collective-permute-start.28
  122.3 3.2 %shard_map.52 = (f32[256,512]{1,0:T(8,128)S(1)}, bf16[256,512]{1,0:T(8,128)(2,1)S(1)}, bf16[256,512]{1,0:T(8,128)(2,1)S(1)}, bf16[256,512]{1,0:T(8,128)(2,1)S(1)}) custom-call(s32[4]{0:T(128)S(1)} %pad_add_fusion.s_ref, f32[16,2048]{1,0:T(8,128)S(1)} %copy-done.6, bf16[2048,2048]{1,0:T(8,128)(2,1)S(1)} %shard_map.49.right_ref, ...), custom_call_target="tpu_custom_call" | custom-call | flops 2147483648 | bytes 10485760 | tf_op jit(solution)/shard_map/pallas_call | solution.py:268
  125.6 2.4 %collective-permute-start.17 = (bf16[256,512]{1,0:T(8,128)(2,1)S(1)}, bf16[256,512]{1,0:T(8,128)(2,1)S(1)}, u32[]{:S(2)}, u32[]{:S(2)}) collective-permute-start(bf16[256,512]{1,0:T(8,128)(2,1)S(1)} %get-tuple-element.54), channel_id=1, source_target_pairs={{0,3},{1,0},{2,1},{3,2},{4,7},{5,4},{6,5},{7,6},{8,11},{9,8},{10,9... | collective-permute-start | bytes 786440 | tf_op jit(solution)/shard_map/ppermute | solution.py:198
  128.0 1.6 %collective-permute-start.18 = (bf16[256,512]{1,0:T(8,128)(2,1)S(1)}, bf16[256,512]{1,0:T(8,128)(2,1)S(1)}, u32[]{:S(2)}, u32[]{:S(2)}) collective-permute-start(bf16[256,512]{1,0:T(8,128)(2,1)S(1)} %get-tuple-element.55), channel_id=1, source_target_pairs={{0,2},{1,3},{2,0},{3,1},{4,6},{5,7},{6,4},{7,5},{8,10},{9,11},{10,... | collective-permute-start | bytes 786440 | tf_op jit(solution)/shard_map/ppermute | solution.py:198
  129.6 1.2 collective-permute-done.27.refs_6_
  130.8 7.1 %collective-permute-done.28.refs_7_ = bf16[256,512]{1,0:T(8,128)(2,1)S(1)} collective-permute-done((bf16[256,512]{1,0:T(8,128)(2,1)S(1)}, bf16[256,512]{1,0:T(8,128)(2,1)S(1)}, u32[]{:S(2)}, u32[]{:S(2)}) %collective-permute-start.28) | collective-permute-done | bytes 262176 | tf_op jit(solution)/shard_map/ppermute | solution.py:198
  137.8 1.3 collective-permute-done.17.refs_1_
  139.1 1.1 collective-permute-done.18.refs_2_
  140.2 2.6 %collective-permute-done.19.refs_3_ = bf16[256,512]{1,0:T(8,128)(2,1)S(1)} collective-permute-done((bf16[256,512]{1,0:T(8,128)(2,1)S(1)}, bf16[256,512]{1,0:T(8,128)(2,1)S(1)}, u32[]{:S(2)}, u32[]{:S(2)}) %collective-permute-start.19) | collective-permute-done | bytes 262176 | tf_op jit(solution)/shard_map/ppermute | solution.py:198
  142.8 1.6 %shard_map.55 = bf16[512,512]{1,0:T(8,128)(2,1)} custom-call(s32[4]{0:T(128)S(1)} %pad_add_fusion.s_ref, f32[256,512]{1,0:T(8,128)S(1)} %get-tuple-element.53.refs_0_, bf16[256,512]{1,0:T(8,128)(2,1)S(1)} %collective-permute-done.17.refs_1_, bf16[256,512]{1,0:T(8,128)(2,1)S(1)} %collective-permute-done.18.refs_2_, ...), custom_call_target="tpu_custom_call" | custom-call | bytes 3145728 | tf_op jit(solution)/shard_map/pallas_call | solution.py:277
  (37 shorter events, 0.1 us)
Async XLA Ops:
  6.5 34.8 %copy-start.9 = (s32[16,64]{1,0:T(8,128)S(1)}, s32[16,64]{1,0:T(8,128)}, u32[]{:S(2)}) copy-start(s32[16,64]{1,0:T(8,128)} %refs_1_.1) | copy-start | bytes 12292
  6.5 71.0 %all-gather.2.cloned.1.call-start = ((), (), s32[]{:S(2)}) async-start(), calls=%async_computation.1 | async-start | bytes 8912896 | tf_op jit(solution)/shard_map/all_gather | solution.py:220
  8.4 38.3 %copy-start.2 = (bf16[128,2048]{1,0:T(8,128)(2,1)S(1)}, bf16[128,2048]{1,0:T(8,128)(2,1)}, u32[]{:S(2)}) copy-start(bf16[128,2048]{1,0:T(8,128)(2,1)} %constant_dynamic-slice_fusion.refs_0_) | copy-start | bytes 1572868
  8.5 17.5 %collective-permute-start.1 = (bf16[128,2048]{1,0:T(8,128)(2,1)}, bf16[128,2048]{1,0:T(8,128)(2,1)}, u32[]{:S(2)}, u32[]{:S(2)}) collective-permute-start(bf16[128,2048]{1,0:T(8,128)(2,1)} %constant_dynamic-slice_fusion.refs_0_), channel_id=1, source_target_pairs={{0,32},{16,48},{32,64},{48,80},{64,96},{80,112},{96,128},{112,144}... | collective-permute-start | bytes 1572872 | tf_op jit(solution)/shard_map/ppermute | solution.py:198
  10.5 15.9 %collective-permute-start.3 = (bf16[128,2048]{1,0:T(8,128)(2,1)}, bf16[128,2048]{1,0:T(8,128)(2,1)}, u32[]{:S(2)}, u32[]{:S(2)}) collective-permute-start(bf16[128,2048]{1,0:T(8,128)(2,1)} %constant_dynamic-slice_fusion.refs_0_), channel_id=1, source_target_pairs={{0,224},{16,240},{32,0},{48,16},{64,32},{80,48},{96,64},{112,80},{... | collective-permute-start | bytes 1572872 | tf_op jit(solution)/shard_map/ppermute | solution.py:198
  12.8 28.5 %all-to-all-start = ((bf16[64,16,128]{2,1,0:T(8,128)(2,1)}), bf16[64,16,128]{2,1,0:T(8,128)(2,1)S(1)}, u32[]{:S(2)}, u32[]{:S(2)}) async-start(bf16[64,16,128]{2,1,0:T(8,128)(2,1)} %broadcast_in_dim.3), calls=%async_computation | async-start | bytes 524288 | tf_op jit(solution)/shard_map/all_to_all | solution.py:212
  25.8 21.0 %collective-permute-start = (bf16[128,2048]{1,0:T(8,128)(2,1)}, bf16[128,2048]{1,0:T(8,128)(2,1)}, u32[]{:S(2)}, u32[]{:S(2)}) collective-permute-start(bf16[128,2048]{1,0:T(8,128)(2,1)} %constant_dynamic-slice_fusion.refs_0_), channel_id=1, source_target_pairs={{0,16},{16,0},{32,48},{48,32},{64,80},{80,64},{96,112},{112,96},{1... | collective-permute-start | bytes 1572872 | tf_op jit(solution)/shard_map/ppermute | solution.py:202
  26.0 20.7 %collective-permute-start.2 = (bf16[128,2048]{1,0:T(8,128)(2,1)}, bf16[128,2048]{1,0:T(8,128)(2,1)}, u32[]{:S(2)}, u32[]{:S(2)}) collective-permute-start(bf16[128,2048]{1,0:T(8,128)(2,1)} %collective-permute-done.1.refs_2_), channel_id=1, source_target_pairs={{0,16},{16,0},{32,48},{48,32},{64,80},{80,64},{96,112},{112,96},{1... | collective-permute-start | bytes 1572872 | tf_op jit(solution)/shard_map/ppermute | solution.py:202
  26.4 20.4 %collective-permute-start.4 = (bf16[128,2048]{1,0:T(8,128)(2,1)}, bf16[128,2048]{1,0:T(8,128)(2,1)}, u32[]{:S(2)}, u32[]{:S(2)}) collective-permute-start(bf16[128,2048]{1,0:T(8,128)(2,1)} %collective-permute-done.3.refs_4_), channel_id=1, source_target_pairs={{0,16},{16,0},{32,48},{48,32},{64,80},{80,64},{96,112},{112,96},{1... | collective-permute-start | bytes 1572872 | tf_op jit(solution)/shard_map/ppermute | solution.py:202
  41.3 1.6 %copy-start.1 = (bf16[512,2048]{1,0:T(8,128)(2,1)S(1)}, bf16[512,2048]{1,0:T(8,128)(2,1)}, u32[]{:S(2)}) copy-start(bf16[512,2048]{1,0:T(8,128)(2,1)} %refs_3_.1) | copy-start | bytes 6291460
  43.0 0.7 copy-start.10
  46.7 3.8 %copy-start.5 = (f32[16,2048]{1,0:T(8,128)}, f32[16,2048]{1,0:T(8,128)S(1)}, u32[]{:S(2)}) copy-start(f32[16,2048]{1,0:T(8,128)S(1)} %get-tuple-element.35.mc_ref) | copy-start | bytes 393220
  46.7 3.8 %copy-start.7 = (f32[64,2048]{1,0:T(8,128)}, f32[64,2048]{1,0:T(8,128)S(1)}, u32[]{:S(2)}) copy-start(f32[64,2048]{1,0:T(8,128)S(1)} %get-tuple-element.36.mk_ref) | copy-start | bytes 1572868
  50.6 7.9 %collective-permute-start.5 = (bf16[128,768]{1,0:T(8,128)(2,1)S(1)}, bf16[128,768]{1,0:T(8,128)(2,1)S(1)}, u32[]{:S(2)}, u32[]{:S(2)}) collective-permute-start(bf16[128,768]{1,0:T(8,128)(2,1)S(1)} %get-tuple-element.41), channel_id=1, source_target_pairs={{0,12},{4,0},{8,4},{12,8},{1,13},{5,1},{9,5},{13,9},{2,14},{6,2},{... | collective-permute-start | bytes 589832 | tf_op jit(solution)/shard_map/ppermute | solution.py:198
  51.9 9.4 %collective-permute-start.6 = (bf16[128,768]{1,0:T(8,128)(2,1)S(1)}, bf16[128,768]{1,0:T(8,128)(2,1)S(1)}, u32[]{:S(2)}, u32[]{:S(2)}) collective-permute-start(bf16[128,768]{1,0:T(8,128)(2,1)S(1)} %get-tuple-element.42), channel_id=1, source_target_pairs={{0,8},{4,12},{8,0},{12,4},{1,9},{5,13},{9,1},{13,5},{2,10},{6,14},... | collective-permute-start | bytes 589832 | tf_op jit(solution)/shard_map/ppermute | solution.py:198
  53.3 10.6 %collective-permute-start.7 = (bf16[128,768]{1,0:T(8,128)(2,1)S(1)}, bf16[128,768]{1,0:T(8,128)(2,1)S(1)}, u32[]{:S(2)}, u32[]{:S(2)}) collective-permute-start(bf16[128,768]{1,0:T(8,128)(2,1)S(1)} %get-tuple-element.43), channel_id=1, source_target_pairs={{0,4},{4,8},{8,12},{12,0},{1,5},{5,9},{9,13},{13,1},{2,6},{6,10},{... | collective-permute-start | bytes 589832 | tf_op jit(solution)/shard_map/ppermute | solution.py:198
  64.5 12.3 %collective-permute-start.10 = (bf16[128,768]{1,0:T(8,128)(2,1)S(1)}, bf16[128,768]{1,0:T(8,128)(2,1)S(1)}, u32[]{:S(2)}, u32[]{:S(2)}) collective-permute-start(bf16[128,768]{1,0:T(8,128)(2,1)S(1)} %shard_map.48.refs_0_), channel_id=1, source_target_pairs={{0,4},{4,8},{8,12},{12,0},{1,5},{5,9},{9,13},{13,1},{2,6},{6,10},{... | collective-permute-start | bytes 589832 | tf_op jit(solution)/shard_map/ppermute | solution.py:198
  64.7 12.1 %collective-permute-start.8 = (bf16[128,768]{1,0:T(8,128)(2,1)S(1)}, bf16[128,768]{1,0:T(8,128)(2,1)S(1)}, u32[]{:S(2)}, u32[]{:S(2)}) collective-permute-start(bf16[128,768]{1,0:T(8,128)(2,1)S(1)} %shard_map.48.refs_0_), channel_id=1, source_target_pairs={{0,12},{4,0},{8,4},{12,8},{1,13},{5,1},{9,5},{13,9},{2,14},{6,2},{... | collective-permute-start | bytes 589832 | tf_op jit(solution)/shard_map/ppermute | solution.py:198
  67.9 9.0 %collective-permute-start.9 = (bf16[128,768]{1,0:T(8,128)(2,1)S(1)}, bf16[128,768]{1,0:T(8,128)(2,1)S(1)}, u32[]{:S(2)}, u32[]{:S(2)}) collective-permute-start(bf16[128,768]{1,0:T(8,128)(2,1)S(1)} %shard_map.48.refs_0_), channel_id=1, source_target_pairs={{0,8},{4,12},{8,0},{12,4},{1,9},{5,13},{9,1},{13,5},{2,10},{6,14},... | collective-permute-start | bytes 589832 | tf_op jit(solution)/shard_map/ppermute | solution.py:198
  76.9 0.7 copy-start.3
  77.6 3.4 %copy-start = (bf16[2048,2048]{1,0:T(8,128)(2,1)S(1)}, bf16[2048,2048]{1,0:T(8,128)(2,1)}, u32[]{:S(2)}) copy-start(bf16[2048,2048]{1,0:T(8,128)(2,1)} %all-gather.2.cloned.1.call-done.gathered_ref.refs_0_) | copy-start | bytes 25165828
  81.0 22.9 %copy-start.8 = (f32[64,2048]{1,0:T(8,128)S(1)}, f32[64,2048]{1,0:T(8,128)}, u32[]{:S(2)}) copy-start(f32[64,2048]{1,0:T(8,128)} %copy-done.7) | copy-start | bytes 1572868
  84.4 10.8 %collective-permute-start.20 = (bf16[64,1280]{1,0:T(8,128)(2,1)S(1)}, bf16[64,1280]{1,0:T(8,128)(2,1)S(1)}, u32[]{:S(2)}, u32[]{:S(2)}) collective-permute-start(bf16[64,1280]{1,0:T(8,128)(2,1)S(1)} %get-tuple-element.58), channel_id=1, source_target_pairs={{0,12},{4,0},{8,4},{12,8},{1,13},{5,1},{9,5},{13,9},{2,14},{6,2},{... | collective-permute-start | bytes 491528 | tf_op jit(solution)/shard_map/ppermute | solution.py:198
  87.4 8.7 %collective-permute-start.21 = (bf16[64,1280]{1,0:T(8,128)(2,1)S(1)}, bf16[64,1280]{1,0:T(8,128)(2,1)S(1)}, u32[]{:S(2)}, u32[]{:S(2)}) collective-permute-start(bf16[64,1280]{1,0:T(8,128)(2,1)S(1)} %get-tuple-element.59), channel_id=1, source_target_pairs={{0,8},{4,12},{8,0},{12,4},{1,9},{5,13},{9,1},{13,5},{2,10},{6,14},... | collective-permute-start | bytes 491528 | tf_op jit(solution)/shard_map/ppermute | solution.py:198
  87.5 11.9 %collective-permute-start.22 = (bf16[64,1280]{1,0:T(8,128)(2,1)S(1)}, bf16[64,1280]{1,0:T(8,128)(2,1)S(1)}, u32[]{:S(2)}, u32[]{:S(2)}) collective-permute-start(bf16[64,1280]{1,0:T(8,128)(2,1)S(1)} %get-tuple-element.60), channel_id=1, source_target_pairs={{0,4},{4,8},{8,12},{12,0},{1,5},{5,9},{9,13},{13,1},{2,6},{6,10},{... | collective-permute-start | bytes 491528 | tf_op jit(solution)/shard_map/ppermute | solution.py:198
  88.4 14.1 %collective-permute-start.11 = (bf16[64,1280]{1,0:T(8,128)(2,1)S(1)}, bf16[64,1280]{1,0:T(8,128)(2,1)S(1)}, u32[]{:S(2)}, u32[]{:S(2)}) collective-permute-start(bf16[64,1280]{1,0:T(8,128)(2,1)S(1)} %get-tuple-element.50), channel_id=1, source_target_pairs={{0,12},{4,0},{8,4},{12,8},{1,13},{5,1},{9,5},{13,9},{2,14},{6,2},{... | collective-permute-start | bytes 491528 | tf_op jit(solution)/shard_map/ppermute | solution.py:198
  90.7 14.4 %collective-permute-start.12 = (bf16[64,1280]{1,0:T(8,128)(2,1)S(1)}, bf16[64,1280]{1,0:T(8,128)(2,1)S(1)}, u32[]{:S(2)}, u32[]{:S(2)}) collective-permute-start(bf16[64,1280]{1,0:T(8,128)(2,1)S(1)} %get-tuple-element.51), channel_id=1, source_target_pairs={{0,8},{4,12},{8,0},{12,4},{1,9},{5,13},{9,1},{13,5},{2,10},{6,14},... | collective-permute-start | bytes 491528 | tf_op jit(solution)/shard_map/ppermute | solution.py:198
  95.2 11.7 %collective-permute-start.13 = (bf16[64,1280]{1,0:T(8,128)(2,1)S(1)}, bf16[64,1280]{1,0:T(8,128)(2,1)S(1)}, u32[]{:S(2)}, u32[]{:S(2)}) collective-permute-start(bf16[64,1280]{1,0:T(8,128)(2,1)S(1)} %get-tuple-element.52), channel_id=1, source_target_pairs={{0,4},{4,8},{8,12},{12,0},{1,5},{5,9},{9,13},{13,1},{2,6},{6,10},{... | collective-permute-start | bytes 491528 | tf_op jit(solution)/shard_map/ppermute | solution.py:198
  99.9 8.8 %collective-permute-start.23 = (bf16[64,1280]{1,0:T(8,128)(2,1)S(1)}, bf16[64,1280]{1,0:T(8,128)(2,1)S(1)}, u32[]{:S(2)}, u32[]{:S(2)}) collective-permute-start(bf16[64,1280]{1,0:T(8,128)(2,1)S(1)} %shard_map.53.refs_4_), channel_id=1, source_target_pairs={{0,12},{4,0},{8,4},{12,8},{1,13},{5,1},{9,5},{13,9},{2,14},{6,2},{... | collective-permute-start | bytes 491528 | tf_op jit(solution)/shard_map/ppermute | solution.py:198
  100.9 9.2 %collective-permute-start.24 = (bf16[64,1280]{1,0:T(8,128)(2,1)S(1)}, bf16[64,1280]{1,0:T(8,128)(2,1)S(1)}, u32[]{:S(2)}, u32[]{:S(2)}) collective-permute-start(bf16[64,1280]{1,0:T(8,128)(2,1)S(1)} %shard_map.53.refs_4_), channel_id=1, source_target_pairs={{0,8},{4,12},{8,0},{12,4},{1,9},{5,13},{9,1},{13,5},{2,10},{6,14},... | collective-permute-start | bytes 491528 | tf_op jit(solution)/shard_map/ppermute | solution.py:198
  102.5 11.9 %collective-permute-start.25 = (bf16[64,1280]{1,0:T(8,128)(2,1)S(1)}, bf16[64,1280]{1,0:T(8,128)(2,1)S(1)}, u32[]{:S(2)}, u32[]{:S(2)}) collective-permute-start(bf16[64,1280]{1,0:T(8,128)(2,1)S(1)} %shard_map.53.refs_4_), channel_id=1, source_target_pairs={{0,4},{4,8},{8,12},{12,0},{1,5},{5,9},{9,13},{13,1},{2,6},{6,10},{... | collective-permute-start | bytes 491528 | tf_op jit(solution)/shard_map/ppermute | solution.py:198
  103.8 10.6 %copy-start.4 = (bf16[128,768]{1,0:T(8,128)(2,1)S(1)}, bf16[128,768]{1,0:T(8,128)(2,1)}, u32[]{:S(2)}) copy-start(bf16[128,768]{1,0:T(8,128)(2,1)} %copy-done.3) | copy-start | bytes 589828
  103.8 10.6 %copy-start.6 = (f32[16,2048]{1,0:T(8,128)S(1)}, f32[16,2048]{1,0:T(8,128)}, u32[]{:S(2)}) copy-start(f32[16,2048]{1,0:T(8,128)} %copy-done.5) | copy-start | bytes 393220
  107.5 13.9 %collective-permute-start.14 = (bf16[64,1280]{1,0:T(8,128)(2,1)S(1)}, bf16[64,1280]{1,0:T(8,128)(2,1)S(1)}, u32[]{:S(2)}, u32[]{:S(2)}) collective-permute-start(bf16[64,1280]{1,0:T(8,128)(2,1)S(1)} %shard_map.51.refs_4_), channel_id=1, source_target_pairs={{0,12},{4,0},{8,4},{12,8},{1,13},{5,1},{9,5},{13,9},{2,14},{6,2},{... | collective-permute-start | bytes 491528 | tf_op jit(solution)/shard_map/ppermute | solution.py:198
  107.7 14.6 %collective-permute-start.15 = (bf16[64,1280]{1,0:T(8,128)(2,1)S(1)}, bf16[64,1280]{1,0:T(8,128)(2,1)S(1)}, u32[]{:S(2)}, u32[]{:S(2)}) collective-permute-start(bf16[64,1280]{1,0:T(8,128)(2,1)S(1)} %shard_map.51.refs_4_), channel_id=1, source_target_pairs={{0,8},{4,12},{8,0},{12,4},{1,9},{5,13},{9,1},{13,5},{2,10},{6,14},... | collective-permute-start | bytes 491528 | tf_op jit(solution)/shard_map/ppermute | solution.py:198
  108.8 13.5 %collective-permute-start.16 = (bf16[64,1280]{1,0:T(8,128)(2,1)S(1)}, bf16[64,1280]{1,0:T(8,128)(2,1)S(1)}, u32[]{:S(2)}, u32[]{:S(2)}) collective-permute-start(bf16[64,1280]{1,0:T(8,128)(2,1)S(1)} %shard_map.51.refs_4_), channel_id=1, source_target_pairs={{0,4},{4,8},{8,12},{12,0},{1,5},{5,9},{9,13},{13,1},{2,6},{6,10},{... | collective-permute-start | bytes 491528 | tf_op jit(solution)/shard_map/ppermute | solution.py:198
  117.7 11.9 %collective-permute-start.26 = (bf16[256,512]{1,0:T(8,128)(2,1)S(1)}, bf16[256,512]{1,0:T(8,128)(2,1)S(1)}, u32[]{:S(2)}, u32[]{:S(2)}) collective-permute-start(bf16[256,512]{1,0:T(8,128)(2,1)S(1)} %get-tuple-element.62), channel_id=1, source_target_pairs={{0,3},{1,0},{2,1},{3,2},{4,7},{5,4},{6,5},{7,6},{8,11},{9,8},{10,9... | collective-permute-start | bytes 786440 | tf_op jit(solution)/shard_map/ppermute | solution.py:198
  120.7 10.1 %collective-permute-start.27 = (bf16[256,512]{1,0:T(8,128)(2,1)S(1)}, bf16[256,512]{1,0:T(8,128)(2,1)S(1)}, u32[]{:S(2)}, u32[]{:S(2)}) collective-permute-start(bf16[256,512]{1,0:T(8,128)(2,1)S(1)} %get-tuple-element.63), channel_id=1, source_target_pairs={{0,2},{1,3},{2,0},{3,1},{4,6},{5,7},{6,4},{7,5},{8,10},{9,11},{10,... | collective-permute-start | bytes 786440 | tf_op jit(solution)/shard_map/ppermute | solution.py:198
  121.4 16.5 %collective-permute-start.28 = (bf16[256,512]{1,0:T(8,128)(2,1)S(1)}, bf16[256,512]{1,0:T(8,128)(2,1)S(1)}, u32[]{:S(2)}, u32[]{:S(2)}) collective-permute-start(bf16[256,512]{1,0:T(8,128)(2,1)S(1)} %get-tuple-element.64), channel_id=1, source_target_pairs={{0,1},{1,2},{2,3},{3,0},{4,5},{5,6},{6,7},{7,4},{8,9},{9,10},{10,1... | collective-permute-start | bytes 786440 | tf_op jit(solution)/shard_map/ppermute | solution.py:198
  125.6 13.6 %collective-permute-start.17 = (bf16[256,512]{1,0:T(8,128)(2,1)S(1)}, bf16[256,512]{1,0:T(8,128)(2,1)S(1)}, u32[]{:S(2)}, u32[]{:S(2)}) collective-permute-start(bf16[256,512]{1,0:T(8,128)(2,1)S(1)} %get-tuple-element.54), channel_id=1, source_target_pairs={{0,3},{1,0},{2,1},{3,2},{4,7},{5,4},{6,5},{7,6},{8,11},{9,8},{10,9... | collective-permute-start | bytes 786440 | tf_op jit(solution)/shard_map/ppermute | solution.py:198
  128.0 12.3 %collective-permute-start.18 = (bf16[256,512]{1,0:T(8,128)(2,1)S(1)}, bf16[256,512]{1,0:T(8,128)(2,1)S(1)}, u32[]{:S(2)}, u32[]{:S(2)}) collective-permute-start(bf16[256,512]{1,0:T(8,128)(2,1)S(1)} %get-tuple-element.55), channel_id=1, source_target_pairs={{0,2},{1,3},{2,0},{3,1},{4,6},{5,7},{6,4},{7,5},{8,10},{9,11},{10,... | collective-permute-start | bytes 786440 | tf_op jit(solution)/shard_map/ppermute | solution.py:198
  129.6 13.3 %collective-permute-start.19 = (bf16[256,512]{1,0:T(8,128)(2,1)S(1)}, bf16[256,512]{1,0:T(8,128)(2,1)S(1)}, u32[]{:S(2)}, u32[]{:S(2)}) collective-permute-start(bf16[256,512]{1,0:T(8,128)(2,1)S(1)} %get-tuple-element.56), channel_id=1, source_target_pairs={{0,1},{1,2},{2,3},{3,0},{4,5},{5,6},{6,7},{7,4},{8,9},{9,10},{10,1... | collective-permute-start | bytes 786440 | tf_op jit(solution)/shard_map/ppermute | solution.py:198
Sparse Core Ops, SparseCore 0:
  9.2 62.2 all-gather.1

commit v5 on v4

--- a/solution.py
+++ b/solution.py
@@ -118,20 +118,19 @@
                 )
 
 
-def product_one_kernel(slots, halves, n_pieces, s_ref, left_ref, mt_ref, *refs):
+def product_one_kernel(slots, halves, half, n_pieces, s_ref, left_ref, mt_ref, *refs):
     pieces, outs, right = refs[:n_pieces], refs[n_pieces:-1], refs[-1]
     if n_pieces > 1:
         load_pieces(pieces, mt_ref, 8 * slots[0], right)
     else:
         load_slots(slots, (s_ref[0], s_ref[1]), pieces[0], mt_ref, right)
     height = 128 // halves
+    left = jnp.concatenate([left_ref[pl.ds(128 * quarter + height * half, height), :] for quarter in range(4)], 0)
     for start in range(0, right.shape[0], 256):
-        block = dot(left_ref[...], right[pl.ds(start, 256), :], NT)
-        for half in range(halves):
-            for quarter in range(4):
-                row = 128 * quarter + height * half
-                out = outs[4 * half + quarter]
-                out[:, pl.ds(start, 256)] = block[row : row + height].astype(out.dtype)
+        block = dot(left, right[pl.ds(start, 256), :], NT)
+        for quarter in range(4):
+            rows = slice(height * quarter, height * quarter + height)
+            outs[quarter][:, pl.ds(start, 256)] = block[rows].astype(outs[quarter].dtype)
 
 
 def square_kernel(first_slot, first_block, s_ref, ms_ref, own_ref, a_ref, b_ref, c_ref, *refs):
@@ -238,17 +237,16 @@
 
     def start(slots, halves, held):
         height, width = 128 // halves, 256 * len(slots)
-        parts = call(
-            functools.partial(product_one_kernel, slots, halves, len(held)),
-            ((shape(height, width, dtype=F32),) + (shape(height, width),) * 3) * halves,
-            3 + len(held),
-            [pltpu.VMEM((width, 2048), BF)],
-            flops=2 * 512 * 2048 * width,
-            byts=2 * 2048 * (512 + width),
-        )(where, left, mt, *held)
         squares = []
         for half in range(halves):
-            mine, *others = parts[4 * half : 4 * half + 4]
+            mine, *others = call(
+                functools.partial(product_one_kernel, slots, halves, half, len(held)),
+                (shape(height, width, dtype=F32),) + (shape(height, width),) * 3,
+                3 + len(held),
+                [pltpu.VMEM((width, 2048), BF)],
+                flops=2 * 512 // halves * 2048 * width,
+                byts=2 * 2048 * (512 + width),
+            )(where, left, mt, *held)
             mine = call(
                 functools.partial(square_kernel, slots[0], half * (4 // halves)),
                 shape(height, width),

time: 152 us -> 152 us (level)
  waiting for transfers between devices: 59.2 us -> 56.7 us
  starting transfers between devices: 46.3 us -> 48.1 us
    all_to_all x1, waiting for transfers between devices: 14.7 us -> 9.09 us  [gather_patterns(): lax.all_to_all(jnp.broadcast_to(both, (64, 16, 128)), ('row', 'col'), 0, 0)]
    ppermute x26, starting transfers between devices: 32.6 us -> 35.7 us  [shift(): lax.ppermute(array, axis, [(i, (i + step) % size) for i in range(size)])]
    ppermute x26, waiting for transfers between devices: 44.5 us -> 47.6 us  [shift(): lax.ppermute(array, axis, [(i, (i + step) % size) for i in range(size)])]
    pallas_call x2 -> x3, Pallas kernels: 7.23 us -> 7.95 us  [start(): call(functools.partial(product_one_kernel, slots, halves, half, len(held)...]
    unnamed x22 -> x26, local copies, waits for them, and re-layouts: 6.41 us -> 6.4 us
  transfers between devices with their start and end apart: 31 -> 31, of which waited for: 15 -> 16; matrix products, arithmetic and copies ran while one was open for 2% -> 2% of each run, Pallas kernels for 11% -> 12%
where the time goes in v5:
time: 152 us; the launch traced here: 151 us
  waiting for transfers between devices  56.7 us (37%)
  starting transfers between devices  48.1 us (32%)
  Pallas kernels  22.2 us (15%)
  between operations  13.6 us (9%)
  local copies, waits for them, and re-layouts  9.04 us (6%)
  other arithmetic  1.56 us (1%)
    ppermute x26, waiting for transfers between devices, shift(): lax.ppermute(array, axis, [(i, (i + step) % size) for i in range(size)])  47.6 us
    ppermute x26, starting transfers between devices, shift(): lax.ppermute(array, axis, [(i, (i + step) % size) for i in range(size)])  35.7 us
    all_to_all x1, starting transfers between devices, gather_patterns(): lax.all_to_all(jnp.broadcast_to(both, (64, 16, 128)), ('row', 'col'), 0, 0)  11.8 us
    all_to_all x1, waiting for transfers between devices, gather_patterns(): lax.all_to_all(jnp.broadcast_to(both, (64, 16, 128)), ('row', 'col'), 0, 0)  9.09 us
    pallas_call x3, Pallas kernels, start(): call(functools.partial(product_one_kernel, slots, halves, half, len(held)...  7.95 us
    pallas_call x2, Pallas kernels, body(): call(functools.partial(product_two_kernel, half, len(first)), (shape(heig...  6.5 us
    unnamed x26, local copies, waits for them, and re-layouts  6.4 us
    pallas_call x1, Pallas kernels, body(): call(prep_kernel, (shape(512, 2048), shape(64, 2048, dtype=F32), shape(64...  3.07 us
  transfers between devices with their start and end apart: 31, of which 16 were waited for; matrix products, arithmetic and copies ran while one was open for 2% of the time, Pallas kernels for 12%

profile of v5, /device:TPU:32, one launch (start us, length us, event | category | flops | bytes accessed | tf_op | source)
XLA Modules:
  0.0 151.2 jit_solution(12256074162799360341)
XLA Ops:
  6.5 1.9 %constant_dynamic-slice_fusion.refs_0_ = bf16[128,2048]{1,0:T(8,128)(2,1)} fusion(bf16[512,2048]{1,0:T(8,128)(2,1)} %refs_3_.1, s32[]{:T(128)S(6)} %select_n.16), kind=kLoop, calls=%fused_computation.2 | loop fusion | bytes 1048580 | tf_op jit(solution)/shard_map/dynamic_slice | solution.py:217
  8.5 1.9 %collective-permute-start.3 = (bf16[128,2048]{1,0:T(8,128)(2,1)}, bf16[128,2048]{1,0:T(8,128)(2,1)}, u32[]{:S(2)}, u32[]{:S(2)}) collective-permute-start(bf16[128,2048]{1,0:T(8,128)(2,1)} %constant_dynamic-slice_fusion.refs_0_), channel_id=1, source_target_pairs={{0,224},{16,240},{32,0},{48,16},{64,32},{80,48},{96,64},{112,80},{... | collective-permute-start | bytes 1572872 | tf_op jit(solution)/shard_map/ppermute | solution.py:197
  10.4 0.2 collective-permute-start.1
  10.6 0.7 convert.7
  11.3 0.7 convert.6
  12.0 0.1 pad_maximum_fusion
  12.0 0.7 broadcast_in_dim.3
  12.8 11.8 %all-to-all-start = ((bf16[64,16,128]{2,1,0:T(8,128)(2,1)}), bf16[64,16,128]{2,1,0:T(8,128)(2,1)S(1)}, u32[]{:S(2)}, u32[]{:S(2)}) async-start(bf16[64,16,128]{2,1,0:T(8,128)(2,1)} %broadcast_in_dim.3), calls=%async_computation | async-start | bytes 524288 | tf_op jit(solution)/shard_map/all_to_all | solution.py:211
  24.6 0.2 collective-permute-start
  24.8 0.4 collective-permute-start.4
  25.2 7.2 %collective-permute-done.1.refs_2_ = bf16[128,2048]{1,0:T(8,128)(2,1)} collective-permute-done((bf16[128,2048]{1,0:T(8,128)(2,1)}, bf16[128,2048]{1,0:T(8,128)(2,1)}, u32[]{:S(2)}, u32[]{:S(2)}) %collective-permute-start.1) | collective-permute-done | bytes 524320 | tf_op jit(solution)/shard_map/ppermute | solution.py:197
  32.4 0.1 pad_add_fusion.s_ref
  32.5 9.1 %all-to-all-done.refs_0_ = bf16[64,16,128]{2,1,0:T(8,128)(2,1)S(1)} async-done(((bf16[64,16,128]{2,1,0:T(8,128)(2,1)}), bf16[64,16,128]{2,1,0:T(8,128)(2,1)S(1)}, u32[]{:S(2)}, u32[]{:S(2)}) %all-to-all-start) | async-done | bytes 262176 | tf_op jit(solution)/shard_map/all_to_all | solution.py:211
  41.5 1.6 %copy-done.1 = bf16[512,2048]{1,0:T(8,128)(2,1)S(1)} copy-done((bf16[512,2048]{1,0:T(8,128)(2,1)S(1)}, bf16[512,2048]{1,0:T(8,128)(2,1)}, u32[]{:S(2)}) %copy-start.1) | copy-done | bytes 2097176
  43.1 0.7 copy-done.10
  43.8 3.1 %shard_map.46 = (bf16[512,2048]{1,0:T(8,128)(2,1)S(1)}, f32[64,2048]{1,0:T(8,128)S(1)}, f32[64,2048]{1,0:T(8,128)S(1)}, f32[16,2048]{1,0:T(8,128)S(1)}, f32[16,2048]{1,0:T(8,128)S(1)}) custom-call(s32[4]{0:T(128)S(1)} %pad_add_fusion.s_ref, bf16[64,16,128]{2,1,0:T(8,128)(2,1)S(1)} %all-to-all-done.refs_0_, s32[16,64]{1,0:T(8,128)S(1)} %copy-done.9, ...), custom_call_target="tpu_custom_call" | custom-call | flops 209715200 | bytes 6291456 | tf_op jit(solution)/shard_map/pallas_call | solution.py:224
  47.0 3.7 %shard_map.47 = (f32[128,768]{1,0:T(8,128)S(1)}, bf16[128,768]{1,0:T(8,128)(2,1)S(1)}, bf16[128,768]{1,0:T(8,128)(2,1)S(1)}, bf16[128,768]{1,0:T(8,128)(2,1)S(1)}) custom-call(s32[4]{0:T(128)S(1)} %pad_add_fusion.s_ref, bf16[512,2048]{1,0:T(8,128)(2,1)S(1)} %get-tuple-element.38.left_ref.refs_0_, f32[64,2048]{1,0:T(8,128)S(1)} %get-tuple-element.39.mt_ref.refs_1_, ...), custom_call_target="tpu_custom_call" | custom-call | flops 1610612736 | bytes 5242880 | tf_op jit(solution)/shard_map/pallas_call | solution.py:242
  50.7 2.3 %collective-permute-start.5 = (bf16[128,768]{1,0:T(8,128)(2,1)S(1)}, bf16[128,768]{1,0:T(8,128)(2,1)S(1)}, u32[]{:S(2)}, u32[]{:S(2)}) collective-permute-start(bf16[128,768]{1,0:T(8,128)(2,1)S(1)} %get-tuple-element.41), channel_id=1, source_target_pairs={{0,12},{4,0},{8,4},{12,8},{1,13},{5,1},{9,5},{13,9},{2,14},{6,2},{... | collective-permute-start | bytes 589832 | tf_op jit(solution)/shard_map/ppermute | solution.py:197
  53.0 0.8 collective-permute-start.6
  53.8 0.1 collective-permute-start.7
  53.9 4.6 %collective-permute-done.5.a_ref = bf16[128,768]{1,0:T(8,128)(2,1)S(1)} collective-permute-done((bf16[128,768]{1,0:T(8,128)(2,1)S(1)}, bf16[128,768]{1,0:T(8,128)(2,1)S(1)}, u32[]{:S(2)}, u32[]{:S(2)}) %collective-permute-start.5) | collective-permute-done | bytes 196640 | tf_op jit(solution)/shard_map/ppermute | solution.py:197
  58.6 3.6 %collective-permute-done.6.b_ref = bf16[128,768]{1,0:T(8,128)(2,1)S(1)} collective-permute-done((bf16[128,768]{1,0:T(8,128)(2,1)S(1)}, bf16[128,768]{1,0:T(8,128)(2,1)S(1)}, u32[]{:S(2)}, u32[]{:S(2)}) %collective-permute-start.6) | collective-permute-done | bytes 196640 | tf_op jit(solution)/shard_map/ppermute | solution.py:197
  62.2 2.1 %collective-permute-done.7.c_ref = bf16[128,768]{1,0:T(8,128)(2,1)S(1)} collective-permute-done((bf16[128,768]{1,0:T(8,128)(2,1)S(1)}, bf16[128,768]{1,0:T(8,128)(2,1)S(1)}, u32[]{:S(2)}, u32[]{:S(2)}) %collective-permute-start.7) | collective-permute-done | bytes 196640 | tf_op jit(solution)/shard_map/ppermute | solution.py:197
  64.3 0.7 shard_map.48.refs_0_
  64.9 1.1 collective-permute-start.10
  66.0 1.5 %collective-permute-start.9 = (bf16[128,768]{1,0:T(8,128)(2,1)S(1)}, bf16[128,768]{1,0:T(8,128)(2,1)S(1)}, u32[]{:S(2)}, u32[]{:S(2)}) collective-permute-start(bf16[128,768]{1,0:T(8,128)(2,1)S(1)} %shard_map.48.refs_0_), channel_id=1, source_target_pairs={{0,8},{4,12},{8,0},{12,4},{1,9},{5,13},{9,1},{13,5},{2,10},{6,14},... | collective-permute-start | bytes 589832 | tf_op jit(solution)/shard_map/ppermute | solution.py:197
  67.5 1.8 %collective-permute-start.8 = (bf16[128,768]{1,0:T(8,128)(2,1)S(1)}, bf16[128,768]{1,0:T(8,128)(2,1)S(1)}, u32[]{:S(2)}, u32[]{:S(2)}) collective-permute-start(bf16[128,768]{1,0:T(8,128)(2,1)S(1)} %shard_map.48.refs_0_), channel_id=1, source_target_pairs={{0,12},{4,0},{8,4},{12,8},{1,13},{5,1},{9,5},{13,9},{2,14},{6,2},{... | collective-permute-start | bytes 589832 | tf_op jit(solution)/shard_map/ppermute | solution.py:197
  69.4 7.6 %collective-permute-done.10.refs_3_ = bf16[128,768]{1,0:T(8,128)(2,1)S(1)} collective-permute-done((bf16[128,768]{1,0:T(8,128)(2,1)S(1)}, bf16[128,768]{1,0:T(8,128)(2,1)S(1)}, u32[]{:S(2)}, u32[]{:S(2)}) %collective-permute-start.10) | collective-permute-done | bytes 196640 | tf_op jit(solution)/shard_map/ppermute | solution.py:197
  76.9 0.6 collective-permute-done.8.refs_1_
  77.6 0.7 copy-done.3
  78.2 3.4 %copy-done = bf16[2048,2048]{1,0:T(8,128)(2,1)S(1)} copy-done((bf16[2048,2048]{1,0:T(8,128)(2,1)S(1)}, bf16[2048,2048]{1,0:T(8,128)(2,1)}, u32[]{:S(2)}) %copy-start) | copy-done | bytes 8388632
  81.6 2.1 %shard_map.50 = (f32[64,1280]{1,0:T(8,128)S(1)}, bf16[64,1280]{1,0:T(8,128)(2,1)S(1)}, bf16[64,1280]{1,0:T(8,128)(2,1)S(1)}, bf16[64,1280]{1,0:T(8,128)(2,1)S(1)}) custom-call(s32[4]{0:T(128)S(1)} %pad_add_fusion.s_ref, bf16[512,2048]{1,0:T(8,128)(2,1)S(1)} %get-tuple-element.38.left_ref.refs_0_, f32[64,2048]{1,0:T(8,128)S(1)} %get-tuple-element.39.mt_ref.refs_1_, ...), custom_call_target="tpu_custom_call" | custom-call | flops 1342177280 | bytes 7340032 | tf_op jit(solution)/shard_map/pallas_call | solution.py:242
  83.8 2.7 %collective-permute-start.11 = (bf16[64,1280]{1,0:T(8,128)(2,1)S(1)}, bf16[64,1280]{1,0:T(8,128)(2,1)S(1)}, u32[]{:S(2)}, u32[]{:S(2)}) collective-permute-start(bf16[64,1280]{1,0:T(8,128)(2,1)S(1)} %get-tuple-element.50), channel_id=1, source_target_pairs={{0,12},{4,0},{8,4},{12,8},{1,13},{5,1},{9,5},{13,9},{2,14},{6,2},{... | collective-permute-start | bytes 491528 | tf_op jit(solution)/shard_map/ppermute | solution.py:197
  86.5 0.2 collective-permute-start.12
  86.6 0.8 collective-permute-start.13
  87.4 2.1 %shard_map.53 = (f32[64,1280]{1,0:T(8,128)S(1)}, bf16[64,1280]{1,0:T(8,128)(2,1)S(1)}, bf16[64,1280]{1,0:T(8,128)(2,1)S(1)}, bf16[64,1280]{1,0:T(8,128)(2,1)S(1)}) custom-call(s32[4]{0:T(128)S(1)} %pad_add_fusion.s_ref, bf16[512,2048]{1,0:T(8,128)(2,1)S(1)} %get-tuple-element.38.left_ref.refs_0_, f32[64,2048]{1,0:T(8,128)S(1)} %get-tuple-element.39.mt_ref.refs_1_, ...), custom_call_target="tpu_custom_call" | custom-call | flops 1342177280 | bytes 7340032 | tf_op jit(solution)/shard_map/pallas_call | solution.py:242
  89.6 2.5 %collective-permute-start.20 = (bf16[64,1280]{1,0:T(8,128)(2,1)S(1)}, bf16[64,1280]{1,0:T(8,128)(2,1)S(1)}, u32[]{:S(2)}, u32[]{:S(2)}) collective-permute-start(bf16[64,1280]{1,0:T(8,128)(2,1)S(1)} %get-tuple-element.58), channel_id=1, source_target_pairs={{0,12},{4,0},{8,4},{12,8},{1,13},{5,1},{9,5},{13,9},{2,14},{6,2},{... | collective-permute-start | bytes 491528 | tf_op jit(solution)/shard_map/ppermute | solution.py:197
  92.1 2.2 %collective-permute-start.21 = (bf16[64,1280]{1,0:T(8,128)(2,1)S(1)}, bf16[64,1280]{1,0:T(8,128)(2,1)S(1)}, u32[]{:S(2)}, u32[]{:S(2)}) collective-permute-start(bf16[64,1280]{1,0:T(8,128)(2,1)S(1)} %get-tuple-element.59), channel_id=1, source_target_pairs={{0,8},{4,12},{8,0},{12,4},{1,9},{5,13},{9,1},{13,5},{2,10},{6,14},... | collective-permute-start | bytes 491528 | tf_op jit(solution)/shard_map/ppermute | solution.py:197
  94.2 0.8 collective-permute-done.12.b_ref
  95.1 3.0 %collective-permute-done.13.c_ref = bf16[64,1280]{1,0:T(8,128)(2,1)S(1)} collective-permute-done((bf16[64,1280]{1,0:T(8,128)(2,1)S(1)}, bf16[64,1280]{1,0:T(8,128)(2,1)S(1)}, u32[]{:S(2)}, u32[]{:S(2)}) %collective-permute-start.13) | collective-permute-done | bytes 163872 | tf_op jit(solution)/shard_map/ppermute | solution.py:197
  98.1 0.6 shard_map.51.refs_4_
  98.7 0.1 collective-permute-start.16
  98.8 2.5 %collective-permute-start.15 = (bf16[64,1280]{1,0:T(8,128)(2,1)S(1)}, bf16[64,1280]{1,0:T(8,128)(2,1)S(1)}, u32[]{:S(2)}, u32[]{:S(2)}) collective-permute-start(bf16[64,1280]{1,0:T(8,128)(2,1)S(1)} %shard_map.51.refs_4_), channel_id=1, source_target_pairs={{0,8},{4,12},{8,0},{12,4},{1,9},{5,13},{9,1},{13,5},{2,10},{6,14},... | collective-permute-start | bytes 491528 | tf_op jit(solution)/shard_map/ppermute | solution.py:197
  101.3 3.0 %collective-permute-start.14 = (bf16[64,1280]{1,0:T(8,128)(2,1)S(1)}, bf16[64,1280]{1,0:T(8,128)(2,1)S(1)}, u32[]{:S(2)}, u32[]{:S(2)}) collective-permute-start(bf16[64,1280]{1,0:T(8,128)(2,1)S(1)} %shard_map.51.refs_4_), channel_id=1, source_target_pairs={{0,12},{4,0},{8,4},{12,8},{1,13},{5,1},{9,5},{13,9},{2,14},{6,2},{... | collective-permute-start | bytes 491528 | tf_op jit(solution)/shard_map/ppermute | solution.py:197
  104.4 1.3 shard_map.49.right_ref
  105.7 0.6 shard_map.54.refs_4_
  106.3 0.1 collective-permute-start.25
  106.4 2.0 %collective-permute-start.24 = (bf16[64,1280]{1,0:T(8,128)(2,1)S(1)}, bf16[64,1280]{1,0:T(8,128)(2,1)S(1)}, u32[]{:S(2)}, u32[]{:S(2)}) collective-permute-start(bf16[64,1280]{1,0:T(8,128)(2,1)S(1)} %shard_map.54.refs_4_), channel_id=1, source_target_pairs={{0,8},{4,12},{8,0},{12,4},{1,9},{5,13},{9,1},{13,5},{2,10},{6,14},... | collective-permute-start | bytes 491528 | tf_op jit(solution)/shard_map/ppermute | solution.py:197
  108.4 1.3 collective-permute-start.23
  109.7 2.9 %collective-permute-done.15.refs_6_ = bf16[64,1280]{1,0:T(8,128)(2,1)S(1)} collective-permute-done((bf16[64,1280]{1,0:T(8,128)(2,1)S(1)}, bf16[64,1280]{1,0:T(8,128)(2,1)S(1)}, u32[]{:S(2)}, u32[]{:S(2)}) %collective-permute-start.15) | collective-permute-done | bytes 163872 | tf_op jit(solution)/shard_map/ppermute | solution.py:197
  112.7 3.3 %shard_map.52 = (f32[256,512]{1,0:T(8,128)S(1)}, bf16[256,512]{1,0:T(8,128)(2,1)S(1)}, bf16[256,512]{1,0:T(8,128)(2,1)S(1)}, bf16[256,512]{1,0:T(8,128)(2,1)S(1)}) custom-call(s32[4]{0:T(128)S(1)} %pad_add_fusion.s_ref, f32[16,2048]{1,0:T(8,128)S(1)} %copy-done.6, bf16[2048,2048]{1,0:T(8,128)(2,1)S(1)} %shard_map.49.right_ref, ...), custom_call_target="tpu_custom_call" | custom-call | flops 2147483648 | bytes 10485760 | tf_op jit(solution)/shard_map/pallas_call | solution.py:266
  116.0 2.9 %collective-permute-start.17 = (bf16[256,512]{1,0:T(8,128)(2,1)S(1)}, bf16[256,512]{1,0:T(8,128)(2,1)S(1)}, u32[]{:S(2)}, u32[]{:S(2)}) collective-permute-start(bf16[256,512]{1,0:T(8,128)(2,1)S(1)} %get-tuple-element.54), channel_id=1, source_target_pairs={{0,3},{1,0},{2,1},{3,2},{4,7},{5,4},{6,5},{7,6},{8,11},{9,8},{10,9... | collective-permute-start | bytes 786440 | tf_op jit(solution)/shard_map/ppermute | solution.py:197
  118.9 0.8 collective-permute-start.18
  119.7 0.9 collective-permute-start.19
  120.6 3.2 %shard_map.55 = (f32[256,512]{1,0:T(8,128)S(1)}, bf16[256,512]{1,0:T(8,128)(2,1)S(1)}, bf16[256,512]{1,0:T(8,128)(2,1)S(1)}, bf16[256,512]{1,0:T(8,128)(2,1)S(1)}) custom-call(s32[4]{0:T(128)S(1)} %pad_add_fusion.s_ref, f32[16,2048]{1,0:T(8,128)S(1)} %copy-done.6, bf16[2048,2048]{1,0:T(8,128)(2,1)S(1)} %shard_map.49.right_ref, ...), custom_call_target="tpu_custom_call" | custom-call | flops 2147483648 | bytes 10485760 | tf_op jit(solution)/shard_map/pallas_call | solution.py:266
  123.8 2.4 %collective-permute-start.26 = (bf16[256,512]{1,0:T(8,128)(2,1)S(1)}, bf16[256,512]{1,0:T(8,128)(2,1)S(1)}, u32[]{:S(2)}, u32[]{:S(2)}) collective-permute-start(bf16[256,512]{1,0:T(8,128)(2,1)S(1)} %get-tuple-element.62), channel_id=1, source_target_pairs={{0,3},{1,0},{2,1},{3,2},{4,7},{5,4},{6,5},{7,6},{8,11},{9,8},{10,9... | collective-permute-start | bytes 786440 | tf_op jit(solution)/shard_map/ppermute | solution.py:197
  126.3 1.5 collective-permute-start.27
  127.8 0.3 collective-permute-done.17.refs_1_
  128.1 1.5 %collective-permute-done.18.refs_2_ = bf16[256,512]{1,0:T(8,128)(2,1)S(1)} collective-permute-done((bf16[256,512]{1,0:T(8,128)(2,1)S(1)}, bf16[256,512]{1,0:T(8,128)(2,1)S(1)}, u32[]{:S(2)}, u32[]{:S(2)}) %collective-permute-start.18) | collective-permute-done | bytes 262176 | tf_op jit(solution)/shard_map/ppermute | solution.py:197
  129.7 6.2 %collective-permute-done.19.refs_3_ = bf16[256,512]{1,0:T(8,128)(2,1)S(1)} collective-permute-done((bf16[256,512]{1,0:T(8,128)(2,1)S(1)}, bf16[256,512]{1,0:T(8,128)(2,1)S(1)}, u32[]{:S(2)}, u32[]{:S(2)}) %collective-permute-start.19) | collective-permute-done | bytes 262176 | tf_op jit(solution)/shard_map/ppermute | solution.py:197
  135.8 3.3 %collective-permute-done.26.refs_5_ = bf16[256,512]{1,0:T(8,128)(2,1)S(1)} collective-permute-done((bf16[256,512]{1,0:T(8,128)(2,1)S(1)}, bf16[256,512]{1,0:T(8,128)(2,1)S(1)}, u32[]{:S(2)}, u32[]{:S(2)}) %collective-permute-start.26) | collective-permute-done | bytes 262176 | tf_op jit(solution)/shard_map/ppermute | solution.py:197
  139.1 1.0 collective-permute-done.27.refs_6_
  140.2 2.7 %collective-permute-done.28.refs_7_ = bf16[256,512]{1,0:T(8,128)(2,1)S(1)} collective-permute-done((bf16[256,512]{1,0:T(8,128)(2,1)S(1)}, bf16[256,512]{1,0:T(8,128)(2,1)S(1)}, u32[]{:S(2)}, u32[]{:S(2)}) %collective-permute-start.28) | collective-permute-done | bytes 262176 | tf_op jit(solution)/shard_map/ppermute | solution.py:197
  142.8 1.6 %shard_map.56 = bf16[512,512]{1,0:T(8,128)(2,1)} custom-call(s32[4]{0:T(128)S(1)} %pad_add_fusion.s_ref, f32[256,512]{1,0:T(8,128)S(1)} %get-tuple-element.53.refs_0_, bf16[256,512]{1,0:T(8,128)(2,1)S(1)} %collective-permute-done.17.refs_1_, bf16[256,512]{1,0:T(8,128)(2,1)S(1)} %collective-permute-done.18.refs_2_, ...), custom_call_target="tpu_custom_call" | custom-call | bytes 3145728 | tf_op jit(solution)/shard_map/pallas_call | solution.py:275
  (43 shorter events, 0.1 us)
Async XLA Ops:
  6.5 35.0 %copy-start.9 = (s32[16,64]{1,0:T(8,128)S(1)}, s32[16,64]{1,0:T(8,128)}, u32[]{:S(2)}) copy-start(s32[16,64]{1,0:T(8,128)} %refs_1_.1) | copy-start | bytes 12292
  6.5 71.7 %all-gather.2.cloned.1.call-start = ((), (), s32[]{:S(2)}) async-start(), calls=%async_computation.1 | async-start | bytes 8912896 | tf_op jit(solution)/shard_map/all_gather | solution.py:219
  8.4 38.5 %copy-start.2 = (bf16[128,2048]{1,0:T(8,128)(2,1)S(1)}, bf16[128,2048]{1,0:T(8,128)(2,1)}, u32[]{:S(2)}) copy-start(bf16[128,2048]{1,0:T(8,128)(2,1)} %constant_dynamic-slice_fusion.refs_0_) | copy-start | bytes 1572868
  8.5 16.3 %collective-permute-start.3 = (bf16[128,2048]{1,0:T(8,128)(2,1)}, bf16[128,2048]{1,0:T(8,128)(2,1)}, u32[]{:S(2)}, u32[]{:S(2)}) collective-permute-start(bf16[128,2048]{1,0:T(8,128)(2,1)} %constant_dynamic-slice_fusion.refs_0_), channel_id=1, source_target_pairs={{0,224},{16,240},{32,0},{48,16},{64,32},{80,48},{96,64},{112,80},{... | collective-permute-start | bytes 1572872 | tf_op jit(solution)/shard_map/ppermute | solution.py:197
  10.4 22.0 %collective-permute-start.1 = (bf16[128,2048]{1,0:T(8,128)(2,1)}, bf16[128,2048]{1,0:T(8,128)(2,1)}, u32[]{:S(2)}, u32[]{:S(2)}) collective-permute-start(bf16[128,2048]{1,0:T(8,128)(2,1)} %constant_dynamic-slice_fusion.refs_0_), channel_id=1, source_target_pairs={{0,32},{16,48},{32,64},{48,80},{64,96},{80,112},{96,128},{112,144}... | collective-permute-start | bytes 1572872 | tf_op jit(solution)/shard_map/ppermute | solution.py:197
  12.8 28.8 %all-to-all-start = ((bf16[64,16,128]{2,1,0:T(8,128)(2,1)}), bf16[64,16,128]{2,1,0:T(8,128)(2,1)S(1)}, u32[]{:S(2)}, u32[]{:S(2)}) async-start(bf16[64,16,128]{2,1,0:T(8,128)(2,1)} %broadcast_in_dim.3), calls=%async_computation | async-start | bytes 524288 | tf_op jit(solution)/shard_map/all_to_all | solution.py:211
  24.6 22.4 %collective-permute-start = (bf16[128,2048]{1,0:T(8,128)(2,1)}, bf16[128,2048]{1,0:T(8,128)(2,1)}, u32[]{:S(2)}, u32[]{:S(2)}) collective-permute-start(bf16[128,2048]{1,0:T(8,128)(2,1)} %constant_dynamic-slice_fusion.refs_0_), channel_id=1, source_target_pairs={{0,16},{16,0},{32,48},{48,32},{64,80},{80,64},{96,112},{112,96},{1... | collective-permute-start | bytes 1572872 | tf_op jit(solution)/shard_map/ppermute | solution.py:201
  24.8 22.1 %collective-permute-start.4 = (bf16[128,2048]{1,0:T(8,128)(2,1)}, bf16[128,2048]{1,0:T(8,128)(2,1)}, u32[]{:S(2)}, u32[]{:S(2)}) collective-permute-start(bf16[128,2048]{1,0:T(8,128)(2,1)} %collective-permute-done.3.refs_4_), channel_id=1, source_target_pairs={{0,16},{16,0},{32,48},{48,32},{64,80},{80,64},{96,112},{112,96},{1... | collective-permute-start | bytes 1572872 | tf_op jit(solution)/shard_map/ppermute | solution.py:201
  32.4 14.6 %collective-permute-start.2 = (bf16[128,2048]{1,0:T(8,128)(2,1)}, bf16[128,2048]{1,0:T(8,128)(2,1)}, u32[]{:S(2)}, u32[]{:S(2)}) collective-permute-start(bf16[128,2048]{1,0:T(8,128)(2,1)} %collective-permute-done.1.refs_2_), channel_id=1, source_target_pairs={{0,16},{16,0},{32,48},{48,32},{64,80},{80,64},{96,112},{112,96},{1... | collective-permute-start | bytes 1572872 | tf_op jit(solution)/shard_map/ppermute | solution.py:201
  41.5 1.6 %copy-start.1 = (bf16[512,2048]{1,0:T(8,128)(2,1)S(1)}, bf16[512,2048]{1,0:T(8,128)(2,1)}, u32[]{:S(2)}) copy-start(bf16[512,2048]{1,0:T(8,128)(2,1)} %refs_3_.1) | copy-start | bytes 6291460
  43.1 0.7 copy-start.10
  46.9 3.8 %copy-start.5 = (f32[16,2048]{1,0:T(8,128)}, f32[16,2048]{1,0:T(8,128)S(1)}, u32[]{:S(2)}) copy-start(f32[16,2048]{1,0:T(8,128)S(1)} %get-tuple-element.35.mc_ref) | copy-start | bytes 393220
  46.9 3.8 %copy-start.7 = (f32[64,2048]{1,0:T(8,128)}, f32[64,2048]{1,0:T(8,128)S(1)}, u32[]{:S(2)}) copy-start(f32[64,2048]{1,0:T(8,128)S(1)} %get-tuple-element.36.mk_ref) | copy-start | bytes 1572868
  50.7 7.9 %collective-permute-start.5 = (bf16[128,768]{1,0:T(8,128)(2,1)S(1)}, bf16[128,768]{1,0:T(8,128)(2,1)S(1)}, u32[]{:S(2)}, u32[]{:S(2)}) collective-permute-start(bf16[128,768]{1,0:T(8,128)(2,1)S(1)} %get-tuple-element.41), channel_id=1, source_target_pairs={{0,12},{4,0},{8,4},{12,8},{1,13},{5,1},{9,5},{13,9},{2,14},{6,2},{... | collective-permute-start | bytes 589832 | tf_op jit(solution)/shard_map/ppermute | solution.py:197
  53.0 9.2 %collective-permute-start.6 = (bf16[128,768]{1,0:T(8,128)(2,1)S(1)}, bf16[128,768]{1,0:T(8,128)(2,1)S(1)}, u32[]{:S(2)}, u32[]{:S(2)}) collective-permute-start(bf16[128,768]{1,0:T(8,128)(2,1)S(1)} %get-tuple-element.42), channel_id=1, source_target_pairs={{0,8},{4,12},{8,0},{12,4},{1,9},{5,13},{9,1},{13,5},{2,10},{6,14},... | collective-permute-start | bytes 589832 | tf_op jit(solution)/shard_map/ppermute | solution.py:197
  53.8 10.4 %collective-permute-start.7 = (bf16[128,768]{1,0:T(8,128)(2,1)S(1)}, bf16[128,768]{1,0:T(8,128)(2,1)S(1)}, u32[]{:S(2)}, u32[]{:S(2)}) collective-permute-start(bf16[128,768]{1,0:T(8,128)(2,1)S(1)} %get-tuple-element.43), channel_id=1, source_target_pairs={{0,4},{4,8},{8,12},{12,0},{1,5},{5,9},{9,13},{13,1},{2,6},{6,10},{... | collective-permute-start | bytes 589832 | tf_op jit(solution)/shard_map/ppermute | solution.py:197
  64.9 12.0 %collective-permute-start.10 = (bf16[128,768]{1,0:T(8,128)(2,1)S(1)}, bf16[128,768]{1,0:T(8,128)(2,1)S(1)}, u32[]{:S(2)}, u32[]{:S(2)}) collective-permute-start(bf16[128,768]{1,0:T(8,128)(2,1)S(1)} %shard_map.48.refs_0_), channel_id=1, source_target_pairs={{0,4},{4,8},{8,12},{12,0},{1,5},{5,9},{9,13},{13,1},{2,6},{6,10},{... | collective-permute-start | bytes 589832 | tf_op jit(solution)/shard_map/ppermute | solution.py:197
  66.0 10.9 %collective-permute-start.9 = (bf16[128,768]{1,0:T(8,128)(2,1)S(1)}, bf16[128,768]{1,0:T(8,128)(2,1)S(1)}, u32[]{:S(2)}, u32[]{:S(2)}) collective-permute-start(bf16[128,768]{1,0:T(8,128)(2,1)S(1)} %shard_map.48.refs_0_), channel_id=1, source_target_pairs={{0,8},{4,12},{8,0},{12,4},{1,9},{5,13},{9,1},{13,5},{2,10},{6,14},... | collective-permute-start | bytes 589832 | tf_op jit(solution)/shard_map/ppermute | solution.py:197
  67.5 10.0 %collective-permute-start.8 = (bf16[128,768]{1,0:T(8,128)(2,1)S(1)}, bf16[128,768]{1,0:T(8,128)(2,1)S(1)}, u32[]{:S(2)}, u32[]{:S(2)}) collective-permute-start(bf16[128,768]{1,0:T(8,128)(2,1)S(1)} %shard_map.48.refs_0_), channel_id=1, source_target_pairs={{0,12},{4,0},{8,4},{12,8},{1,13},{5,1},{9,5},{13,9},{2,14},{6,2},{... | collective-permute-start | bytes 589832 | tf_op jit(solution)/shard_map/ppermute | solution.py:197
  77.6 0.7 copy-start.3
  78.2 3.4 %copy-start = (bf16[2048,2048]{1,0:T(8,128)(2,1)S(1)}, bf16[2048,2048]{1,0:T(8,128)(2,1)}, u32[]{:S(2)}) copy-start(bf16[2048,2048]{1,0:T(8,128)(2,1)} %all-gather.2.cloned.1.call-done.gathered_ref.refs_0_) | copy-start | bytes 25165828
  81.6 22.7 %slice-start = ((s8[8388608]{0:T(1024)(128)(4,1)}), s8[4194304]{0:T(1024)(128)(4,1)S(1)}, s32[]{:S(2)}) async-start(s8[8388608]{0:T(1024)(128)(4,1)} %bitcast.4), calls=%async_computation.2 | async-start | bytes 8388608
  83.8 10.5 %collective-permute-start.11 = (bf16[64,1280]{1,0:T(8,128)(2,1)S(1)}, bf16[64,1280]{1,0:T(8,128)(2,1)S(1)}, u32[]{:S(2)}, u32[]{:S(2)}) collective-permute-start(bf16[64,1280]{1,0:T(8,128)(2,1)S(1)} %get-tuple-element.50), channel_id=1, source_target_pairs={{0,12},{4,0},{8,4},{12,8},{1,13},{5,1},{9,5},{13,9},{2,14},{6,2},{... | collective-permute-start | bytes 491528 | tf_op jit(solution)/shard_map/ppermute | solution.py:197
  86.5 8.6 %collective-permute-start.12 = (bf16[64,1280]{1,0:T(8,128)(2,1)S(1)}, bf16[64,1280]{1,0:T(8,128)(2,1)S(1)}, u32[]{:S(2)}, u32[]{:S(2)}) collective-permute-start(bf16[64,1280]{1,0:T(8,128)(2,1)S(1)} %get-tuple-element.51), channel_id=1, source_target_pairs={{0,8},{4,12},{8,0},{12,4},{1,9},{5,13},{9,1},{13,5},{2,10},{6,14},... | collective-permute-start | bytes 491528 | tf_op jit(solution)/shard_map/ppermute | solution.py:197
  86.6 17.7 %slice-start.1 = ((s8[8388608]{0:T(1024)(128)(4,1)}), s8[4194304]{0:T(1024)(128)(4,1)S(1)}, s32[]{:S(2)}) async-start(s8[8388608]{0:T(1024)(128)(4,1)} %bitcast.4), calls=%async_computation.3 | async-start | bytes 8388608
  86.6 17.7 %copy-start.8 = (f32[64,2048]{1,0:T(8,128)S(1)}, f32[64,2048]{1,0:T(8,128)}, u32[]{:S(2)}) copy-start(f32[64,2048]{1,0:T(8,128)} %copy-done.7) | copy-start | bytes 1572868
  86.6 11.4 %collective-permute-start.13 = (bf16[64,1280]{1,0:T(8,128)(2,1)S(1)}, bf16[64,1280]{1,0:T(8,128)(2,1)S(1)}, u32[]{:S(2)}, u32[]{:S(2)}) collective-permute-start(bf16[64,1280]{1,0:T(8,128)(2,1)S(1)} %get-tuple-element.52), channel_id=1, source_target_pairs={{0,4},{4,8},{8,12},{12,0},{1,5},{5,9},{9,13},{13,1},{2,6},{6,10},{... | collective-permute-start | bytes 491528 | tf_op jit(solution)/shard_map/ppermute | solution.py:197
  89.6 11.8 %collective-permute-start.20 = (bf16[64,1280]{1,0:T(8,128)(2,1)S(1)}, bf16[64,1280]{1,0:T(8,128)(2,1)S(1)}, u32[]{:S(2)}, u32[]{:S(2)}) collective-permute-start(bf16[64,1280]{1,0:T(8,128)(2,1)S(1)} %get-tuple-element.58), channel_id=1, source_target_pairs={{0,12},{4,0},{8,4},{12,8},{1,13},{5,1},{9,5},{13,9},{2,14},{6,2},{... | collective-permute-start | bytes 491528 | tf_op jit(solution)/shard_map/ppermute | solution.py:197
  92.1 13.5 %collective-permute-start.21 = (bf16[64,1280]{1,0:T(8,128)(2,1)S(1)}, bf16[64,1280]{1,0:T(8,128)(2,1)S(1)}, u32[]{:S(2)}, u32[]{:S(2)}) collective-permute-start(bf16[64,1280]{1,0:T(8,128)(2,1)S(1)} %get-tuple-element.59), channel_id=1, source_target_pairs={{0,8},{4,12},{8,0},{12,4},{1,9},{5,13},{9,1},{13,5},{2,10},{6,14},... | collective-permute-start | bytes 491528 | tf_op jit(solution)/shard_map/ppermute | solution.py:197
  94.2 11.4 %collective-permute-start.22 = (bf16[64,1280]{1,0:T(8,128)(2,1)S(1)}, bf16[64,1280]{1,0:T(8,128)(2,1)S(1)}, u32[]{:S(2)}, u32[]{:S(2)}) collective-permute-start(bf16[64,1280]{1,0:T(8,128)(2,1)S(1)} %get-tuple-element.60), channel_id=1, source_target_pairs={{0,4},{4,8},{8,12},{12,0},{1,5},{5,9},{9,13},{13,1},{2,6},{6,10},{... | collective-permute-start | bytes 491528 | tf_op jit(solution)/shard_map/ppermute | solution.py:197
  98.7 9.7 %collective-permute-start.16 = (bf16[64,1280]{1,0:T(8,128)(2,1)S(1)}, bf16[64,1280]{1,0:T(8,128)(2,1)S(1)}, u32[]{:S(2)}, u32[]{:S(2)}) collective-permute-start(bf16[64,1280]{1,0:T(8,128)(2,1)S(1)} %shard_map.51.refs_4_), channel_id=1, source_target_pairs={{0,4},{4,8},{8,12},{12,0},{1,5},{5,9},{9,13},{13,1},{2,6},{6,10},{... | collective-permute-start | bytes 491528 | tf_op jit(solution)/shard_map/ppermute | solution.py:197
  98.8 13.9 %collective-permute-start.15 = (bf16[64,1280]{1,0:T(8,128)(2,1)S(1)}, bf16[64,1280]{1,0:T(8,128)(2,1)S(1)}, u32[]{:S(2)}, u32[]{:S(2)}) collective-permute-start(bf16[64,1280]{1,0:T(8,128)(2,1)S(1)} %shard_map.51.refs_4_), channel_id=1, source_target_pairs={{0,8},{4,12},{8,0},{12,4},{1,9},{5,13},{9,1},{13,5},{2,10},{6,14},... | collective-permute-start | bytes 491528 | tf_op jit(solution)/shard_map/ppermute | solution.py:197
  101.3 11.4 %collective-permute-start.14 = (bf16[64,1280]{1,0:T(8,128)(2,1)S(1)}, bf16[64,1280]{1,0:T(8,128)(2,1)S(1)}, u32[]{:S(2)}, u32[]{:S(2)}) collective-permute-start(bf16[64,1280]{1,0:T(8,128)(2,1)S(1)} %shard_map.51.refs_4_), channel_id=1, source_target_pairs={{0,12},{4,0},{8,4},{12,8},{1,13},{5,1},{9,5},{13,9},{2,14},{6,2},{... | collective-permute-start | bytes 491528 | tf_op jit(solution)/shard_map/ppermute | solution.py:197
  104.3 8.3 %copy-start.4 = (bf16[128,768]{1,0:T(8,128)(2,1)S(1)}, bf16[128,768]{1,0:T(8,128)(2,1)}, u32[]{:S(2)}) copy-start(bf16[128,768]{1,0:T(8,128)(2,1)} %copy-done.3) | copy-start | bytes 589828
  104.4 8.3 %copy-start.6 = (f32[16,2048]{1,0:T(8,128)S(1)}, f32[16,2048]{1,0:T(8,128)}, u32[]{:S(2)}) copy-start(f32[16,2048]{1,0:T(8,128)} %copy-done.5) | copy-start | bytes 393220
  106.3 13.4 %collective-permute-start.25 = (bf16[64,1280]{1,0:T(8,128)(2,1)S(1)}, bf16[64,1280]{1,0:T(8,128)(2,1)S(1)}, u32[]{:S(2)}, u32[]{:S(2)}) collective-permute-start(bf16[64,1280]{1,0:T(8,128)(2,1)S(1)} %shard_map.54.refs_4_), channel_id=1, source_target_pairs={{0,4},{4,8},{8,12},{12,0},{1,5},{5,9},{9,13},{13,1},{2,6},{6,10},{... | collective-permute-start | bytes 491528 | tf_op jit(solution)/shard_map/ppermute | solution.py:197
  106.4 14.2 %collective-permute-start.24 = (bf16[64,1280]{1,0:T(8,128)(2,1)S(1)}, bf16[64,1280]{1,0:T(8,128)(2,1)S(1)}, u32[]{:S(2)}, u32[]{:S(2)}) collective-permute-start(bf16[64,1280]{1,0:T(8,128)(2,1)S(1)} %shard_map.54.refs_4_), channel_id=1, source_target_pairs={{0,8},{4,12},{8,0},{12,4},{1,9},{5,13},{9,1},{13,5},{2,10},{6,14},... | collective-permute-start | bytes 491528 | tf_op jit(solution)/shard_map/ppermute | solution.py:197
  108.4 12.2 %collective-permute-start.23 = (bf16[64,1280]{1,0:T(8,128)(2,1)S(1)}, bf16[64,1280]{1,0:T(8,128)(2,1)S(1)}, u32[]{:S(2)}, u32[]{:S(2)}) collective-permute-start(bf16[64,1280]{1,0:T(8,128)(2,1)S(1)} %shard_map.54.refs_4_), channel_id=1, source_target_pairs={{0,12},{4,0},{8,4},{12,8},{1,13},{5,1},{9,5},{13,9},{2,14},{6,2},{... | collective-permute-start | bytes 491528 | tf_op jit(solution)/shard_map/ppermute | solution.py:197
  116.0 12.2 %collective-permute-start.17 = (bf16[256,512]{1,0:T(8,128)(2,1)S(1)}, bf16[256,512]{1,0:T(8,128)(2,1)S(1)}, u32[]{:S(2)}, u32[]{:S(2)}) collective-permute-start(bf16[256,512]{1,0:T(8,128)(2,1)S(1)} %get-tuple-element.54), channel_id=1, source_target_pairs={{0,3},{1,0},{2,1},{3,2},{4,7},{5,4},{6,5},{7,6},{8,11},{9,8},{10,9... | collective-permute-start | bytes 786440 | tf_op jit(solution)/shard_map/ppermute | solution.py:197
  118.9 10.8 %collective-permute-start.18 = (bf16[256,512]{1,0:T(8,128)(2,1)S(1)}, bf16[256,512]{1,0:T(8,128)(2,1)S(1)}, u32[]{:S(2)}, u32[]{:S(2)}) collective-permute-start(bf16[256,512]{1,0:T(8,128)(2,1)S(1)} %get-tuple-element.55), channel_id=1, source_target_pairs={{0,2},{1,3},{2,0},{3,1},{4,6},{5,7},{6,4},{7,5},{8,10},{9,11},{10,... | collective-permute-start | bytes 786440 | tf_op jit(solution)/shard_map/ppermute | solution.py:197
  119.7 16.1 %collective-permute-start.19 = (bf16[256,512]{1,0:T(8,128)(2,1)S(1)}, bf16[256,512]{1,0:T(8,128)(2,1)S(1)}, u32[]{:S(2)}, u32[]{:S(2)}) collective-permute-start(bf16[256,512]{1,0:T(8,128)(2,1)S(1)} %get-tuple-element.56), channel_id=1, source_target_pairs={{0,1},{1,2},{2,3},{3,0},{4,5},{5,6},{6,7},{7,4},{8,9},{9,10},{10,1... | collective-permute-start | bytes 786440 | tf_op jit(solution)/shard_map/ppermute | solution.py:197
  123.8 15.3 %collective-permute-start.26 = (bf16[256,512]{1,0:T(8,128)(2,1)S(1)}, bf16[256,512]{1,0:T(8,128)(2,1)S(1)}, u32[]{:S(2)}, u32[]{:S(2)}) collective-permute-start(bf16[256,512]{1,0:T(8,128)(2,1)S(1)} %get-tuple-element.62), channel_id=1, source_target_pairs={{0,3},{1,0},{2,1},{3,2},{4,7},{5,4},{6,5},{7,6},{8,11},{9,8},{10,9... | collective-permute-start | bytes 786440 | tf_op jit(solution)/shard_map/ppermute | solution.py:197
  126.3 13.9 %collective-permute-start.27 = (bf16[256,512]{1,0:T(8,128)(2,1)S(1)}, bf16[256,512]{1,0:T(8,128)(2,1)S(1)}, u32[]{:S(2)}, u32[]{:S(2)}) collective-permute-start(bf16[256,512]{1,0:T(8,128)(2,1)S(1)} %get-tuple-element.63), channel_id=1, source_target_pairs={{0,2},{1,3},{2,0},{3,1},{4,6},{5,7},{6,4},{7,5},{8,10},{9,11},{10,... | collective-permute-start | bytes 786440 | tf_op jit(solution)/shard_map/ppermute | solution.py:197
  128.1 14.7 %collective-permute-start.28 = (bf16[256,512]{1,0:T(8,128)(2,1)S(1)}, bf16[256,512]{1,0:T(8,128)(2,1)S(1)}, u32[]{:S(2)}, u32[]{:S(2)}) collective-permute-start(bf16[256,512]{1,0:T(8,128)(2,1)S(1)} %get-tuple-element.64), channel_id=1, source_target_pairs={{0,1},{1,2},{2,3},{3,0},{4,5},{5,6},{6,7},{7,4},{8,9},{9,10},{10,1... | collective-permute-start | bytes 786440 | tf_op jit(solution)/shard_map/ppermute | solution.py:197
Sparse Core Ops, SparseCore 0:
  9.2 63.9 all-gather.1

commit v6 on v5

--- a/solution.py
+++ b/solution.py
@@ -20,7 +20,7 @@
 HALVES = 2
 
 
-def call(kernel, out_shape, n_in, scratch=(), flops=0, byts=0, mib=24, aliases={}):
+def call(kernel, out_shape, n_in, scratch=(), flops=0, byts=0, mib=16, aliases={}):
     return pl.pallas_call(
         kernel,
         out_shape=out_shape,

time: 152 us -> 152 us (level)
  no operation moved by 1% of the time
where the time goes in v6:
time: 152 us; the launch traced here: 151 us
  waiting for transfers between devices  56.7 us (37%)
  starting transfers between devices  48.1 us (32%)
  Pallas kernels  22.2 us (15%)
  between operations  13.6 us (9%)
  local copies, waits for them, and re-layouts  9.04 us (6%)
  other arithmetic  1.56 us (1%)
    ppermute x26, waiting for transfers between devices, shift(): lax.ppermute(array, axis, [(i, (i + step) % size) for i in range(size)])  47.6 us
    ppermute x26, starting transfers between devices, shift(): lax.ppermute(array, axis, [(i, (i + step) % size) for i in range(size)])  35.7 us
    all_to_all x1, starting transfers between devices, gather_patterns(): lax.all_to_all(jnp.broadcast_to(both, (64, 16, 128)), ('row', 'col'), 0, 0)  11.8 us
    all_to_all x1, waiting for transfers between devices, gather_patterns(): lax.all_to_all(jnp.broadcast_to(both, (64, 16, 128)), ('row', 'col'), 0, 0)  9.09 us
    pallas_call x3, Pallas kernels, start(): call(functools.partial(product_one_kernel, slots, halves, half, len(held)...  7.95 us
    pallas_call x2, Pallas kernels, body(): call(functools.partial(product_two_kernel, half, len(first)), (shape(heig...  6.5 us
    unnamed x26, local copies, waits for them, and re-layouts  6.4 us
    pallas_call x1, Pallas kernels, body(): call(prep_kernel, (shape(512, 2048), shape(64, 2048, dtype=F32), shape(64...  3.07 us
  transfers between devices with their start and end apart: 31, of which 16 were waited for; matrix products, arithmetic and copies ran while one was open for 2% of the time, Pallas kernels for 12%

profile of v6, /device:TPU:32, one launch (start us, length us, event | category | flops | bytes accessed | tf_op | source)
XLA Modules:
  0.0 151.2 jit_solution(7354463810568242403)
XLA Ops:
  6.5 1.9 %constant_dynamic-slice_fusion.refs_0_ = bf16[128,2048]{1,0:T(8,128)(2,1)} fusion(bf16[512,2048]{1,0:T(8,128)(2,1)} %refs_3_.1, s32[]{:T(128)S(6)} %select_n.16), kind=kLoop, calls=%fused_computation.2 | loop fusion | bytes 1048580 | tf_op jit(solution)/shard_map/dynamic_slice | solution.py:217
  8.5 1.9 %collective-permute-start.3 = (bf16[128,2048]{1,0:T(8,128)(2,1)}, bf16[128,2048]{1,0:T(8,128)(2,1)}, u32[]{:S(2)}, u32[]{:S(2)}) collective-permute-start(bf16[128,2048]{1,0:T(8,128)(2,1)} %constant_dynamic-slice_fusion.refs_0_), channel_id=1, source_target_pairs={{0,224},{16,240},{32,0},{48,16},{64,32},{80,48},{96,64},{112,80},{... | collective-permute-start | bytes 1572872 | tf_op jit(solution)/shard_map/ppermute | solution.py:197
  10.4 0.2 collective-permute-start.1
  10.6 0.7 convert.7
  11.3 0.7 convert.6
  12.0 0.1 pad_maximum_fusion
  12.0 0.7 broadcast_in_dim.3
  12.8 11.8 %all-to-all-start = ((bf16[64,16,128]{2,1,0:T(8,128)(2,1)}), bf16[64,16,128]{2,1,0:T(8,128)(2,1)S(1)}, u32[]{:S(2)}, u32[]{:S(2)}) async-start(bf16[64,16,128]{2,1,0:T(8,128)(2,1)} %broadcast_in_dim.3), calls=%async_computation | async-start | bytes 524288 | tf_op jit(solution)/shard_map/all_to_all | solution.py:211
  24.6 0.2 collective-permute-start
  24.8 0.4 collective-permute-start.4
  25.2 7.2 %collective-permute-done.1.refs_2_ = bf16[128,2048]{1,0:T(8,128)(2,1)} collective-permute-done((bf16[128,2048]{1,0:T(8,128)(2,1)}, bf16[128,2048]{1,0:T(8,128)(2,1)}, u32[]{:S(2)}, u32[]{:S(2)}) %collective-permute-start.1) | collective-permute-done | bytes 524320 | tf_op jit(solution)/shard_map/ppermute | solution.py:197
  32.4 0.1 pad_add_fusion.s_ref
  32.5 9.1 %all-to-all-done.refs_0_ = bf16[64,16,128]{2,1,0:T(8,128)(2,1)S(1)} async-done(((bf16[64,16,128]{2,1,0:T(8,128)(2,1)}), bf16[64,16,128]{2,1,0:T(8,128)(2,1)S(1)}, u32[]{:S(2)}, u32[]{:S(2)}) %all-to-all-start) | async-done | bytes 262176 | tf_op jit(solution)/shard_map/all_to_all | solution.py:211
  41.5 1.6 %copy-done.1 = bf16[512,2048]{1,0:T(8,128)(2,1)S(1)} copy-done((bf16[512,2048]{1,0:T(8,128)(2,1)S(1)}, bf16[512,2048]{1,0:T(8,128)(2,1)}, u32[]{:S(2)}) %copy-start.1) | copy-done | bytes 2097176
  43.1 0.7 copy-done.10
  43.8 3.1 %shard_map.46 = (bf16[512,2048]{1,0:T(8,128)(2,1)S(1)}, f32[64,2048]{1,0:T(8,128)S(1)}, f32[64,2048]{1,0:T(8,128)S(1)}, f32[16,2048]{1,0:T(8,128)S(1)}, f32[16,2048]{1,0:T(8,128)S(1)}) custom-call(s32[4]{0:T(128)S(1)} %pad_add_fusion.s_ref, bf16[64,16,128]{2,1,0:T(8,128)(2,1)S(1)} %all-to-all-done.refs_0_, s32[16,64]{1,0:T(8,128)S(1)} %copy-done.9, ...), custom_call_target="tpu_custom_call" | custom-call | flops 209715200 | bytes 6291456 | tf_op jit(solution)/shard_map/pallas_call | solution.py:224
  47.0 3.7 %shard_map.47 = (f32[128,768]{1,0:T(8,128)S(1)}, bf16[128,768]{1,0:T(8,128)(2,1)S(1)}, bf16[128,768]{1,0:T(8,128)(2,1)S(1)}, bf16[128,768]{1,0:T(8,128)(2,1)S(1)}) custom-call(s32[4]{0:T(128)S(1)} %pad_add_fusion.s_ref, bf16[512,2048]{1,0:T(8,128)(2,1)S(1)} %get-tuple-element.38.left_ref.refs_0_, f32[64,2048]{1,0:T(8,128)S(1)} %get-tuple-element.39.mt_ref.refs_1_, ...), custom_call_target="tpu_custom_call" | custom-call | flops 1610612736 | bytes 5242880 | tf_op jit(solution)/shard_map/pallas_call | solution.py:242
  50.7 2.3 %collective-permute-start.5 = (bf16[128,768]{1,0:T(8,128)(2,1)S(1)}, bf16[128,768]{1,0:T(8,128)(2,1)S(1)}, u32[]{:S(2)}, u32[]{:S(2)}) collective-permute-start(bf16[128,768]{1,0:T(8,128)(2,1)S(1)} %get-tuple-element.41), channel_id=1, source_target_pairs={{0,12},{4,0},{8,4},{12,8},{1,13},{5,1},{9,5},{13,9},{2,14},{6,2},{... | collective-permute-start | bytes 589832 | tf_op jit(solution)/shard_map/ppermute | solution.py:197
  53.0 0.8 collective-permute-start.6
  53.8 0.1 collective-permute-start.7
  53.9 4.6 %collective-permute-done.5.a_ref = bf16[128,768]{1,0:T(8,128)(2,1)S(1)} collective-permute-done((bf16[128,768]{1,0:T(8,128)(2,1)S(1)}, bf16[128,768]{1,0:T(8,128)(2,1)S(1)}, u32[]{:S(2)}, u32[]{:S(2)}) %collective-permute-start.5) | collective-permute-done | bytes 196640 | tf_op jit(solution)/shard_map/ppermute | solution.py:197
  58.6 3.6 %collective-permute-done.6.b_ref = bf16[128,768]{1,0:T(8,128)(2,1)S(1)} collective-permute-done((bf16[128,768]{1,0:T(8,128)(2,1)S(1)}, bf16[128,768]{1,0:T(8,128)(2,1)S(1)}, u32[]{:S(2)}, u32[]{:S(2)}) %collective-permute-start.6) | collective-permute-done | bytes 196640 | tf_op jit(solution)/shard_map/ppermute | solution.py:197
  62.2 2.1 %collective-permute-done.7.c_ref = bf16[128,768]{1,0:T(8,128)(2,1)S(1)} collective-permute-done((bf16[128,768]{1,0:T(8,128)(2,1)S(1)}, bf16[128,768]{1,0:T(8,128)(2,1)S(1)}, u32[]{:S(2)}, u32[]{:S(2)}) %collective-permute-start.7) | collective-permute-done | bytes 196640 | tf_op jit(solution)/shard_map/ppermute | solution.py:197
  64.3 0.7 shard_map.48.refs_0_
  64.9 1.1 collective-permute-start.10
  66.0 1.5 %collective-permute-start.9 = (bf16[128,768]{1,0:T(8,128)(2,1)S(1)}, bf16[128,768]{1,0:T(8,128)(2,1)S(1)}, u32[]{:S(2)}, u32[]{:S(2)}) collective-permute-start(bf16[128,768]{1,0:T(8,128)(2,1)S(1)} %shard_map.48.refs_0_), channel_id=1, source_target_pairs={{0,8},{4,12},{8,0},{12,4},{1,9},{5,13},{9,1},{13,5},{2,10},{6,14},... | collective-permute-start | bytes 589832 | tf_op jit(solution)/shard_map/ppermute | solution.py:197
  67.5 1.8 %collective-permute-start.8 = (bf16[128,768]{1,0:T(8,128)(2,1)S(1)}, bf16[128,768]{1,0:T(8,128)(2,1)S(1)}, u32[]{:S(2)}, u32[]{:S(2)}) collective-permute-start(bf16[128,768]{1,0:T(8,128)(2,1)S(1)} %shard_map.48.refs_0_), channel_id=1, source_target_pairs={{0,12},{4,0},{8,4},{12,8},{1,13},{5,1},{9,5},{13,9},{2,14},{6,2},{... | collective-permute-start | bytes 589832 | tf_op jit(solution)/shard_map/ppermute | solution.py:197
  69.4 7.6 %collective-permute-done.10.refs_3_ = bf16[128,768]{1,0:T(8,128)(2,1)S(1)} collective-permute-done((bf16[128,768]{1,0:T(8,128)(2,1)S(1)}, bf16[128,768]{1,0:T(8,128)(2,1)S(1)}, u32[]{:S(2)}, u32[]{:S(2)}) %collective-permute-start.10) | collective-permute-done | bytes 196640 | tf_op jit(solution)/shard_map/ppermute | solution.py:197
  76.9 0.6 collective-permute-done.8.refs_1_
  77.6 0.7 copy-done.3
  78.2 3.4 %copy-done = bf16[2048,2048]{1,0:T(8,128)(2,1)S(1)} copy-done((bf16[2048,2048]{1,0:T(8,128)(2,1)S(1)}, bf16[2048,2048]{1,0:T(8,128)(2,1)}, u32[]{:S(2)}) %copy-start) | copy-done | bytes 8388632
  81.6 2.1 %shard_map.50 = (f32[64,1280]{1,0:T(8,128)S(1)}, bf16[64,1280]{1,0:T(8,128)(2,1)S(1)}, bf16[64,1280]{1,0:T(8,128)(2,1)S(1)}, bf16[64,1280]{1,0:T(8,128)(2,1)S(1)}) custom-call(s32[4]{0:T(128)S(1)} %pad_add_fusion.s_ref, bf16[512,2048]{1,0:T(8,128)(2,1)S(1)} %get-tuple-element.38.left_ref.refs_0_, f32[64,2048]{1,0:T(8,128)S(1)} %get-tuple-element.39.mt_ref.refs_1_, ...), custom_call_target="tpu_custom_call" | custom-call | flops 1342177280 | bytes 7340032 | tf_op jit(solution)/shard_map/pallas_call | solution.py:242
  83.8 2.7 %collective-permute-start.11 = (bf16[64,1280]{1,0:T(8,128)(2,1)S(1)}, bf16[64,1280]{1,0:T(8,128)(2,1)S(1)}, u32[]{:S(2)}, u32[]{:S(2)}) collective-permute-start(bf16[64,1280]{1,0:T(8,128)(2,1)S(1)} %get-tuple-element.50), channel_id=1, source_target_pairs={{0,12},{4,0},{8,4},{12,8},{1,13},{5,1},{9,5},{13,9},{2,14},{6,2},{... | collective-permute-start | bytes 491528 | tf_op jit(solution)/shard_map/ppermute | solution.py:197
  86.5 0.2 collective-permute-start.12
  86.6 0.8 collective-permute-start.13
  87.4 2.1 %shard_map.53 = (f32[64,1280]{1,0:T(8,128)S(1)}, bf16[64,1280]{1,0:T(8,128)(2,1)S(1)}, bf16[64,1280]{1,0:T(8,128)(2,1)S(1)}, bf16[64,1280]{1,0:T(8,128)(2,1)S(1)}) custom-call(s32[4]{0:T(128)S(1)} %pad_add_fusion.s_ref, bf16[512,2048]{1,0:T(8,128)(2,1)S(1)} %get-tuple-element.38.left_ref.refs_0_, f32[64,2048]{1,0:T(8,128)S(1)} %get-tuple-element.39.mt_ref.refs_1_, ...), custom_call_target="tpu_custom_call" | custom-call | flops 1342177280 | bytes 7340032 | tf_op jit(solution)/shard_map/pallas_call | solution.py:242
  89.6 2.5 %collective-permute-start.20 = (bf16[64,1280]{1,0:T(8,128)(2,1)S(1)}, bf16[64,1280]{1,0:T(8,128)(2,1)S(1)}, u32[]{:S(2)}, u32[]{:S(2)}) collective-permute-start(bf16[64,1280]{1,0:T(8,128)(2,1)S(1)} %get-tuple-element.58), channel_id=1, source_target_pairs={{0,12},{4,0},{8,4},{12,8},{1,13},{5,1},{9,5},{13,9},{2,14},{6,2},{... | collective-permute-start | bytes 491528 | tf_op jit(solution)/shard_map/ppermute | solution.py:197
  92.1 2.2 %collective-permute-start.21 = (bf16[64,1280]{1,0:T(8,128)(2,1)S(1)}, bf16[64,1280]{1,0:T(8,128)(2,1)S(1)}, u32[]{:S(2)}, u32[]{:S(2)}) collective-permute-start(bf16[64,1280]{1,0:T(8,128)(2,1)S(1)} %get-tuple-element.59), channel_id=1, source_target_pairs={{0,8},{4,12},{8,0},{12,4},{1,9},{5,13},{9,1},{13,5},{2,10},{6,14},... | collective-permute-start | bytes 491528 | tf_op jit(solution)/shard_map/ppermute | solution.py:197
  94.2 0.8 collective-permute-done.12.b_ref
  95.1 3.0 %collective-permute-done.13.c_ref = bf16[64,1280]{1,0:T(8,128)(2,1)S(1)} collective-permute-done((bf16[64,1280]{1,0:T(8,128)(2,1)S(1)}, bf16[64,1280]{1,0:T(8,128)(2,1)S(1)}, u32[]{:S(2)}, u32[]{:S(2)}) %collective-permute-start.13) | collective-permute-done | bytes 163872 | tf_op jit(solution)/shard_map/ppermute | solution.py:197
  98.1 0.6 shard_map.51.refs_4_
  98.7 0.1 collective-permute-start.16
  98.8 2.5 %collective-permute-start.15 = (bf16[64,1280]{1,0:T(8,128)(2,1)S(1)}, bf16[64,1280]{1,0:T(8,128)(2,1)S(1)}, u32[]{:S(2)}, u32[]{:S(2)}) collective-permute-start(bf16[64,1280]{1,0:T(8,128)(2,1)S(1)} %shard_map.51.refs_4_), channel_id=1, source_target_pairs={{0,8},{4,12},{8,0},{12,4},{1,9},{5,13},{9,1},{13,5},{2,10},{6,14},... | collective-permute-start | bytes 491528 | tf_op jit(solution)/shard_map/ppermute | solution.py:197
  101.3 3.0 %collective-permute-start.14 = (bf16[64,1280]{1,0:T(8,128)(2,1)S(1)}, bf16[64,1280]{1,0:T(8,128)(2,1)S(1)}, u32[]{:S(2)}, u32[]{:S(2)}) collective-permute-start(bf16[64,1280]{1,0:T(8,128)(2,1)S(1)} %shard_map.51.refs_4_), channel_id=1, source_target_pairs={{0,12},{4,0},{8,4},{12,8},{1,13},{5,1},{9,5},{13,9},{2,14},{6,2},{... | collective-permute-start | bytes 491528 | tf_op jit(solution)/shard_map/ppermute | solution.py:197
  104.4 1.3 shard_map.49.right_ref
  105.7 0.6 shard_map.54.refs_4_
  106.3 0.1 collective-permute-start.25
  106.4 2.0 %collective-permute-start.24 = (bf16[64,1280]{1,0:T(8,128)(2,1)S(1)}, bf16[64,1280]{1,0:T(8,128)(2,1)S(1)}, u32[]{:S(2)}, u32[]{:S(2)}) collective-permute-start(bf16[64,1280]{1,0:T(8,128)(2,1)S(1)} %shard_map.54.refs_4_), channel_id=1, source_target_pairs={{0,8},{4,12},{8,0},{12,4},{1,9},{5,13},{9,1},{13,5},{2,10},{6,14},... | collective-permute-start | bytes 491528 | tf_op jit(solution)/shard_map/ppermute | solution.py:197
  108.4 1.3 collective-permute-start.23
  109.7 2.9 %collective-permute-done.15.refs_6_ = bf16[64,1280]{1,0:T(8,128)(2,1)S(1)} collective-permute-done((bf16[64,1280]{1,0:T(8,128)(2,1)S(1)}, bf16[64,1280]{1,0:T(8,128)(2,1)S(1)}, u32[]{:S(2)}, u32[]{:S(2)}) %collective-permute-start.15) | collective-permute-done | bytes 163872 | tf_op jit(solution)/shard_map/ppermute | solution.py:197
  112.7 3.3 %shard_map.52 = (f32[256,512]{1,0:T(8,128)S(1)}, bf16[256,512]{1,0:T(8,128)(2,1)S(1)}, bf16[256,512]{1,0:T(8,128)(2,1)S(1)}, bf16[256,512]{1,0:T(8,128)(2,1)S(1)}) custom-call(s32[4]{0:T(128)S(1)} %pad_add_fusion.s_ref, f32[16,2048]{1,0:T(8,128)S(1)} %copy-done.6, bf16[2048,2048]{1,0:T(8,128)(2,1)S(1)} %shard_map.49.right_ref, ...), custom_call_target="tpu_custom_call" | custom-call | flops 2147483648 | bytes 10485760 | tf_op jit(solution)/shard_map/pallas_call | solution.py:266
  116.0 2.9 %collective-permute-start.17 = (bf16[256,512]{1,0:T(8,128)(2,1)S(1)}, bf16[256,512]{1,0:T(8,128)(2,1)S(1)}, u32[]{:S(2)}, u32[]{:S(2)}) collective-permute-start(bf16[256,512]{1,0:T(8,128)(2,1)S(1)} %get-tuple-element.54), channel_id=1, source_target_pairs={{0,3},{1,0},{2,1},{3,2},{4,7},{5,4},{6,5},{7,6},{8,11},{9,8},{10,9... | collective-permute-start | bytes 786440 | tf_op jit(solution)/shard_map/ppermute | solution.py:197
  118.9 0.8 collective-permute-start.18
  119.7 0.9 collective-permute-start.19
  120.6 3.2 %shard_map.55 = (f32[256,512]{1,0:T(8,128)S(1)}, bf16[256,512]{1,0:T(8,128)(2,1)S(1)}, bf16[256,512]{1,0:T(8,128)(2,1)S(1)}, bf16[256,512]{1,0:T(8,128)(2,1)S(1)}) custom-call(s32[4]{0:T(128)S(1)} %pad_add_fusion.s_ref, f32[16,2048]{1,0:T(8,128)S(1)} %copy-done.6, bf16[2048,2048]{1,0:T(8,128)(2,1)S(1)} %shard_map.49.right_ref, ...), custom_call_target="tpu_custom_call" | custom-call | flops 2147483648 | bytes 10485760 | tf_op jit(solution)/shard_map/pallas_call | solution.py:266
  123.8 2.4 %collective-permute-start.26 = (bf16[256,512]{1,0:T(8,128)(2,1)S(1)}, bf16[256,512]{1,0:T(8,128)(2,1)S(1)}, u32[]{:S(2)}, u32[]{:S(2)}) collective-permute-start(bf16[256,512]{1,0:T(8,128)(2,1)S(1)} %get-tuple-element.62), channel_id=1, source_target_pairs={{0,3},{1,0},{2,1},{3,2},{4,7},{5,4},{6,5},{7,6},{8,11},{9,8},{10,9... | collective-permute-start | bytes 786440 | tf_op jit(solution)/shard_map/ppermute | solution.py:197
  126.3 1.5 collective-permute-start.27
  127.8 0.3 collective-permute-done.17.refs_1_
  128.1 1.5 %collective-permute-done.18.refs_2_ = bf16[256,512]{1,0:T(8,128)(2,1)S(1)} collective-permute-done((bf16[256,512]{1,0:T(8,128)(2,1)S(1)}, bf16[256,512]{1,0:T(8,128)(2,1)S(1)}, u32[]{:S(2)}, u32[]{:S(2)}) %collective-permute-start.18) | collective-permute-done | bytes 262176 | tf_op jit(solution)/shard_map/ppermute | solution.py:197
  129.7 6.2 %collective-permute-done.19.refs_3_ = bf16[256,512]{1,0:T(8,128)(2,1)S(1)} collective-permute-done((bf16[256,512]{1,0:T(8,128)(2,1)S(1)}, bf16[256,512]{1,0:T(8,128)(2,1)S(1)}, u32[]{:S(2)}, u32[]{:S(2)}) %collective-permute-start.19) | collective-permute-done | bytes 262176 | tf_op jit(solution)/shard_map/ppermute | solution.py:197
  135.8 3.3 %collective-permute-done.26.refs_5_ = bf16[256,512]{1,0:T(8,128)(2,1)S(1)} collective-permute-done((bf16[256,512]{1,0:T(8,128)(2,1)S(1)}, bf16[256,512]{1,0:T(8,128)(2,1)S(1)}, u32[]{:S(2)}, u32[]{:S(2)}) %collective-permute-start.26) | collective-permute-done | bytes 262176 | tf_op jit(solution)/shard_map/ppermute | solution.py:197
  139.1 1.0 collective-permute-done.27.refs_6_
  140.2 2.7 %collective-permute-done.28.refs_7_ = bf16[256,512]{1,0:T(8,128)(2,1)S(1)} collective-permute-done((bf16[256,512]{1,0:T(8,128)(2,1)S(1)}, bf16[256,512]{1,0:T(8,128)(2,1)S(1)}, u32[]{:S(2)}, u32[]{:S(2)}) %collective-permute-start.28) | collective-permute-done | bytes 262176 | tf_op jit(solution)/shard_map/ppermute | solution.py:197
  142.8 1.6 %shard_map.56 = bf16[512,512]{1,0:T(8,128)(2,1)} custom-call(s32[4]{0:T(128)S(1)} %pad_add_fusion.s_ref, f32[256,512]{1,0:T(8,128)S(1)} %get-tuple-element.53.refs_0_, bf16[256,512]{1,0:T(8,128)(2,1)S(1)} %collective-permute-done.17.refs_1_, bf16[256,512]{1,0:T(8,128)(2,1)S(1)} %collective-permute-done.18.refs_2_, ...), custom_call_target="tpu_custom_call" | custom-call | bytes 3145728 | tf_op jit(solution)/shard_map/pallas_call | solution.py:275
  (43 shorter events, 0.1 us)
Async XLA Ops:
  6.5 35.0 %copy-start.9 = (s32[16,64]{1,0:T(8,128)S(1)}, s32[16,64]{1,0:T(8,128)}, u32[]{:S(2)}) copy-start(s32[16,64]{1,0:T(8,128)} %refs_1_.1) | copy-start | bytes 12292
  6.5 71.7 %all-gather.2.cloned.1.call-start = ((), (), s32[]{:S(2)}) async-start(), calls=%async_computation.1 | async-start | bytes 8912896 | tf_op jit(solution)/shard_map/all_gather | solution.py:219
  8.4 38.5 %copy-start.2 = (bf16[128,2048]{1,0:T(8,128)(2,1)S(1)}, bf16[128,2048]{1,0:T(8,128)(2,1)}, u32[]{:S(2)}) copy-start(bf16[128,2048]{1,0:T(8,128)(2,1)} %constant_dynamic-slice_fusion.refs_0_) | copy-start | bytes 1572868
  8.5 16.3 %collective-permute-start.3 = (bf16[128,2048]{1,0:T(8,128)(2,1)}, bf16[128,2048]{1,0:T(8,128)(2,1)}, u32[]{:S(2)}, u32[]{:S(2)}) collective-permute-start(bf16[128,2048]{1,0:T(8,128)(2,1)} %constant_dynamic-slice_fusion.refs_0_), channel_id=1, source_target_pairs={{0,224},{16,240},{32,0},{48,16},{64,32},{80,48},{96,64},{112,80},{... | collective-permute-start | bytes 1572872 | tf_op jit(solution)/shard_map/ppermute | solution.py:197
  10.4 22.0 %collective-permute-start.1 = (bf16[128,2048]{1,0:T(8,128)(2,1)}, bf16[128,2048]{1,0:T(8,128)(2,1)}, u32[]{:S(2)}, u32[]{:S(2)}) collective-permute-start(bf16[128,2048]{1,0:T(8,128)(2,1)} %constant_dynamic-slice_fusion.refs_0_), channel_id=1, source_target_pairs={{0,32},{16,48},{32,64},{48,80},{64,96},{80,112},{96,128},{112,144}... | collective-permute-start | bytes 1572872 | tf_op jit(solution)/shard_map/ppermute | solution.py:197
  12.8 28.8 %all-to-all-start = ((bf16[64,16,128]{2,1,0:T(8,128)(2,1)}), bf16[64,16,128]{2,1,0:T(8,128)(2,1)S(1)}, u32[]{:S(2)}, u32[]{:S(2)}) async-start(bf16[64,16,128]{2,1,0:T(8,128)(2,1)} %broadcast_in_dim.3), calls=%async_computation | async-start | bytes 524288 | tf_op jit(solution)/shard_map/all_to_all | solution.py:211
  24.6 22.4 %collective-permute-start = (bf16[128,2048]{1,0:T(8,128)(2,1)}, bf16[128,2048]{1,0:T(8,128)(2,1)}, u32[]{:S(2)}, u32[]{:S(2)}) collective-permute-start(bf16[128,2048]{1,0:T(8,128)(2,1)} %constant_dynamic-slice_fusion.refs_0_), channel_id=1, source_target_pairs={{0,16},{16,0},{32,48},{48,32},{64,80},{80,64},{96,112},{112,96},{1... | collective-permute-start | bytes 1572872 | tf_op jit(solution)/shard_map/ppermute | solution.py:201
  24.8 22.1 %collective-permute-start.4 = (bf16[128,2048]{1,0:T(8,128)(2,1)}, bf16[128,2048]{1,0:T(8,128)(2,1)}, u32[]{:S(2)}, u32[]{:S(2)}) collective-permute-start(bf16[128,2048]{1,0:T(8,128)(2,1)} %collective-permute-done.3.refs_4_), channel_id=1, source_target_pairs={{0,16},{16,0},{32,48},{48,32},{64,80},{80,64},{96,112},{112,96},{1... | collective-permute-start | bytes 1572872 | tf_op jit(solution)/shard_map/ppermute | solution.py:201
  32.4 14.6 %collective-permute-start.2 = (bf16[128,2048]{1,0:T(8,128)(2,1)}, bf16[128,2048]{1,0:T(8,128)(2,1)}, u32[]{:S(2)}, u32[]{:S(2)}) collective-permute-start(bf16[128,2048]{1,0:T(8,128)(2,1)} %collective-permute-done.1.refs_2_), channel_id=1, source_target_pairs={{0,16},{16,0},{32,48},{48,32},{64,80},{80,64},{96,112},{112,96},{1... | collective-permute-start | bytes 1572872 | tf_op jit(solution)/shard_map/ppermute | solution.py:201
  41.5 1.6 %copy-start.1 = (bf16[512,2048]{1,0:T(8,128)(2,1)S(1)}, bf16[512,2048]{1,0:T(8,128)(2,1)}, u32[]{:S(2)}) copy-start(bf16[512,2048]{1,0:T(8,128)(2,1)} %refs_3_.1) | copy-start | bytes 6291460
  43.1 0.7 copy-start.10
  46.9 3.8 %copy-start.5 = (f32[16,2048]{1,0:T(8,128)}, f32[16,2048]{1,0:T(8,128)S(1)}, u32[]{:S(2)}) copy-start(f32[16,2048]{1,0:T(8,128)S(1)} %get-tuple-element.35.mc_ref) | copy-start | bytes 393220
  46.9 3.8 %copy-start.7 = (f32[64,2048]{1,0:T(8,128)}, f32[64,2048]{1,0:T(8,128)S(1)}, u32[]{:S(2)}) copy-start(f32[64,2048]{1,0:T(8,128)S(1)} %get-tuple-element.36.mk_ref) | copy-start | bytes 1572868
  50.7 7.9 %collective-permute-start.5 = (bf16[128,768]{1,0:T(8,128)(2,1)S(1)}, bf16[128,768]{1,0:T(8,128)(2,1)S(1)}, u32[]{:S(2)}, u32[]{:S(2)}) collective-permute-start(bf16[128,768]{1,0:T(8,128)(2,1)S(1)} %get-tuple-element.41), channel_id=1, source_target_pairs={{0,12},{4,0},{8,4},{12,8},{1,13},{5,1},{9,5},{13,9},{2,14},{6,2},{... | collective-permute-start | bytes 589832 | tf_op jit(solution)/shard_map/ppermute | solution.py:197
  53.0 9.2 %collective-permute-start.6 = (bf16[128,768]{1,0:T(8,128)(2,1)S(1)}, bf16[128,768]{1,0:T(8,128)(2,1)S(1)}, u32[]{:S(2)}, u32[]{:S(2)}) collective-permute-start(bf16[128,768]{1,0:T(8,128)(2,1)S(1)} %get-tuple-element.42), channel_id=1, source_target_pairs={{0,8},{4,12},{8,0},{12,4},{1,9},{5,13},{9,1},{13,5},{2,10},{6,14},... | collective-permute-start | bytes 589832 | tf_op jit(solution)/shard_map/ppermute | solution.py:197
  53.8 10.4 %collective-permute-start.7 = (bf16[128,768]{1,0:T(8,128)(2,1)S(1)}, bf16[128,768]{1,0:T(8,128)(2,1)S(1)}, u32[]{:S(2)}, u32[]{:S(2)}) collective-permute-start(bf16[128,768]{1,0:T(8,128)(2,1)S(1)} %get-tuple-element.43), channel_id=1, source_target_pairs={{0,4},{4,8},{8,12},{12,0},{1,5},{5,9},{9,13},{13,1},{2,6},{6,10},{... | collective-permute-start | bytes 589832 | tf_op jit(solution)/shard_map/ppermute | solution.py:197
  64.9 12.0 %collective-permute-start.10 = (bf16[128,768]{1,0:T(8,128)(2,1)S(1)}, bf16[128,768]{1,0:T(8,128)(2,1)S(1)}, u32[]{:S(2)}, u32[]{:S(2)}) collective-permute-start(bf16[128,768]{1,0:T(8,128)(2,1)S(1)} %shard_map.48.refs_0_), channel_id=1, source_target_pairs={{0,4},{4,8},{8,12},{12,0},{1,5},{5,9},{9,13},{13,1},{2,6},{6,10},{... | collective-permute-start | bytes 589832 | tf_op jit(solution)/shard_map/ppermute | solution.py:197
  66.0 10.9 %collective-permute-start.9 = (bf16[128,768]{1,0:T(8,128)(2,1)S(1)}, bf16[128,768]{1,0:T(8,128)(2,1)S(1)}, u32[]{:S(2)}, u32[]{:S(2)}) collective-permute-start(bf16[128,768]{1,0:T(8,128)(2,1)S(1)} %shard_map.48.refs_0_), channel_id=1, source_target_pairs={{0,8},{4,12},{8,0},{12,4},{1,9},{5,13},{9,1},{13,5},{2,10},{6,14},... | collective-permute-start | bytes 589832 | tf_op jit(solution)/shard_map/ppermute | solution.py:197
  67.5 10.0 %collective-permute-start.8 = (bf16[128,768]{1,0:T(8,128)(2,1)S(1)}, bf16[128,768]{1,0:T(8,128)(2,1)S(1)}, u32[]{:S(2)}, u32[]{:S(2)}) collective-permute-start(bf16[128,768]{1,0:T(8,128)(2,1)S(1)} %shard_map.48.refs_0_), channel_id=1, source_target_pairs={{0,12},{4,0},{8,4},{12,8},{1,13},{5,1},{9,5},{13,9},{2,14},{6,2},{... | collective-permute-start | bytes 589832 | tf_op jit(solution)/shard_map/ppermute | solution.py:197
  77.6 0.7 copy-start.3
  78.2 3.4 %copy-start = (bf16[2048,2048]{1,0:T(8,128)(2,1)S(1)}, bf16[2048,2048]{1,0:T(8,128)(2,1)}, u32[]{:S(2)}) copy-start(bf16[2048,2048]{1,0:T(8,128)(2,1)} %all-gather.2.cloned.1.call-done.gathered_ref.refs_0_) | copy-start | bytes 25165828
  81.6 22.7 %slice-start = ((s8[8388608]{0:T(1024)(128)(4,1)}), s8[4194304]{0:T(1024)(128)(4,1)S(1)}, s32[]{:S(2)}) async-start(s8[8388608]{0:T(1024)(128)(4,1)} %bitcast.4), calls=%async_computation.2 | async-start | bytes 8388608
  83.8 10.5 %collective-permute-start.11 = (bf16[64,1280]{1,0:T(8,128)(2,1)S(1)}, bf16[64,1280]{1,0:T(8,128)(2,1)S(1)}, u32[]{:S(2)}, u32[]{:S(2)}) collective-permute-start(bf16[64,1280]{1,0:T(8,128)(2,1)S(1)} %get-tuple-element.50), channel_id=1, source_target_pairs={{0,12},{4,0},{8,4},{12,8},{1,13},{5,1},{9,5},{13,9},{2,14},{6,2},{... | collective-permute-start | bytes 491528 | tf_op jit(solution)/shard_map/ppermute | solution.py:197
  86.5 8.6 %collective-permute-start.12 = (bf16[64,1280]{1,0:T(8,128)(2,1)S(1)}, bf16[64,1280]{1,0:T(8,128)(2,1)S(1)}, u32[]{:S(2)}, u32[]{:S(2)}) collective-permute-start(bf16[64,1280]{1,0:T(8,128)(2,1)S(1)} %get-tuple-element.51), channel_id=1, source_target_pairs={{0,8},{4,12},{8,0},{12,4},{1,9},{5,13},{9,1},{13,5},{2,10},{6,14},... | collective-permute-start | bytes 491528 | tf_op jit(solution)/shard_map/ppermute | solution.py:197
  86.6 17.7 %slice-start.1 = ((s8[8388608]{0:T(1024)(128)(4,1)}), s8[4194304]{0:T(1024)(128)(4,1)S(1)}, s32[]{:S(2)}) async-start(s8[8388608]{0:T(1024)(128)(4,1)} %bitcast.4), calls=%async_computation.3 | async-start | bytes 8388608
  86.6 17.7 %copy-start.8 = (f32[64,2048]{1,0:T(8,128)S(1)}, f32[64,2048]{1,0:T(8,128)}, u32[]{:S(2)}) copy-start(f32[64,2048]{1,0:T(8,128)} %copy-done.7) | copy-start | bytes 1572868
  86.6 11.4 %collective-permute-start.13 = (bf16[64,1280]{1,0:T(8,128)(2,1)S(1)}, bf16[64,1280]{1,0:T(8,128)(2,1)S(1)}, u32[]{:S(2)}, u32[]{:S(2)}) collective-permute-start(bf16[64,1280]{1,0:T(8,128)(2,1)S(1)} %get-tuple-element.52), channel_id=1, source_target_pairs={{0,4},{4,8},{8,12},{12,0},{1,5},{5,9},{9,13},{13,1},{2,6},{6,10},{... | collective-permute-start | bytes 491528 | tf_op jit(solution)/shard_map/ppermute | solution.py:197
  89.6 11.8 %collective-permute-start.20 = (bf16[64,1280]{1,0:T(8,128)(2,1)S(1)}, bf16[64,1280]{1,0:T(8,128)(2,1)S(1)}, u32[]{:S(2)}, u32[]{:S(2)}) collective-permute-start(bf16[64,1280]{1,0:T(8,128)(2,1)S(1)} %get-tuple-element.58), channel_id=1, source_target_pairs={{0,12},{4,0},{8,4},{12,8},{1,13},{5,1},{9,5},{13,9},{2,14},{6,2},{... | collective-permute-start | bytes 491528 | tf_op jit(solution)/shard_map/ppermute | solution.py:197
  92.1 13.5 %collective-permute-start.21 = (bf16[64,1280]{1,0:T(8,128)(2,1)S(1)}, bf16[64,1280]{1,0:T(8,128)(2,1)S(1)}, u32[]{:S(2)}, u32[]{:S(2)}) collective-permute-start(bf16[64,1280]{1,0:T(8,128)(2,1)S(1)} %get-tuple-element.59), channel_id=1, source_target_pairs={{0,8},{4,12},{8,0},{12,4},{1,9},{5,13},{9,1},{13,5},{2,10},{6,14},... | collective-permute-start | bytes 491528 | tf_op jit(solution)/shard_map/ppermute | solution.py:197
  94.2 11.4 %collective-permute-start.22 = (bf16[64,1280]{1,0:T(8,128)(2,1)S(1)}, bf16[64,1280]{1,0:T(8,128)(2,1)S(1)}, u32[]{:S(2)}, u32[]{:S(2)}) collective-permute-start(bf16[64,1280]{1,0:T(8,128)(2,1)S(1)} %get-tuple-element.60), channel_id=1, source_target_pairs={{0,4},{4,8},{8,12},{12,0},{1,5},{5,9},{9,13},{13,1},{2,6},{6,10},{... | collective-permute-start | bytes 491528 | tf_op jit(solution)/shard_map/ppermute | solution.py:197
  98.7 9.7 %collective-permute-start.16 = (bf16[64,1280]{1,0:T(8,128)(2,1)S(1)}, bf16[64,1280]{1,0:T(8,128)(2,1)S(1)}, u32[]{:S(2)}, u32[]{:S(2)}) collective-permute-start(bf16[64,1280]{1,0:T(8,128)(2,1)S(1)} %shard_map.51.refs_4_), channel_id=1, source_target_pairs={{0,4},{4,8},{8,12},{12,0},{1,5},{5,9},{9,13},{13,1},{2,6},{6,10},{... | collective-permute-start | bytes 491528 | tf_op jit(solution)/shard_map/ppermute | solution.py:197
  98.8 13.9 %collective-permute-start.15 = (bf16[64,1280]{1,0:T(8,128)(2,1)S(1)}, bf16[64,1280]{1,0:T(8,128)(2,1)S(1)}, u32[]{:S(2)}, u32[]{:S(2)}) collective-permute-start(bf16[64,1280]{1,0:T(8,128)(2,1)S(1)} %shard_map.51.refs_4_), channel_id=1, source_target_pairs={{0,8},{4,12},{8,0},{12,4},{1,9},{5,13},{9,1},{13,5},{2,10},{6,14},... | collective-permute-start | bytes 491528 | tf_op jit(solution)/shard_map/ppermute | solution.py:197
  101.3 11.4 %collective-permute-start.14 = (bf16[64,1280]{1,0:T(8,128)(2,1)S(1)}, bf16[64,1280]{1,0:T(8,128)(2,1)S(1)}, u32[]{:S(2)}, u32[]{:S(2)}) collective-permute-start(bf16[64,1280]{1,0:T(8,128)(2,1)S(1)} %shard_map.51.refs_4_), channel_id=1, source_target_pairs={{0,12},{4,0},{8,4},{12,8},{1,13},{5,1},{9,5},{13,9},{2,14},{6,2},{... | collective-permute-start | bytes 491528 | tf_op jit(solution)/shard_map/ppermute | solution.py:197
  104.3 8.3 %copy-start.4 = (bf16[128,768]{1,0:T(8,128)(2,1)S(1)}, bf16[128,768]{1,0:T(8,128)(2,1)}, u32[]{:S(2)}) copy-start(bf16[128,768]{1,0:T(8,128)(2,1)} %copy-done.3) | copy-start | bytes 589828
  104.4 8.3 %copy-start.6 = (f32[16,2048]{1,0:T(8,128)S(1)}, f32[16,2048]{1,0:T(8,128)}, u32[]{:S(2)}) copy-start(f32[16,2048]{1,0:T(8,128)} %copy-done.5) | copy-start | bytes 393220
  106.3 13.4 %collective-permute-start.25 = (bf16[64,1280]{1,0:T(8,128)(2,1)S(1)}, bf16[64,1280]{1,0:T(8,128)(2,1)S(1)}, u32[]{:S(2)}, u32[]{:S(2)}) collective-permute-start(bf16[64,1280]{1,0:T(8,128)(2,1)S(1)} %shard_map.54.refs_4_), channel_id=1, source_target_pairs={{0,4},{4,8},{8,12},{12,0},{1,5},{5,9},{9,13},{13,1},{2,6},{6,10},{... | collective-permute-start | bytes 491528 | tf_op jit(solution)/shard_map/ppermute | solution.py:197
  106.4 14.2 %collective-permute-start.24 = (bf16[64,1280]{1,0:T(8,128)(2,1)S(1)}, bf16[64,1280]{1,0:T(8,128)(2,1)S(1)}, u32[]{:S(2)}, u32[]{:S(2)}) collective-permute-start(bf16[64,1280]{1,0:T(8,128)(2,1)S(1)} %shard_map.54.refs_4_), channel_id=1, source_target_pairs={{0,8},{4,12},{8,0},{12,4},{1,9},{5,13},{9,1},{13,5},{2,10},{6,14},... | collective-permute-start | bytes 491528 | tf_op jit(solution)/shard_map/ppermute | solution.py:197
  108.4 12.2 %collective-permute-start.23 = (bf16[64,1280]{1,0:T(8,128)(2,1)S(1)}, bf16[64,1280]{1,0:T(8,128)(2,1)S(1)}, u32[]{:S(2)}, u32[]{:S(2)}) collective-permute-start(bf16[64,1280]{1,0:T(8,128)(2,1)S(1)} %shard_map.54.refs_4_), channel_id=1, source_target_pairs={{0,12},{4,0},{8,4},{12,8},{1,13},{5,1},{9,5},{13,9},{2,14},{6,2},{... | collective-permute-start | bytes 491528 | tf_op jit(solution)/shard_map/ppermute | solution.py:197
  116.0 12.2 %collective-permute-start.17 = (bf16[256,512]{1,0:T(8,128)(2,1)S(1)}, bf16[256,512]{1,0:T(8,128)(2,1)S(1)}, u32[]{:S(2)}, u32[]{:S(2)}) collective-permute-start(bf16[256,512]{1,0:T(8,128)(2,1)S(1)} %get-tuple-element.54), channel_id=1, source_target_pairs={{0,3},{1,0},{2,1},{3,2},{4,7},{5,4},{6,5},{7,6},{8,11},{9,8},{10,9... | collective-permute-start | bytes 786440 | tf_op jit(solution)/shard_map/ppermute | solution.py:197
  118.9 10.8 %collective-permute-start.18 = (bf16[256,512]{1,0:T(8,128)(2,1)S(1)}, bf16[256,512]{1,0:T(8,128)(2,1)S(1)}, u32[]{:S(2)}, u32[]{:S(2)}) collective-permute-start(bf16[256,512]{1,0:T(8,128)(2,1)S(1)} %get-tuple-element.55), channel_id=1, source_target_pairs={{0,2},{1,3},{2,0},{3,1},{4,6},{5,7},{6,4},{7,5},{8,10},{9,11},{10,... | collective-permute-start | bytes 786440 | tf_op jit(solution)/shard_map/ppermute | solution.py:197
  119.7 16.1 %collective-permute-start.19 = (bf16[256,512]{1,0:T(8,128)(2,1)S(1)}, bf16[256,512]{1,0:T(8,128)(2,1)S(1)}, u32[]{:S(2)}, u32[]{:S(2)}) collective-permute-start(bf16[256,512]{1,0:T(8,128)(2,1)S(1)} %get-tuple-element.56), channel_id=1, source_target_pairs={{0,1},{1,2},{2,3},{3,0},{4,5},{5,6},{6,7},{7,4},{8,9},{9,10},{10,1... | collective-permute-start | bytes 786440 | tf_op jit(solution)/shard_map/ppermute | solution.py:197
  123.8 15.3 %collective-permute-start.26 = (bf16[256,512]{1,0:T(8,128)(2,1)S(1)}, bf16[256,512]{1,0:T(8,128)(2,1)S(1)}, u32[]{:S(2)}, u32[]{:S(2)}) collective-permute-start(bf16[256,512]{1,0:T(8,128)(2,1)S(1)} %get-tuple-element.62), channel_id=1, source_target_pairs={{0,3},{1,0},{2,1},{3,2},{4,7},{5,4},{6,5},{7,6},{8,11},{9,8},{10,9... | collective-permute-start | bytes 786440 | tf_op jit(solution)/shard_map/ppermute | solution.py:197
  126.3 13.9 %collective-permute-start.27 = (bf16[256,512]{1,0:T(8,128)(2,1)S(1)}, bf16[256,512]{1,0:T(8,128)(2,1)S(1)}, u32[]{:S(2)}, u32[]{:S(2)}) collective-permute-start(bf16[256,512]{1,0:T(8,128)(2,1)S(1)} %get-tuple-element.63), channel_id=1, source_target_pairs={{0,2},{1,3},{2,0},{3,1},{4,6},{5,7},{6,4},{7,5},{8,10},{9,11},{10,... | collective-permute-start | bytes 786440 | tf_op jit(solution)/shard_map/ppermute | solution.py:197
  128.1 14.7 %collective-permute-start.28 = (bf16[256,512]{1,0:T(8,128)(2,1)S(1)}, bf16[256,512]{1,0:T(8,128)(2,1)S(1)}, u32[]{:S(2)}, u32[]{:S(2)}) collective-permute-start(bf16[256,512]{1,0:T(8,128)(2,1)S(1)} %get-tuple-element.64), channel_id=1, source_target_pairs={{0,1},{1,2},{2,3},{3,0},{4,5},{5,6},{6,7},{7,4},{8,9},{9,10},{10,1... | collective-permute-start | bytes 786440 | tf_op jit(solution)/shard_map/ppermute | solution.py:197
Sparse Core Ops, SparseCore 0:
  9.2 63.9 all-gather.1
